TPU v7x, 32 devices: a whole 2x2x4 slice. The times are simulated.
32 devices in a mesh: clip: 2 (over y), seq: 4 (over z), tm: 2 (over x), chan: 2 (over core).
Axes of the slice: x: 2, y: 2, z: 4, core: 2. Of those that a mesh axis runs over, the one named last changes fastest.
Arguments:
- latents: bfloat16 [4, 16, 28800], P(('clip', 'tm'), None, 'seq'), parts along dimension 0, may hold values from -6 to 6
- conv_in: bfloat16 [3, 3, 3, 16, 512], P(None, None, None, None, 'chan'), may hold values from -0.3125 to 0.3125
- conv_up: bfloat16 [3, 3, 3, 512, 256], P(None, None, None, None, 'chan'), may hold values from -0.0546875 to 0.0546875
- to_pixels: bfloat16 [256, 12], P('chan'), may hold values from -0.375 to 0.375
- slot_anchor: int32 [4, 3, 16], P(('clip', 'tm'), None, 'seq'), parts along dimension 0, may hold values from 0 to 144, as said below
- slot_count: int32 [4, 4], P(('clip', 'tm'), 'seq'), parts along dimension 0, may hold values from 1 to 4, 8 in all within a row
Outputs:
- pixels: bfloat16 [4, 16, 3, 1, 128], P(('clip', 'tm'), 'seq'), parts along dimension 0
There are 2 independent parts, one for each index of `clip`. A program takes and returns all parts, laid end to end along the dimension named above; an argument that names none is the same for every part. Nothing has to cross between parts.
Inputs may be any that keep to these rules, and one draw needn't show every extreme that they name: `slot_count`: over the devices of one temporal group the counts sum to 2 times the number of devices; the largest count of each group is 4. `slot_anchor`: component 0 is a frame from 0 to 3, component 1 a row from 0 to 43, component 2 a column from 0 to 144; tiles may intersect; slots at or past a device's count are unused.
All inputs are finite; a program needn't handle non-finite values.
Results may differ from a plain program's by a relative error of at most 0.0059.
Values may be sent and summed in bfloat16 or wider, within the bound.
No kernel may reach another device: no remote copies, remote signals or barrier semaphores. Data moves between devices by JAX's collectives and lax.ppermute only.
A program may use at most 64 MiB of HBM per device.

v0:
```python
import jax
import jax.numpy as jnp
from jax import lax
from jax.sharding import PartitionSpec as P

C_LAT = 16
H_LAT = 45
W_LAT = 160
FG = 4
TF = 1
TH = 2
TW = 16
MAXT = 4


def passed_along(x, axis, by):
    size = lax.axis_size(axis)
    pairs = [(i, i + by) for i in range(size) if 0 <= i + by < size]
    return lax.ppermute(x, axis, pairs)


def edge_mask(row_start, col_start):
    row_ids = row_start + jnp.arange(TH + 2, dtype=jnp.int32)
    col_ids = col_start + jnp.arange(TW + 2, dtype=jnp.int32)
    row_in = (row_ids >= 0) & (row_ids < H_LAT)
    col_in = (col_ids >= 0) & (col_ids < W_LAT)
    return (row_in[:, None] & col_in[None, :]).astype(jnp.float32)


def convolve(volume, kernel, layout):
    return lax.conv_general_dilated(
        volume,
        kernel,
        (1, 1, 1),
        "VALID",
        dimension_numbers=(layout, "DHWIO", "NDHWC"),
        preferred_element_type=jnp.float32,
    )


def decode_tiles(windows, anchors, in_kernel, conv_up, to_pixels):
    item_count = windows.shape[0]
    pre_act = convolve(windows, in_kernel, "NCDHW")
    edge_keep = jax.vmap(edge_mask)(anchors[1] - 1, anchors[2] - 1)
    hidden = (jax.nn.silu(pre_act) * edge_keep[:, None, :, :, None]).astype(jnp.bfloat16)
    hidden = lax.all_gather(hidden, "chan", axis=4, tiled=True)
    mid_pre = convolve(hidden, conv_up, "NDHWC")
    upper = jax.nn.silu(mid_pre).astype(jnp.bfloat16)
    flat_upper = upper.reshape(item_count, -1, upper.shape[-1])
    partial_colors = jnp.einsum(
        "mvc,ck->mkv", flat_upper, to_pixels, preferred_element_type=jnp.float32
    )
    colors = lax.psum(partial_colors, "chan")
    shaped = (
        colors.reshape(item_count, 3, 2, 2, TF, TH, TW)
        .transpose(0, 1, 4, 5, 2, 6, 3)
        .reshape(item_count, 3, TF, 4 * TH * TW)
    )
    return shaped.astype(jnp.bfloat16)


def fetch_windows(current, previous, everyone, work_mine, seq_size, seq_rank):
    item_count = work_mine.shape[1]
    per_frame = seq_size // FG
    shard_len = current.shape[1]
    frame_here = seq_rank // per_frame
    part_start = seq_rank % per_frame * shard_len
    sources = jnp.concatenate([previous, current], axis=1)
    frame_start = everyone[0] + FG - 4
    row_ids = everyone[1][:, None] - 2 + jnp.arange(TH + 4, dtype=jnp.int32)[None, :]
    col_ids = everyone[2][:, None] - 2 + jnp.arange(TW + 4, dtype=jnp.int32)[None, :]
    row_in = (row_ids >= 0) & (row_ids < H_LAT)
    col_in = (col_ids >= 0) & (col_ids < W_LAT)
    token_ids = row_ids[:, :, None] * W_LAT + col_ids[:, None, :] - part_start
    in_shard = row_in[:, :, None] & col_in[:, None, :] & (token_ids >= 0) & (token_ids < shard_len)
    which_half = jnp.arange(2, dtype=jnp.int32)
    frame_pos = which_half[None, :] * FG + frame_here - frame_start[:, None]
    frame_ok = (frame_pos >= 0) & (frame_pos < TF + 4)
    usable = in_shard[:, None, :, :] & frame_ok[:, :, None, None]
    flat_index = (
        which_half[None, :, None, None] * shard_len
        + jnp.clip(token_ids, 0, shard_len - 1)[:, None, :, :]
    )
    picked = jnp.take(sources, flat_index.reshape(-1), axis=1)
    picked = jnp.where(usable.reshape(-1)[None, :], picked, jnp.zeros((), jnp.bfloat16))
    received = lax.all_to_all(picked, "seq", split_axis=1, concat_axis=1, tiled=True)
    received = received.reshape(C_LAT, seq_size, item_count, 2, TH + 4, TW + 4)
    source_frames = jnp.arange(seq_size, dtype=jnp.int32) // per_frame
    my_start = work_mine[0] + FG - 4
    position = (
        which_half[None, None, :] * FG + source_frames[:, None, None] - my_start[None, :, None]
    )
    onehot = (position[..., None] == jnp.arange(TF + 4, dtype=jnp.int32)).astype(jnp.bfloat16)
    windows = jnp.einsum("sjwk,csjwab->jckab", onehot, received, preferred_element_type=jnp.float32)
    return windows.astype(jnp.bfloat16)


def local(latents, conv_in, conv_up, to_pixels, slot_anchor, slot_count):
    seq_size = lax.axis_size("seq")
    seq_rank = lax.axis_index("seq")
    current = latents[0]
    previous = passed_along(current, "tm", 1)
    work_mine = slot_anchor[0]
    everyone = lax.all_gather(slot_anchor, "seq", axis=2, tiled=True)[0]
    windows = fetch_windows(current, previous, everyone, work_mine, seq_size, seq_rank)
    decoded = decode_tiles(windows, work_mine, conv_in, conv_up, to_pixels)
    slot_ids = jnp.arange(MAXT, dtype=jnp.int32)
    is_live = slot_ids < slot_count[0, 0]
    result = jnp.where(is_live[:, None, None, None], decoded, jnp.zeros((), jnp.bfloat16))
    return result[None]


def solution(mesh):
    placed = (
        P(("clip", "tm"), None, "seq"),
        P(None, None, None, None, "chan"),
        P(None, None, None, None, "chan"),
        P("chan", None),
        P(("clip", "tm"), None, "seq"),
        P(("clip", "tm"), "seq"),
    )
    return jax.shard_map(
        local,
        mesh=mesh,
        in_specs=placed,
        out_specs=P(("clip", "tm"), "seq", None, None, None),
        check_vma=False,
    )
```

profile of v0, /device:TPU:0, one launch (start us, length us, event | category | flops | bytes accessed | tf_op | source)
XLA Modules:
  0.0 103.9 jit_solution(1173367473099802442)
XLA Ops:
  0.0 5.8 %collective-permute-start = (bf16[16,7200]{1,0:T(8,128)(2,1)}, bf16[16,7200]{1,0:T(8,128)(2,1)}, u32[]{:S(2)}, u32[]{:S(2)}) collective-permute-start(bf16[16,7200]{1,0:T(8,128)(2,1)} %bitcast.74), channel_id=1, source_target_pairs={{0,2},{1,3},{4,6},{5,7},{8,10},{9,11},{12,14},{13,15},{16,18},{17,... | collective-permute-start | bytes 691208 | tf_op jit(solution)/shard_map/ppermute | solution.py:19
  5.8 0.6 iota_multiply_fusion.1
  6.4 0.5 iota_multiply_fusion
  6.9 1.2 %add_bitcast_fusion.1 = (s32[4]{0:T(128)}, s32[4]{0:T(128)}, s32[4]{0:T(128)}) fusion(s32[1,3,4]{2,0,1:T(1,128)} %param.10), kind=kLoop, calls=%fused_computation.69 | loop fusion | flops 8 | bytes 96 | tf_op jit(solution)/shard_map/sub | solution.py:44
  8.1 0.8 copy.54
  8.9 12.1 %all_gather.6 = s32[1,3,16]{1,0,2:T(1,128)S(1)} all-gather(s32[1,3,4]{1,0,2:T(1,128)S(1)} %copy.54), channel_id=1, replica_groups=mesh['clip'=2,'seq'=4,'tm'=2,'chan'=2] {'seq'}, dimensions={2}, use_global_device_ids=true | all-gather | bytes 240 | tf_op jit(solution)/shard_map/all_gather | solution.py:104
  21.0 1.2 %slice_reduce_fusion = (s32[16]{0:T(128)}, s32[16]{0:T(128)S(1)}, s32[16]{0:T(128)S(1)}) fusion(s32[1,3,16]{1,0,2:T(1,128)S(1)} %all_gather.6), kind=kLoop, calls=%fused_computation.42 | loop fusion | flops 32 | bytes 384 | tf_op jit(solution)/shard_map/slice | solution.py:69
  22.2 0.7 fusion.31
  22.8 0.1 fusion.26
  22.9 0.7 compare_and_fusion.1
  23.6 0.1 iota_add_fusion
  23.6 0.1 add_clamp_fusion
  23.7 1.3 %broadcast_add_fusion = s32[16,2,6,20]{3,2,1,0:T(8,128)} fusion(s32[16,6,20]{2,1,0:T(8,128)S(1)} %add_clamp_fusion, s32[2]{0:T(128)} %iota_multiply_fusion), kind=kLoop, calls=%fused_computation.29 | loop fusion | flops 3840 | bytes 23048 | tf_op jit(solution)/shard_map/add | solution.py:81
  25.1 1.6 %add.251 = s32[3840,1]{0,1:T(1,128)} reshape(s32[16,2,6,20]{3,2,1,0:T(8,128)} %broadcast_add_fusion) | data formatting | bytes 30720 | tf_op jit(solution)/shard_map/add | solution.py:81
  26.7 1.6 %add.248 = s32[4,960]{1,0:T(4,128)} reshape(s32[16,2,6,20]{3,2,1,0:T(8,128)} %broadcast_add_fusion) | data formatting | bytes 30720 | tf_op jit(solution)/shard_map/add | solution.py:81
  29.0 1.3 %iota_add_fusion.4 = s32[4,2]{0,1:T(2,128)} fusion(s32[2]{0:T(128)} %iota_multiply_fusion.1), kind=kLoop, calls=%fused_computation.67 | loop fusion | flops 8 | bytes 40 | tf_op jit(solution)/shard_map/add | solution.py:91
  30.3 1.2 %fusion.38 = pred[4,4]{1,0:T(4,128)(4,1)} fusion(s32[4]{0:T(128)} %get-tuple-element.8), kind=kLoop, calls=%fused_computation.64 | loop fusion | flops 64 | bytes 32 | tf_op jit(solution)/shard_map/vmap()/and | solution.py:25
  31.5 1.2 %fusion.39 = pred[4,18]{1,0:T(4,128)(4,1)} fusion(s32[4]{0:T(128)} %get-tuple-element.10), kind=kLoop, calls=%fused_computation.65 | loop fusion | flops 288 | bytes 88 | tf_op jit(solution)/shard_map/vmap()/and | solution.py:26
  32.7 1.3 %compare_and_fusion.2 = pred[16,2]{0,1:T(4,128)(4,1)} fusion(s32[16]{0:T(128)} %get-tuple-element.5, s32[2]{0:T(128)S(1)} %broadcast_add_fusion.1), kind=kLoop, calls=%fused_computation.66 | loop fusion | flops 128 | bytes 104 | tf_op jit(solution)/shard_map/and | solution.py:78
  33.9 1.3 %copy.55 = pred[16,2]{1,0:T(8,128)(4,1)} copy(pred[16,2]{0,1:T(4,128)(4,1)} %compare_and_fusion.2) | data formatting | bytes 64 | tf_op jit(solution)/shard_map/and | solution.py:78
  35.2 1.3 %compare_and_fusion = pred[4,960]{1,0:T(4,128)(4,1)} fusion(s32[4,960]{1,0:T(4,128)} %add.248), kind=kLoop, calls=%fused_computation.40 | loop fusion | flops 23040 | bytes 19200 | tf_op jit(solution)/shard_map/jit(_take)/and | solution.py:84
  36.6 0.8 fusion.24
  37.3 0.6 pad_clamp_fusion
  37.9 0.8 fusion.21
  38.7 1.4 %broadcast_and_fusion = pred[16,2,6,20]{3,2,1,0:T(8,128)(4,1)} fusion(pred[16,2]{1,0:T(8,128)(4,1)} %copy.55, pred[16,6,20]{2,1,0:T(8,128)(4,1)S(1)} %fusion.21), kind=kLoop, calls=%fused_computation.32 | loop fusion | flops 3840 | bytes 5792 | tf_op jit(solution)/shard_map/and | solution.py:79
  40.1 0.5 iota_compare_fusion.3
  40.6 1.5 %and.134 = pred[4,960]{1,0:T(4,128)(4,1)} reshape(pred[16,2,6,20]{3,2,1,0:T(8,128)(4,1)} %broadcast_and_fusion) | data formatting | bytes 7680 | tf_op jit(solution)/shard_map/and | solution.py:79
  42.1 1.3 %and_convert_fusion = f32[4,4,18]{1,2,0:T(8,128)} fusion(pred[4,18]{1,0:T(4,128)(4,1)} %fusion.39, pred[4,4]{1,0:T(4,128)(4,1)} %fusion.38), kind=kLoop, calls=%fused_computation.33 | loop fusion | flops 576 | bytes 1240 | tf_op jit(solution)/shard_map/vmap()/convert_element_type | solution.py:27
  43.4 2.0 %pad_maximum_fusion = bf16[16,14400]{1,0:T(8,128)(2,1)} fusion(bf16[16,7200]{1,0:T(8,128)(2,1)} %bitcast.75, bf16[16,7200]{1,0:T(8,128)(2,1)} %collective-permute-done), kind=kLoop, calls=%fused_computation.21 | loop fusion | flops 921600 | bytes 921600 | tf_op jit(solution)/shard_map/concatenate | solution.py:68
  45.4 3.9 %copy.56 = bf16[16,14400]{0,1:T(8,128)(2,1)} copy(bf16[16,14400]{1,0:T(8,128)(2,1)} %pad_maximum_fusion) | data formatting | bytes 921600 | tf_op jit(solution)/shard_map/concatenate | solution.py:68
  49.3 10.4 %gather_fusion = bf16[3840,16]{1,0:T(8,128)(2,1)} fusion(bf16[16,14400]{0,1:T(8,128)(2,1)} %copy.56, s32[4096]{0:T(1024)S(1)} %copy-done.2), kind=kCustom, calls=%fused_computation | custom fusion | bytes 261120 | tf_op jit(solution)/shard_map/jit(_take)/gather | solution.py:84
  59.7 2.1 %copy.57 = bf16[16,4,960]{2,0,1:T(8,128)(2,1)} copy(bf16[16,4,960]{0,2,1:T(8,128)(2,1)} %bitcast.72) | data formatting | bytes 245760 | tf_op jit(solution)/shard_map/jit(_take)/gather | solution.py:84
  61.8 1.6 %select_select_fusion = bf16[16,4,960]{2,0,1:T(8,128)(2,1)} fusion(bf16[16,4,960]{2,0,1:T(8,128)(2,1)} %copy.57, pred[4,960]{1,0:T(4,128)(4,1)} %compare_and_fusion, pred[4,960]{1,0:T(4,128)(4,1)} %and.134), kind=kLoop, calls=%fused_computation.22 | loop fusion | flops 122880 | bytes 253440 | tf_op jit(solution)/shard_map/jit(_where)/select_n | solution.py:85
  63.4 3.9 %all-to-all-start = ((bf16[16,4,960]{2,0,1:T(8,128)(2,1)}), bf16[16,4,960]{2,0,1:T(8,128)(2,1)}, u32[]{:S(2)}, u32[]{:S(2)}) async-start(bf16[16,4,960]{2,0,1:T(8,128)(2,1)} %select_select_fusion), calls=%async_computation | async-start | bytes 262144 | tf_op jit(solution)/shard_map/all_to_all | solution.py:86
  67.4 0.7 broadcast_subtract_fusion
  68.1 5.2 %all-to-all-done = bf16[16,4,960]{2,0,1:T(8,128)(2,1)} async-done(((bf16[16,4,960]{2,0,1:T(8,128)(2,1)}), bf16[16,4,960]{2,0,1:T(8,128)(2,1)}, u32[]{:S(2)}, u32[]{:S(2)}) %all-to-all-start) | async-done | bytes 122912 | tf_op jit(solution)/shard_map/all_to_all | solution.py:86
  73.4 3.4 %reshape.361 = bf16[16,4,4,2,6,20]{5,4,3,2,0,1:T(8,128)(2,1)} reshape(bf16[16,4,960]{2,0,1:T(8,128)(2,1)} %all-to-all-done) | data formatting | bytes 245760 | tf_op jit(solution)/shard_map/reshape | solution.py:87
  76.7 3.1 %fusion.6 = bf16[16,6,4,20,5]{3,4,1,0,2:T(8,128)(2,1)} fusion(bf16[16,4,4,2,6,20]{5,4,3,2,0,1:T(8,128)(2,1)} %reshape.361, s32[4,4,2]{0,2,1:T(2,128)S(1)} %broadcast_subtract_fusion), kind=kOutput, calls=%fused_computation.11 | convolution fusion | flops 652960 | bytes 199808 | tf_op jit(solution)/shard_map/sjwk,csjwab->jckab/dot_general | solution.py:94
  79.8 2.7 %copy.72 = bf16[16,6,4,20,5]{0,2,4,3,1:T(4,128)(2,1)} copy(bf16[16,6,4,20,5]{3,4,1,0,2:T(8,128)(2,1)} %fusion.6) | data formatting | bytes 153600
  82.5 1.4 %pad.clone = bf16[16,6,4,24,5]{0,2,4,3,1:T(4,128)(2,1)S(1)} pad(bf16[16,6,4,20,5]{0,2,4,3,1:T(4,128)(2,1)} %copy.72, bf16[]{:T(256)} %constant.93.clone.1), padding=0_0x0_0x0_0x0_4x0_0 | pad | bytes 168962 | tf_op jit(solution)/shard_map/convert_element_type | solution.py:95
  83.9 0.0 copy-start.5
  83.9 0.0 copy-start.7
  83.9 0.1 slice.39
  84.1 0.6 fusion.7
  84.7 0.1 copy-done.5
  84.9 1.4 %divide_multiply_fusion = f32[3,4,32,3,256]{4,2,3,1,0:T(8,128)S(1)} fusion(bf16[3,3,3,16,256]{4,3,2,1,0:T(8,128)(2,1)S(1)} %copy-done.5, bf16[16,6,4,8,5,5]{0,2,5,4,3,1:T(4,128)(2,1)S(1)} %fusion.7, pred[32,3]{0,1:T(4,128)(4,1)S(1)} %copy-done.7), kind=kOutput, calls=%fused_computation.15 | convolution fusion | flops 256278528 | bytes 1554528 | tf_op jit(solution)/shard_map/conv_general_dilated | solution.py:31
  86.3 0.8 copy.62
  87.0 0.0 copy-done.1
  87.1 0.2 fusion.16
  87.3 2.6 %all_gather.7 = bf16[4,3,4,18,512]{4,2,3,0,1:T(4,128)(2,1)S(1)} all-gather(bf16[4,3,4,18,256]{4,2,3,0,1:T(4,128)(2,1)S(1)} %fusion.16), channel_id=1, replica_groups=mesh['clip'=2,'seq'=4,'tm'=2,'chan'=2] {'chan'}, dimensions={4}, use_global_device_ids=true | all-gather | bytes 1327104 | tf_op jit(solution)/shard_map/all_gather | solution.py:46
  89.9 0.5 copy.73
  90.4 0.5 pad.2.clone
  90.9 0.3 slice.41
  91.1 0.0 copy-start.6
  91.2 0.9 fusion.2
  92.1 0.0 copy-start.3
  92.1 1.5 %multiply_convert_fusion = bf16[1,2,32,3,128]{4,2,3,1,0:T(8,128)(2,1)S(1)} fusion(bf16[3,3,3,512,128]{4,3,2,1,0:T(8,128)(2,1)S(1)} %copy-done, bf16[3,4,4,8,5,512]{5,2,4,3,1,0:T(4,128)(2,1)S(1)} %fusion.2, pred[32,3]{0,1:T(4,128)(4,1)S(1)} %copy-done.6), kind=kOutput, calls=%fused_computation.26 | convolution fusion | flops 679624704 | bytes 5554272 | tf_op jit(solution)/shard_map/conv_general_dilated | solution.py:31
  93.8 0.1 fusion.32
  93.9 0.6 copy.92
  94.5 4.0 %psum.7 = bf16[4,12,32]{2,0,1:T(4,128)(2,1)S(1)} all-reduce(f32[4,12,32]{2,0,1:T(4,128)} %bitcast.78), channel_id=1, replica_groups=mesh['clip'=2,'seq'=4,'tm'=2,'chan'=2] {'chan'}, use_global_device_ids=true, to_apply=%region_0.1 | all-reduce | flops 1536 | bytes 9216 | tf_op jit(solution)/shard_map/psum | solution.py:53
  98.5 0.7 convert_element_type.44
  99.2 1.6 %copy.68 = bf16[4,3,1,2,2,16,2]{0,6,5,4,3,1,2:T(2,128)(2,1)} copy(bf16[4,3,1,2,2,16,2]{5,3,0,6,4,1,2:T(2,128)(2,1)} %bitcast.79) | data formatting | bytes 6144 | tf_op jit(solution)/shard_map/convert_element_type | solution.py:59
  100.8 1.5 %broadcast_select_fusion = bf16[1,4,3,1,128]{1,4,2,3,0:T(8,128)(2,1)} fusion(bf16[1,4,3,1,128]{1,4,2,3,0:T(8,128)(2,1)} %bitcast.73, pred[4]{0:T(512)(128)(4,1)S(1)} %copy-done.4), kind=kLoop, calls=%fused_computation.27 | loop fusion | flops 1536 | bytes 6148 | tf_op jit(solution)/shard_map/jit(_where)/select_n | solution.py:109
  102.4 1.6 %copy.69 = bf16[1,4,3,1,128]{4,1,3,2,0:T(4,128)(2,1)} copy(bf16[1,4,3,1,128]{1,4,2,3,0:T(8,128)(2,1)} %broadcast_select_fusion) | data formatting | bytes 6144 | tf_op jit(solution)/shard_map/jit(_where)/select_n | solution.py:109
  (15 shorter events, 0.1 us)
Async XLA Ops:
  0.0 92.1 %copy-start = (bf16[3,3,3,512,128]{4,3,2,1,0:T(8,128)(2,1)S(1)}, bf16[3,3,3,512,128]{4,3,2,1,0:T(8,128)(2,1)}, u32[]{:S(2)}) copy-start(bf16[3,3,3,512,128]{4,3,2,1,0:T(8,128)(2,1)} %param.8) | copy-start | bytes 10616836
  0.0 43.4 %collective-permute-start = (bf16[16,7200]{1,0:T(8,128)(2,1)}, bf16[16,7200]{1,0:T(8,128)(2,1)}, u32[]{:S(2)}, u32[]{:S(2)}) collective-permute-start(bf16[16,7200]{1,0:T(8,128)(2,1)} %bitcast.74), channel_id=1, source_target_pairs={{0,2},{1,3},{4,6},{5,7},{8,10},{9,11},{12,14},{13,15},{16,18},{17,... | collective-permute-start | bytes 691208 | tf_op jit(solution)/shard_map/ppermute | solution.py:19
  45.4 3.9 %copy-start.2 = (s32[4096]{0:T(1024)S(1)}, s32[4096]{0:T(1024)}, u32[]{:S(2)}) copy-start(s32[4096]{0:T(1024)} %pad_clamp_fusion) | copy-start | bytes 49156
  63.4 9.9 %all-to-all-start = ((bf16[16,4,960]{2,0,1:T(8,128)(2,1)}), bf16[16,4,960]{2,0,1:T(8,128)(2,1)}, u32[]{:S(2)}, u32[]{:S(2)}) async-start(bf16[16,4,960]{2,0,1:T(8,128)(2,1)} %select_select_fusion), calls=%async_computation | async-start | bytes 262144 | tf_op jit(solution)/shard_map/all_to_all | solution.py:86
  83.9 0.9 copy-start.5
  83.9 0.9 copy-start.7
  86.3 0.8 copy-start.1
  91.1 0.9 copy-start.6
  92.1 1.7 %copy-start.3 = (bf16[128,12]{0,1:T(8,128)(2,1)S(1)}, bf16[128,12]{0,1:T(8,128)(2,1)}, u32[]{:S(2)}) copy-start(bf16[128,12]{0,1:T(8,128)(2,1)} %param.9) | copy-start | bytes 9220
  92.1 8.8 %copy-start.4 = (pred[4]{0:T(512)(128)(4,1)S(1)}, pred[4]{0:T(512)(128)(4,1)}, u32[]{:S(2)}) copy-start(pred[4]{0:T(512)(128)(4,1)} %iota_compare_fusion.3) | copy-start | bytes 16
where the time goes:
time: 105 us; the launch traced here: 104 us
  local copies, waits for them, and re-layouts  37.6 us (36%)
  other arithmetic  25.6 us (24%)
  blocking collectives  18.7 us (18%)
  starting transfers between devices  9.72 us (9%)
  matrix products  6.14 us (6%)
  waiting for transfers between devices  5.25 us (5%)
    gather x2, local copies, waits for them, and re-layouts, fetch_windows(): picked = jnp.take(sources, flat_index.reshape(-1), axis=1)  12.6 us
    all_gather x1, blocking collectives, local(): everyone = lax.all_gather(slot_anchor, 'seq', axis=2, tiled=True)[0]  12.1 us
    ppermute x1, starting transfers between devices, passed_along(): return lax.ppermute(x, axis, pairs)  5.78 us
    all_to_all x1, waiting for transfers between devices, fetch_windows(): lax.all_to_all(picked, 'seq', split_axis=1, concat_axis=1, tiled=True)  5.25 us
    unnamed x19, local copies, waits for them, and re-layouts  4.11 us
    psum x1, blocking collectives, decode_tiles(): colors = lax.psum(partial_colors, 'chan')  4.02 us
    all_to_all x1, starting transfers between devices, fetch_windows(): lax.all_to_all(picked, 'seq', split_axis=1, concat_axis=1, tiled=True)  3.93 us
    concatenate x1, local copies, waits for them, and re-layouts, fetch_windows(): sources = jnp.concatenate([previous, current], axis=1)  3.87 us
  transfers between devices with their start and end apart: 2, of which 1 were waited for; matrix products, arithmetic and copies ran while one was open for 25% of the time, Pallas kernels for 0%

commit v1 on v0

v1 whole, which is shorter than its diff:
```python
import functools

import jax
import jax.numpy as jnp
from jax import lax
from jax.experimental import pallas as pl
from jax.experimental.pallas import tpu as pltpu
from jax.sharding import PartitionSpec as P

H_LAT = 45
W_LAT = 160
C_LAT = 16
C_MID = 512
FG = 4
TH = 2
TW = 16
MAXT = 4
ROWS = TH + 4
COLS = TW + 4
LANES = 128
ITEM = LANES // MAXT
TAPS = 3
BF16 = jnp.bfloat16
F32 = jnp.float32
VMEM = pl.BlockSpec(memory_space=pltpu.VMEM)
SMEM = pl.BlockSpec(memory_space=pltpu.SMEM)


def lane_ids(rows):
    return lax.broadcasted_iota(jnp.int32, (rows, LANES), 1)


def silu(v):
    return v * (0.5 * jnp.tanh(0.5 * v) + 0.5)


def cut_windows(n, *refs):
    anchors, (cur_ref, prev_ref), outs, src = refs[:n], refs[n : n + 2], refs[n + 2 : -1], refs[-1]
    shard = cur_ref.shape[1]
    per_frame = n // FG
    part_start = lax.rem(lax.axis_index("seq"), per_frame) * shard
    src[:C_LAT, :shard] = prev_ref[...].astype(F32)
    src[C_LAT:, :shard] = cur_ref[...].astype(F32)
    last_base = (shard - 1) // LANES * LANES
    lane = lane_ids(2 * C_LAT)
    for k in range(n):
        for rho in range(ROWS):
            total = jnp.zeros((2 * C_LAT, LANES), F32)
            for i in range(MAXT):
                col0 = anchors[k][0, 2, i] - 2
                start = (anchors[k][0, 1, i] - 2 + rho) * W_LAT + col0 - part_start
                base = jnp.clip(start // LANES * LANES, 0, last_base)
                base = pl.multiple_of(base, LANES)
                off = start - base
                low = src[:, pl.ds(base, LANES)]
                high = src[:, pl.ds(base + LANES, LANES)]
                both = jnp.where(lane >= off, low, high)
                moved = pltpu.roll(both, (ITEM * i - off) & (LANES - 1), 1)
                cell = lane - ITEM * i
                first = jnp.maximum(jnp.maximum(-col0, -start), 0)
                end = jnp.minimum(jnp.minimum(W_LAT - col0, shard - start), COLS)
                total = jnp.where((cell >= first) & (cell < end), moved, total)
            total = total.astype(BF16)
            outs[k][0, rho] = total[:C_LAT]
            outs[k][1, rho] = total[C_LAT:]


def arrange_weights(own_in, other_in, up, pix, in_t, up_t, pix_t):
    me = lax.axis_index("chan")
    half = own_in.shape[1]
    in_t[pl.ds(pl.multiple_of(me * half, half), half), :] = own_in[...].T
    in_t[pl.ds(pl.multiple_of((1 - me) * half, half), half), :] = other_in[...].T
    outs = up.shape[-1]
    for a in range(TAPS):
        for b in range(TAPS):
            for c in range(TAPS):
                at = (a * TAPS + c) * C_MID
                up_t[b * outs : (b + 1) * outs, at : at + C_MID] = up[a, b, c].T
    row = lax.broadcasted_iota(jnp.int32, (32, 12), 0)
    col = lax.broadcasted_iota(jnp.int32, (32, 12), 1)
    pick = ((row % 8) * 4 + row // 8 == col) & (row % 8 < 3)
    pix_t[...] = lax.dot_general(
        pick.astype(BF16), pix[...], (((1,), (1,)), ((), ())), preferred_element_type=F32
    ).astype(BF16)


def decode(n, *refs):
    anchor, parts, (in_t, up_t, pix_t, out, held, hidden) = refs[0], refs[1 : n + 1], refs[n + 1 :]
    per_frame = n // FG
    me = lax.axis_index("seq")
    for k in range(n):
        held[lax.rem(me + n - k, n)] = parts[k][...]
    lane = lane_ids(C_LAT)
    parity = (lane // TW) % 2
    frames = []
    for j in range(5):
        frames.append([])
        where = []
        for i in range(MAXT):
            at = anchor[0, 0, i] + j
            where.append((at // FG, lax.rem(at, FG) * per_frame))
        for rho in range(ROWS):
            total = jnp.zeros((C_LAT, LANES), F32)
            for i, (late, rank) in enumerate(where):
                piece = held[rank, late, rho].astype(F32)
                for p in range(1, per_frame):
                    piece += held[rank + p, late, rho].astype(F32)
                total = jnp.where(lane // ITEM == i, piece, total)
            frames[j].append(total)

    def shifted(v, by):
        by %= LANES
        return v if by == 0 else pltpu.roll(v, by, 1)

    cells = [
        [
            [
                jnp.where(parity == 0, shifted(frames[j][rho], -dx), shifted(frames[j][rho + 1], TW - dx)).astype(BF16)
                for rho in range(5)
            ]
            for dx in range(5)
        ]
        for j in range(5)
    ]
    one_lane = lane_ids(1)
    item, y, x = one_lane // ITEM, (one_lane // TW) % 2, one_lane % TW

    def per_item(values):
        result = jnp.full((1, LANES), values[0], jnp.int32)
        for i in range(1, MAXT):
            result = jnp.where(item == i, values[i], result)
        return result

    row0 = per_item([anchor[0, 1, i] for i in range(MAXT)]) - 1 + y
    col0 = per_item([anchor[0, 2, i] for i in range(MAXT)]) - 1 + x
    rows = jnp.concatenate([row0, row0 + 2], axis=1)
    cols = jnp.concatenate([col0, col0], axis=1)
    row_keep = (rows >= 0) & (rows < H_LAT)
    for t in range(TAPS):
        for c2 in (0, 2):
            sides = []
            for side in (0, 2):
                sides.append(
                    jnp.concatenate(
                        [cells[t + a][c2 + c][b + side] for a in range(TAPS) for b in range(TAPS) for c in range(TAPS)],
                        axis=0,
                    )
                )
            volume = jnp.concatenate(sides, axis=1)
            pre = jnp.dot(in_t[...], volume, preferred_element_type=F32)
            keep = row_keep & (cols + c2 >= 0) & (cols + c2 < W_LAT)
            hidden[pl.ds((t * TAPS + c2) * C_MID, C_MID), :] = jnp.where(keep, silu(pre), 0.0).astype(BF16)
        left = hidden[pl.ds(t * TAPS * C_MID, C_MID), :].astype(F32)
        right = hidden[pl.ds((t * TAPS + 2) * C_MID, C_MID), :].astype(F32)
        last = lax.broadcasted_iota(jnp.int32, left.shape, 1) % TW == TW - 1
        mid = jnp.where(last, pltpu.roll(right, 1, 1), pltpu.roll(left, 2 * LANES - 1, 1))
        hidden[pl.ds((t * TAPS + 1) * C_MID, C_MID), :] = mid.astype(BF16)
    sums = jnp.dot(up_t[...], hidden[...], preferred_element_type=F32)
    outs = sums.shape[0] // TAPS
    first, mid, last = sums[:outs, :LANES], sums[outs : 2 * outs], sums[2 * outs :, LANES:]
    par = (lane_ids(outs) // TW) % 2
    crossed = jnp.where(
        par == 0, pltpu.roll(mid[:, :LANES], LANES - TW, 1), pltpu.roll(mid[:, LANES:], TW, 1)
    )
    upper = silu(first + last + crossed).astype(BF16)
    out[...] = jnp.dot(pix_t[...], upper, preferred_element_type=F32)


def shuffle(count, own, other, out):
    colors = (own[...] + other[...]).astype(BF16).astype(F32)
    lane = lane_ids(8)
    p, q = (lane // 32) % 2, lane % 2
    for i in range(MAXT):
        source = i * ITEM + (lane // 64) * TW + (lane % 32) // 2
        pixel = jnp.zeros((8, LANES), F32)
        for pq in range(4):
            moved = jnp.take_along_axis(colors[8 * pq : 8 * pq + 8], source, axis=1)
            pixel = jnp.where(2 * p + q == pq, moved, pixel)
        pixel = jnp.where(i < count[0, 0], pixel, 0.0).astype(BF16)
        for e in range(3):
            out[0, i, e] = pixel[e : e + 1]


def rotated(x, axis, by):
    size = lax.axis_size(axis)
    return lax.ppermute(x, axis, [(i, (i + by) % size) for i in range(size)])


def local(latents, conv_in, conv_up, to_pixels, slot_anchor, slot_count):
    n = lax.axis_size("seq")
    current = latents[0]
    shard = current.shape[1]
    in_flat = conv_in.reshape(-1, conv_in.shape[-1])
    anchors = [slot_anchor] + [rotated(slot_anchor, "seq", -k) for k in range(1, n)]
    tm_size = lax.axis_size("tm")
    previous = lax.ppermute(current, "tm", [(i, i + 1) for i in range(tm_size - 1)])
    other_in = rotated(in_flat, "chan", 1)
    outs = conv_up.shape[-1]
    in_t, up_t, pix_t = pl.pallas_call(
        arrange_weights,
        out_shape=(
            jax.ShapeDtypeStruct((C_MID, in_flat.shape[0]), BF16),
            jax.ShapeDtypeStruct((TAPS * outs, TAPS * TAPS * C_MID), BF16),
            jax.ShapeDtypeStruct((32, outs), BF16),
        ),
        in_specs=[VMEM] * 4,
        out_specs=(VMEM,) * 3,
        compiler_params=pltpu.CompilerParams(vmem_limit_bytes=32 << 20),
        name="arrange_weights",
    )(in_flat, other_in, conv_up, to_pixels)
    message = (2, ROWS, C_LAT, LANES)
    padded = (shard - 1) // LANES * LANES + 2 * LANES
    cut = pl.pallas_call(
        functools.partial(cut_windows, n),
        out_shape=[jax.ShapeDtypeStruct(message, BF16)] * n,
        in_specs=[SMEM] * n + [VMEM] * 2,
        out_specs=[VMEM] * n,
        scratch_shapes=[pltpu.VMEM((2 * C_LAT, padded), F32)],
        compiler_params=pltpu.CompilerParams(vmem_limit_bytes=16 << 20),
        name="cut_windows",
    )(*anchors, current, previous)
    parts = [cut[0]] + [rotated(cut[k], "seq", k) for k in range(1, n)]
    colors = pl.pallas_call(
        functools.partial(decode, n),
        out_shape=jax.ShapeDtypeStruct((32, LANES), F32),
        in_specs=[SMEM] + [VMEM] * (n + 3),
        out_specs=VMEM,
        scratch_shapes=[
            pltpu.VMEM((n,) + message, BF16),
            pltpu.VMEM((TAPS * TAPS * C_MID, 2 * LANES), BF16),
        ],
        compiler_params=pltpu.CompilerParams(vmem_limit_bytes=32 << 20),
        name="decode",
    )(slot_anchor, *parts, in_t, up_t, pix_t)
    other = rotated(colors, "chan", 1)
    return pl.pallas_call(
        shuffle,
        out_shape=jax.ShapeDtypeStruct((1, MAXT, 3, 1, LANES), BF16),
        in_specs=[SMEM, VMEM, VMEM],
        out_specs=VMEM,
        name="shuffle",
    )(slot_count, colors, other)


def solution(mesh):
    placed = (
        P(("clip", "tm"), None, "seq"),
        P(None, None, None, None, "chan"),
        P(None, None, None, None, "chan"),
        P("chan", None),
        P(("clip", "tm"), None, "seq"),
        P(("clip", "tm"), "seq"),
    )
    return jax.shard_map(
        local,
        mesh=mesh,
        in_specs=placed,
        out_specs=P(("clip", "tm"), "seq", None, None, None),
        check_vma=False,
    )
```

time: 105 us -> 35.1 us (0.33)
  local copies, waits for them, and re-layouts: 37.6 us -> 7.24 us
  other arithmetic: 25.6 us -> 0 us
  blocking collectives: 18.7 us -> 0 us
  Pallas kernels: 0 us -> 8.14 us
  matrix products: 6.14 us -> 0 us
  starting transfers between devices: 9.72 us -> 13.6 us
    all_gather x2 -> x0, blocking collectives: 14.7 us -> none  [the longest x1 12.1 us: local(): everyone = lax.all_gather(slot_anchor, 'seq', axis=2, tiled=True)[0]]
    gather x2 -> x0, local copies, waits for them, and re-layouts: 12.6 us -> none  [fetch_windows(): picked = jnp.take(sources, flat_index.reshape(-1), axis=1)]
    and x8 -> x0, other arithmetic: 8.45 us -> none  [the longest x1 1.4 us: fetch_windows(): usable = in_shard[:, None, :, :] & frame_ok[:, :, None, None]]
    pallas_call x0 -> x4, Pallas kernels: none -> 8.14 us  [the longest x1 3.59 us: local(): pl.pallas_call(functools.partial(decode, n), out_shape=jax.ShapeDtypeStru...]
    ppermute x1 -> x9, starting transfers between devices: 5.78 us -> 13.6 us  [the longest x8 8.78 us: rotated(): return lax.ppermute(x, axis, [(i, (i + by) % size) for i in range(size)])]
    all_to_all x1 -> x0, waiting for transfers between devices: 5.25 us -> none  [fetch_windows(): lax.all_to_all(picked, 'seq', split_axis=1, concat_axis=1, tiled=True)]
    ppermute x1 -> x9, waiting for transfers between devices: 0.01 us -> 4.91 us  [the longest x8 4.9 us: rotated(): return lax.ppermute(x, axis, [(i, (i + by) % size) for i in range(size)])]
    psum x1 -> x0, blocking collectives: 4.02 us -> none  [decode_tiles(): colors = lax.psum(partial_colors, 'chan')]
  transfers between devices with their start and end apart: 2 -> 9, of which waited for: 1 -> 4; matrix products, arithmetic and copies ran while one was open for 25% -> 4% of each run, Pallas kernels for 0% -> 9%
where the time goes in v1:
time: 35.1 us; the launch traced here: 34.7 us
  starting transfers between devices  13.6 us (39%)
  Pallas kernels  8.14 us (23%)
  local copies, waits for them, and re-layouts  7.24 us (21%)
  waiting for transfers between devices  4.91 us (14%)
  between operations  0.75 us (2%)
    ppermute x8, starting transfers between devices, rotated(): return lax.ppermute(x, axis, [(i, (i + by) % size) for i in range(size)])  8.78 us
    unnamed x12, local copies, waits for them, and re-layouts  5.97 us
    ppermute x8, waiting for transfers between devices, rotated(): return lax.ppermute(x, axis, [(i, (i + by) % size) for i in range(size)])  4.9 us
    ppermute x1, starting transfers between devices, local(): lax.ppermute(current, 'tm', [(i, i + 1) for i in range(tm_size - 1)])  4.85 us
    pallas_call x1, Pallas kernels, local(): pl.pallas_call(functools.partial(decode, n), out_shape=jax.ShapeDtypeStru...  3.59 us
    pallas_call x1, Pallas kernels, local(): pl.pallas_call(functools.partial(cut_windows, n), out_shape=[jax.ShapeDty...  2.01 us
    pallas_call x1, Pallas kernels, local(): pl.pallas_call(shuffle, out_shape=jax.ShapeDtypeStruct((1, MAXT, 3, 1, LA...  1.44 us
    pallas_call x1, local copies, waits for them, and re-layouts, local(): pl.pallas_call(shuffle, out_shape=jax.ShapeDtypeStruct((1, MAXT, 3, 1, LA...  1.27 us
  transfers between devices with their start and end apart: 9, of which 4 were waited for; matrix products, arithmetic and copies ran while one was open for 4% of the time, Pallas kernels for 9%

profile of v1, /device:TPU:0, one launch (start us, length us, event | category | flops | bytes accessed | tf_op | source)
XLA Modules:
  0.0 34.7 jit_solution(8396828519088897766)
XLA Ops:
  0.0 4.8 %collective-permute-start.3 = (bf16[16,7200]{1,0:T(8,128)(2,1)}, bf16[16,7200]{1,0:T(8,128)(2,1)S(1)}, u32[]{:S(2)}, u32[]{:S(2)}) collective-permute-start(bf16[16,7200]{1,0:T(8,128)(2,1)} %bitcast.2), channel_id=1, source_target_pairs={{0,2},{1,3},{4,6},{5,7},{8,10},{9,11},{12,14},{13,15},{16,18},{17,... | collective-permute-start | bytes 691208 | tf_op jit(solution)/shard_map/ppermute | solution.py:196
  4.9 0.1 collective-permute-start.7
  4.9 0.7 %copy.12.refs_0_ = s32[1,3,4]{2,1,0:T(4,128)S(1)} copy(s32[1,3,4]{2,0,1:T(1,128)} %param.10) | data formatting | bytes 96 | tf_op args[4]
  5.6 3.6 %collective-permute-start = (s32[1,3,4]{2,1,0:T(4,128)S(1)}, s32[1,3,4]{2,1,0:T(4,128)S(1)}, u32[]{:S(2)}, u32[]{:S(2)}) collective-permute-start(s32[1,3,4]{2,1,0:T(4,128)S(1)} %copy.12.refs_0_), channel_id=1, source_target_pairs={{0,12},{4,0},{8,4},{12,8},{1,13},{5,1},{9,5},{13,9},{2,14},{6,2},{... | collective-permute-start | bytes 152 | tf_op jit(solution)/shard_map/ppermute | solution.py:186
  9.2 0.0 collective-permute-start.1
  9.2 1.0 %collective-permute-start.2 = (s32[1,3,4]{2,1,0:T(4,128)S(1)}, s32[1,3,4]{2,1,0:T(4,128)S(1)}, u32[]{:S(2)}, u32[]{:S(2)}) collective-permute-start(s32[1,3,4]{2,1,0:T(4,128)S(1)} %copy.12.refs_0_), channel_id=1, source_target_pairs={{0,4},{4,8},{8,12},{12,0},{1,5},{5,9},{9,13},{13,1},{2,6},{6,10},{... | collective-permute-start | bytes 152 | tf_op jit(solution)/shard_map/ppermute | solution.py:186
  10.2 0.3 collective-permute-done.refs_1_
  10.5 3.2 %collective-permute-done.1.refs_2_ = s32[1,3,4]{2,1,0:T(4,128)S(1)} collective-permute-done((s32[1,3,4]{2,1,0:T(4,128)S(1)}, s32[1,3,4]{2,1,0:T(4,128)S(1)}, u32[]{:S(2)}, u32[]{:S(2)}) %collective-permute-start.1) | collective-permute-done | bytes 80 | tf_op jit(solution)/shard_map/ppermute | solution.py:186
  13.7 0.9 %collective-permute-done.2.refs_3_ = s32[1,3,4]{2,1,0:T(4,128)S(1)} collective-permute-done((s32[1,3,4]{2,1,0:T(4,128)S(1)}, s32[1,3,4]{2,1,0:T(4,128)S(1)}, u32[]{:S(2)}, u32[]{:S(2)}) %collective-permute-start.2) | collective-permute-done | bytes 80 | tf_op jit(solution)/shard_map/ppermute | solution.py:186
  14.6 0.0 collective-permute-done.3.refs_5_
  14.6 0.0 copy-start.1
  14.6 0.9 %copy-done.1 = bf16[1,16,7200]{2,1,0:T(8,128)(2,1)S(1)} copy-done((bf16[1,16,7200]{2,1,0:T(8,128)(2,1)S(1)}, bf16[1,16,7200]{2,1,0:T(8,128)(2,1)}, u32[]{:S(2)}) %copy-start.1) | copy-done | bytes 230424
  15.6 2.0 %cut_windows.1 = (bf16[2,6,16,128]{3,2,1,0:T(8,128)(2,1)S(1)}, bf16[2,6,16,128]{3,2,1,0:T(8,128)(2,1)S(1)}, bf16[2,6,16,128]{3,2,1,0:T(8,128)(2,1)S(1)}, bf16[2,6,16,128]{3,2,1,0:T(8,128)(2,1)S(1)}) custom-call(s32[1,3,4]{2,1,0:T(4,128)S(1)} %copy.12.refs_0_, s32[1,3,4]{2,1,0:T(4,128)S(1)} %collective-permute-done.refs_1_, ...), custom_call_target="tpu_custom_call" | custom-call | tf_op jit(solution)/shard_map/cut_windows/pallas_call | solution.py:213
  17.6 0.1 collective-permute-start.4
  17.6 1.2 %collective-permute-start.5 = (bf16[2,6,16,128]{3,2,1,0:T(8,128)(2,1)S(1)}, bf16[2,6,16,128]{3,2,1,0:T(8,128)(2,1)S(1)}, u32[]{:S(2)}, u32[]{:S(2)}) collective-permute-start(bf16[2,6,16,128]{3,2,1,0:T(8,128)(2,1)S(1)} %get-tuple-element.14), channel_id=1, source_target_pairs={{0,8},{4,12},{8,0},{12,4},{1,9},{5,13},{9,1},{13,5},{2,10},{6,14},... | collective-permute-start | bytes 147464 | tf_op jit(solution)/shard_map/ppermute | solution.py:186
  18.8 2.8 %collective-permute-start.6 = (bf16[2,6,16,128]{3,2,1,0:T(8,128)(2,1)S(1)}, bf16[2,6,16,128]{3,2,1,0:T(8,128)(2,1)S(1)}, u32[]{:S(2)}, u32[]{:S(2)}) collective-permute-start(bf16[2,6,16,128]{3,2,1,0:T(8,128)(2,1)S(1)} %get-tuple-element.15), channel_id=1, source_target_pairs={{0,12},{4,0},{8,4},{12,8},{1,13},{5,1},{9,5},{13,9},{2,14},{6,2},{... | collective-permute-start | bytes 147464 | tf_op jit(solution)/shard_map/ppermute | solution.py:186
  21.7 0.8 %copy.11.pix = bf16[128,12]{1,0:T(8,128)(2,1)S(1)} copy(bf16[128,12]{0,1:T(8,128)(2,1)} %param.9) | data formatting | bytes 6144 | tf_op args[3]
  22.5 0.0 collective-permute-done.7.other_in
  22.5 0.0 copy-start
  22.5 2.0 %copy-done = bf16[3,3,3,512,128]{4,3,2,1,0:T(8,128)(2,1)S(1)} copy-done((bf16[3,3,3,512,128]{4,3,2,1,0:T(8,128)(2,1)S(1)}, bf16[3,3,3,512,128]{4,3,2,1,0:T(8,128)(2,1)}, u32[]{:S(2)}) %copy-start) | copy-done | bytes 3538968
  24.5 0.0 copy-start.2
  24.5 0.9 %copy-done.2 = bf16[3,3,3,16,256]{4,3,2,1,0:T(8,128)(2,1)S(1)} copy-done((bf16[3,3,3,16,256]{4,3,2,1,0:T(8,128)(2,1)S(1)}, bf16[3,3,3,16,256]{4,3,2,1,0:T(8,128)(2,1)}, u32[]{:S(2)}) %copy-start.2) | copy-done | bytes 221208
  25.4 1.1 %arrange_weights.1 = (bf16[512,432]{1,0:T(8,128)(2,1)S(1)}, bf16[384,4608]{1,0:T(8,128)(2,1)S(1)}, bf16[32,128]{1,0:T(8,128)(2,1)S(1)}) custom-call(bf16[432,256]{1,0:T(8,128)(2,1)S(1)} %bitcast.5, bf16[432,256]{1,0:T(8,128)(2,1)S(1)} %collective-permute-done.7.other_in, bf16[3,3,3,512,128]{4,3,2,1,0:T(8,128)(2,1)S(1)} %copy-done, bf16[128,12]{1,0:T(8,128)(2,1)S(1)} %copy.11.pix), custom_call_target="tpu_custom_call" | custom-call | tf_op jit(solution)/shard_map/arrange_weights/pallas_call | solution.py:199
  26.5 0.0 collective-permute-done.4.refs_2_
  26.5 0.0 collective-permute-done.5.refs_3_
  26.6 0.0 collective-permute-done.6.refs_4_
  26.6 3.6 %decode.1.own = f32[32,128]{1,0:T(8,128)S(1)} custom-call(s32[1,3,4]{2,1,0:T(4,128)S(1)} %copy.12.refs_0_, bf16[2,6,16,128]{3,2,1,0:T(8,128)(2,1)S(1)} %get-tuple-element.12.refs_1_, bf16[2,6,16,128]{3,2,1,0:T(8,128)(2,1)S(1)} %collective-permute-done.4.refs_2_, bf16[2,6,16,128]{3,2,1,0:T(8,128)(2,1)S(1)} %collective-permute-done.5.refs_3_, ...), custom_call_target="tpu_custom_call" | custom-call | tf_op jit(solution)/shard_map/decode/pallas_call | solution.py:223
  30.2 0.0 copy-start.3
  30.2 0.0 collective-permute-start.8
  30.8 0.5 %collective-permute-done.8.other = f32[32,128]{1,0:T(8,128)S(1)} collective-permute-done((f32[32,128]{1,0:T(8,128)S(1)}, f32[32,128]{1,0:T(8,128)S(1)}, u32[]{:S(2)}, u32[]{:S(2)}) %collective-permute-start.8) | collective-permute-done | bytes 16416 | tf_op jit(solution)/shard_map/ppermute | solution.py:186
  31.4 0.0 copy-done.3
  31.4 0.0 copy-start.4
  31.4 0.6 %copy-done.4 = f32[32,128]{1,0:T(8,128)} copy-done((f32[32,128]{1,0:T(8,128)}, f32[32,128]{1,0:T(8,128)S(1)}, u32[]{:S(2)}) %copy-start.4) | copy-done | bytes 16408
  32.0 1.4 %shuffle.1 = bf16[1,4,3,1,128]{4,3,2,1,0:T(2,128)(2,1)} custom-call(s32[1,1]{1,0:T(1,128)S(6)} %copy.14.count, f32[32,128]{1,0:T(8,128)} %copy-done.3, f32[32,128]{1,0:T(8,128)} %copy-done.4), custom_call_target="tpu_custom_call" | custom-call | tf_op jit(solution)/shard_map/shuffle/pallas_call | solution.py:236
  33.4 1.3 %copy.13 = bf16[1,4,3,1,128]{4,1,3,2,0:T(4,128)(2,1)} copy(bf16[1,4,3,1,128]{4,3,2,1,0:T(2,128)(2,1)} %shuffle.1) | data formatting | bytes 6144 | tf_op jit(solution)/shard_map/shuffle/pallas_call | solution.py:236
Async XLA Ops:
  0.0 14.6 %collective-permute-start.3 = (bf16[16,7200]{1,0:T(8,128)(2,1)}, bf16[16,7200]{1,0:T(8,128)(2,1)S(1)}, u32[]{:S(2)}, u32[]{:S(2)}) collective-permute-start(bf16[16,7200]{1,0:T(8,128)(2,1)} %bitcast.2), channel_id=1, source_target_pairs={{0,2},{1,3},{4,6},{5,7},{8,10},{9,11},{12,14},{13,15},{16,18},{17,... | collective-permute-start | bytes 691208 | tf_op jit(solution)/shard_map/ppermute | solution.py:196
  4.9 17.6 %collective-permute-start.7 = (bf16[432,256]{1,0:T(8,128)(2,1)}, bf16[432,256]{1,0:T(8,128)(2,1)S(1)}, u32[]{:S(2)}, u32[]{:S(2)}) collective-permute-start(bf16[432,256]{1,0:T(8,128)(2,1)} %bitcast.4), channel_id=1, source_target_pairs={{0,1},{1,0},{2,3},{3,2},{4,5},{5,4},{6,7},{7,6},{8,9},{9,8},{10,11... | collective-permute-start | bytes 663560 | tf_op jit(solution)/shard_map/ppermute | solution.py:186
  5.6 4.9 %collective-permute-start = (s32[1,3,4]{2,1,0:T(4,128)S(1)}, s32[1,3,4]{2,1,0:T(4,128)S(1)}, u32[]{:S(2)}, u32[]{:S(2)}) collective-permute-start(s32[1,3,4]{2,1,0:T(4,128)S(1)} %copy.12.refs_0_), channel_id=1, source_target_pairs={{0,12},{4,0},{8,4},{12,8},{1,13},{5,1},{9,5},{13,9},{2,14},{6,2},{... | collective-permute-start | bytes 152 | tf_op jit(solution)/shard_map/ppermute | solution.py:186
  9.2 4.5 %collective-permute-start.1 = (s32[1,3,4]{2,1,0:T(4,128)S(1)}, s32[1,3,4]{2,1,0:T(4,128)S(1)}, u32[]{:S(2)}, u32[]{:S(2)}) collective-permute-start(s32[1,3,4]{2,1,0:T(4,128)S(1)} %copy.12.refs_0_), channel_id=1, source_target_pairs={{0,8},{4,12},{8,0},{12,4},{1,9},{5,13},{9,1},{13,5},{2,10},{6,14},... | collective-permute-start | bytes 152 | tf_op jit(solution)/shard_map/ppermute | solution.py:186
  9.2 5.4 %collective-permute-start.2 = (s32[1,3,4]{2,1,0:T(4,128)S(1)}, s32[1,3,4]{2,1,0:T(4,128)S(1)}, u32[]{:S(2)}, u32[]{:S(2)}) collective-permute-start(s32[1,3,4]{2,1,0:T(4,128)S(1)} %copy.12.refs_0_), channel_id=1, source_target_pairs={{0,4},{4,8},{8,12},{12,0},{1,5},{5,9},{9,13},{13,1},{2,6},{6,10},{... | collective-permute-start | bytes 152 | tf_op jit(solution)/shard_map/ppermute | solution.py:186
  14.6 0.9 %copy-start.1 = (bf16[1,16,7200]{2,1,0:T(8,128)(2,1)S(1)}, bf16[1,16,7200]{2,1,0:T(8,128)(2,1)}, u32[]{:S(2)}) copy-start(bf16[1,16,7200]{2,1,0:T(8,128)(2,1)} %param.6) | copy-start | bytes 691204
  17.6 9.0 %collective-permute-start.4 = (bf16[2,6,16,128]{3,2,1,0:T(8,128)(2,1)S(1)}, bf16[2,6,16,128]{3,2,1,0:T(8,128)(2,1)S(1)}, u32[]{:S(2)}, u32[]{:S(2)}) collective-permute-start(bf16[2,6,16,128]{3,2,1,0:T(8,128)(2,1)S(1)} %get-tuple-element.13), channel_id=1, source_target_pairs={{0,4},{4,8},{8,12},{12,0},{1,5},{5,9},{9,13},{13,1},{2,6},{6,10},{... | collective-permute-start | bytes 147464 | tf_op jit(solution)/shard_map/ppermute | solution.py:186
  17.6 8.9 %collective-permute-start.5 = (bf16[2,6,16,128]{3,2,1,0:T(8,128)(2,1)S(1)}, bf16[2,6,16,128]{3,2,1,0:T(8,128)(2,1)S(1)}, u32[]{:S(2)}, u32[]{:S(2)}) collective-permute-start(bf16[2,6,16,128]{3,2,1,0:T(8,128)(2,1)S(1)} %get-tuple-element.14), channel_id=1, source_target_pairs={{0,8},{4,12},{8,0},{12,4},{1,9},{5,13},{9,1},{13,5},{2,10},{6,14},... | collective-permute-start | bytes 147464 | tf_op jit(solution)/shard_map/ppermute | solution.py:186
  18.8 7.7 %collective-permute-start.6 = (bf16[2,6,16,128]{3,2,1,0:T(8,128)(2,1)S(1)}, bf16[2,6,16,128]{3,2,1,0:T(8,128)(2,1)S(1)}, u32[]{:S(2)}, u32[]{:S(2)}) collective-permute-start(bf16[2,6,16,128]{3,2,1,0:T(8,128)(2,1)S(1)} %get-tuple-element.15), channel_id=1, source_target_pairs={{0,12},{4,0},{8,4},{12,8},{1,13},{5,1},{9,5},{13,9},{2,14},{6,2},{... | collective-permute-start | bytes 147464 | tf_op jit(solution)/shard_map/ppermute | solution.py:186
  22.5 2.0 %copy-start = (bf16[3,3,3,512,128]{4,3,2,1,0:T(8,128)(2,1)S(1)}, bf16[3,3,3,512,128]{4,3,2,1,0:T(8,128)(2,1)}, u32[]{:S(2)}) copy-start(bf16[3,3,3,512,128]{4,3,2,1,0:T(8,128)(2,1)} %up.1) | copy-start | bytes 10616836
  24.5 0.9 %copy-start.2 = (bf16[3,3,3,16,256]{4,3,2,1,0:T(8,128)(2,1)S(1)}, bf16[3,3,3,16,256]{4,3,2,1,0:T(8,128)(2,1)}, u32[]{:S(2)}) copy-start(bf16[3,3,3,16,256]{4,3,2,1,0:T(8,128)(2,1)} %param.7) | copy-start | bytes 663556
  30.2 1.2 %copy-start.3 = (f32[32,128]{1,0:T(8,128)}, f32[32,128]{1,0:T(8,128)S(1)}, u32[]{:S(2)}) copy-start(f32[32,128]{1,0:T(8,128)S(1)} %decode.1.own) | copy-start | bytes 49156
  30.2 1.2 %collective-permute-start.8 = (f32[32,128]{1,0:T(8,128)S(1)}, f32[32,128]{1,0:T(8,128)S(1)}, u32[]{:S(2)}, u32[]{:S(2)}) collective-permute-start(f32[32,128]{1,0:T(8,128)S(1)} %decode.1.own), channel_id=1, source_target_pairs={{0,1},{1,0},{2,3},{3,2},{4,5},{5,4},{6,7},{7,6},{8,9},{9,8},{10,11... | collective-permute-start | bytes 49160 | tf_op jit(solution)/shard_map/ppermute | solution.py:186
  31.4 0.6 %copy-start.4 = (f32[32,128]{1,0:T(8,128)}, f32[32,128]{1,0:T(8,128)S(1)}, u32[]{:S(2)}) copy-start(f32[32,128]{1,0:T(8,128)S(1)} %collective-permute-done.8.other) | copy-start | bytes 49156

commit v2 on v0

v2 whole, which is shorter than its diff:
```python
import functools

import jax
import jax.numpy as jnp
from jax import lax
from jax.experimental import pallas as pl
from jax.experimental.pallas import tpu as pltpu
from jax.sharding import PartitionSpec as P

H_LAT = 45
W_LAT = 160
C_LAT = 16
C_MID = 512
FG = 4
TH = 2
TW = 16
MAXT = 4
ROWS = TH + 4
COLS = TW + 4
LANES = 128
ITEM = LANES // MAXT
TAPS = 3
WIDE = 24
BF16 = jnp.bfloat16
F32 = jnp.float32
VMEM = pl.BlockSpec(memory_space=pltpu.VMEM)
SMEM = pl.BlockSpec(memory_space=pltpu.SMEM)
HBM = pl.BlockSpec(memory_space=pltpu.HBM)
ANY = pl.BlockSpec(memory_space=pl.ANY)


def lane_ids(rows):
    return lax.broadcasted_iota(jnp.int32, (rows, LANES), 1)


def silu(v):
    return v * (0.5 * jnp.tanh(0.5 * v) + 0.5)


def fetched(sources, targets, sems):
    copies = [pltpu.make_async_copy(*pair, sems.at[i]) for i, pair in enumerate(zip(sources, targets))]
    for copy in copies:
        copy.start()
    return copies


def stage(ready, *refs):
    del ready
    sources, (cur_out, *outs, cur, sems) = refs[:5], refs[5:]
    copies = []
    for i, pair in enumerate(zip(sources, (cur, *outs))):
        copies.append(pltpu.make_async_copy(*pair, sems.at[i]))
        copies[i].start()
    copies[0].wait()
    cur_out[:, : cur.shape[1]] = cur[...]
    for copy in copies[1:]:
        copy.wait()


def cut_windows(n, *refs):
    count = n // 2 + 1
    anchors, (cur, prev_ref), outs, prev = refs[:count], refs[count : count + 2], refs[count + 2 : -1], refs[-1]
    shard = prev_ref.shape[1]
    per_frame = n // FG
    part_start = lax.rem(lax.axis_index("seq"), per_frame) * shard
    last_base = (shard - 1) // LANES * LANES
    lane = lane_ids(C_LAT)
    prev[:, :shard] = prev_ref[...]
    for k in range(count):
        for i in range(MAXT):
            row0 = anchors[k][1, 0, i] - 2
            col0 = anchors[k][2, 0, i] - 2
            first = jnp.maximum(-col0, 0)
            end = jnp.minimum(W_LAT - col0, COLS)
            totals = [jnp.zeros((C_LAT, LANES), BF16)] * 2
            for rho in range(ROWS):
                start = (row0 + rho) * W_LAT + col0 - part_start
                base = jnp.clip(start & -LANES, 0, last_base)
                base = pl.multiple_of(base, LANES)
                off = start - base
                from_low = lane >= off
                least = COLS * rho + jnp.maximum(first, -start)
                past = COLS * rho + jnp.minimum(end, shard - start)
                keep = (lane >= least) & (lane < past)
                for half, source in enumerate((prev, cur)):
                    low = source[:, pl.ds(base, LANES)]
                    high = source[:, pl.ds(base + LANES, LANES)]
                    moved = pltpu.roll(jnp.where(from_low, low, high), (COLS * rho - off) & (LANES - 1), 1)
                    totals[half] = jnp.where(keep, moved, totals[half])
            for half in range(2):
                outs[k][half, i] = totals[half]


def decode(n, *refs):
    anchor, count, parts = refs[0], refs[1], refs[2 : n + 2]
    own_in, other_in, own_pix, other_pix, own_up, other_up, out, held, hidden, lined = refs[n + 2 :]
    per_frame = n // FG
    me = lax.axis_index("seq")
    core = lax.axis_index("chan")
    held[me] = parts[0][...]
    for k in range(1, n // 2):
        by = jnp.where(core == 0, k, n - k)
        held[lax.rem(me + n - by, n)] = parts[2 * k - 1][...]
        held[lax.rem(me + by, n)] = parts[2 * k][...]
    held[lax.rem(me + n // 2, n)] = parts[n - 1][...]
    lane = lane_ids(C_LAT)

    moved = []
    for j in range(5):
        where = []
        for i in range(MAXT):
            at = anchor[0, 0, i] + j
            where.append((at // FG, lax.rem(at, FG) * per_frame))
        moved.append([])
        pieces = []
        for i, (late, rank) in enumerate(where):
            piece = held[rank, late, i]
            for p in range(1, per_frame):
                piece += held[rank + p, late, i]
            pieces.append(piece)
        for rho in range(ROWS):
            total = None
            for i, piece in enumerate(pieces):
                by = (ITEM * i - COLS * rho) % LANES
                piece = pltpu.roll(piece, by, 1) if by else piece
                total = piece if i == 0 else jnp.where(lane >= ITEM * i, piece, total)
            moved[j].append([total] + [pltpu.roll(total, LANES - c, 1) for c in range(1, TAPS)])

    x = lax.broadcasted_iota(jnp.int32, (WIDE, LANES), 0)
    quarter = C_MID // 4
    for t in range(TAPS):
        cells = jnp.concatenate(
            [
                jnp.concatenate(
                    [moved[t + a][r + b][c] for a in range(TAPS) for b in range(TAPS) for c in range(TAPS)], axis=0
                )
                for r in range(TH + 2)
            ],
            axis=1,
        ).T
        for weights, first in ((own_in, core), (other_in, 1 - core)):
            pre = jnp.dot(cells, weights[...], preferred_element_type=F32)
            for r in range(TH + 2):
                for i in range(MAXT):
                    row = anchor[1, 0, i] - 1 + r
                    col = anchor[2, 0, i] - 1 + x
                    width = jnp.where((row >= 0) & (row < H_LAT), W_LAT, 0)
                    at = (r * MAXT + i) * ITEM
                    value = silu(pre[at : at + WIDE])
                    for q in range(2):
                        hidden[t, r * MAXT + i, 2 * first + q] = jnp.where(
                            (col >= 0) & (col < width), value[:, q * quarter : (q + 1) * quarter], 0.0
                        )
        for c in range(TAPS):
            for ri in range((TH + 2) * MAXT):
                for q in range(4):
                    lined[t * TAPS + c, ri * TW : (ri + 1) * TW, q * quarter : (q + 1) * quarter] = hidden[
                        t, ri, q, c : c + TW
                    ].astype(BF16)
    outs = own_up.shape[-1]
    span = MAXT * TW
    total = jnp.zeros((TH * span, 2 * outs), F32)
    for a in range(TAPS):
        for c in range(TAPS):
            for b in range(TAPS):
                weights = jnp.concatenate([own_up[a, b, c], other_up[a, b, c]], axis=1)
                rows = lined[a * TAPS + c, b * span : (b + TH) * span]
                total += jnp.dot(rows, weights, preferred_element_type=F32)
    upper = silu(total).astype(BF16)
    row = lax.broadcasted_iota(jnp.int32, (32, 12), 0)
    col = lax.broadcasted_iota(jnp.int32, (32, 12), 1)
    pick = ((row % 8) * 4 + row // 8 == col) & (row % 8 < 3)
    pix = jnp.concatenate([own_pix[...], other_pix[...]], axis=1)
    pix = jnp.dot(pick.astype(BF16), pix, preferred_element_type=F32).astype(BF16)
    colors = lax.dot_general(pix, upper, (((1,), (1,)), ((), ())), preferred_element_type=F32)
    colors = colors.astype(BF16).astype(F32)
    lane = lane_ids(8)
    p, q = (lane // 32) % 2, lane % 2
    for i in range(MAXT):
        source = (lane // 64) * span + i * TW + (lane % 32) // 2
        pixel = jnp.zeros((8, LANES), F32)
        for pq in range(4):
            found = jnp.take_along_axis(colors[8 * pq : 8 * pq + 8], source, axis=1)
            pixel = jnp.where(2 * p + q == pq, found, pixel)
        pixel = jnp.where(i < count[0, 0], pixel, 0.0).astype(BF16)
        for e in range(3):
            out[0, e, 0, i : i + 1] = pixel[e : e + 1]


def in_hbm(x):
    return pltpu.with_memory_space_constraint(x, pltpu.HBM)


def swapped(x):
    return lax.ppermute(x, "chan", [(0, 1), (1, 0)])


def spread(x, by):
    size = lax.axis_size("seq")
    pairs = []
    for at in range(size):
        pairs.append((2 * at, 2 * ((at + by) % size)))
        pairs.append((2 * at + 1, 2 * ((at - by) % size) + 1))
    return lax.ppermute(x, ("seq", "chan"), pairs)


def local(latents, conv_in, conv_up, to_pixels, slot_anchor, slot_count):
    n = lax.axis_size("seq")
    current = latents[0]
    shard = current.shape[1]
    anchor = slot_anchor.transpose(1, 0, 2)
    in_flat = conv_in.reshape(-1, conv_in.shape[-1])
    pix = to_pixels.T
    anchors = [spread(anchor, -k) for k in range(1, n // 2 + 1)]
    tm_size = lax.axis_size("tm")
    previous = lax.ppermute(current, "tm", [(i, i + 1) for i in range(tm_size - 1)])
    other_in, other_pix, other_up = swapped(in_flat), swapped(pix), swapped(conv_up)
    padded = (shard - 1) // LANES * LANES + 2 * LANES
    own = (anchor, in_flat, pix, conv_up)
    cur_pad, anchor, own_in, own_pix, own_up = pl.pallas_call(
        stage,
        out_shape=[jax.ShapeDtypeStruct((C_LAT, padded), BF16)] + [jax.ShapeDtypeStruct(x.shape, x.dtype) for x in own],
        in_specs=[ANY] + [HBM] * 5,
        out_specs=[VMEM] * 5,
        scratch_shapes=[pltpu.VMEM(current.shape, BF16), pltpu.SemaphoreType.DMA((5,))],
        compiler_params=pltpu.CompilerParams(vmem_limit_bytes=8 << 20),
        cost_estimate=pl.CostEstimate(flops=1, bytes_accessed=1, transcendentals=0),
        name="stage",
    )(anchors[-1], *map(in_hbm, (current, *own)))
    message = jax.ShapeDtypeStruct((2, MAXT, C_LAT, LANES), BF16)
    cut = pl.pallas_call(
        functools.partial(cut_windows, n),
        out_shape=[message] * (n // 2 + 1),
        in_specs=[SMEM] * (n // 2 + 1) + [VMEM] * 2,
        out_specs=[VMEM] * (n // 2 + 1),
        scratch_shapes=[pltpu.VMEM((C_LAT, padded), BF16)],
        compiler_params=pltpu.CompilerParams(vmem_limit_bytes=4 << 20),
        name="cut_windows",
    )(anchor, *anchors, cur_pad, previous)
    parts = [cut[0]]
    for k in range(1, n // 2):
        arrived = spread(cut[k], k)
        parts += [arrived, swapped(arrived)]
    parts.append(spread(cut[n // 2], n // 2))
    pixels = pl.pallas_call(
        functools.partial(decode, n),
        out_shape=jax.ShapeDtypeStruct((1, 3, 1, MAXT, LANES), BF16),
        in_specs=[SMEM, SMEM] + [VMEM] * (n + 6),
        out_specs=VMEM,
        scratch_shapes=[
            pltpu.VMEM((n,) + message.shape, BF16),
            pltpu.VMEM((TAPS, (TH + 2) * MAXT, 4, WIDE, C_MID // 4), F32),
            pltpu.VMEM((TAPS * TAPS, (TH + 2) * MAXT * TW, C_MID), BF16),
        ],
        compiler_params=pltpu.CompilerParams(vmem_limit_bytes=32 << 20),
        name="decode",
    )(anchor, slot_count, *parts, own_in, other_in, own_pix, other_pix, own_up, other_up)
    return pixels.transpose(0, 3, 1, 2, 4)


def solution(mesh):
    placed = (
        P(("clip", "tm"), None, "seq"),
        P(None, None, None, None, "chan"),
        P(None, None, None, None, "chan"),
        P("chan", None),
        P(("clip", "tm"), None, "seq"),
        P(("clip", "tm"), "seq"),
    )
    return jax.shard_map(
        local,
        mesh=mesh,
        in_specs=placed,
        out_specs=P(("clip", "tm"), "seq", None, None, None),
        check_vma=False,
    )
```

time: 105 us -> 25.5 us (0.24)
  local copies, waits for them, and re-layouts: 37.6 us -> 0.01 us
  other arithmetic: 25.6 us -> 0 us
  blocking collectives: 18.7 us -> 0 us
  Pallas kernels: 0 us -> 8.37 us
  matrix products: 6.14 us -> 0 us
  starting transfers between devices: 9.72 us -> 13.8 us
  waiting for transfers between devices: 5.25 us -> 2.48 us
    all_gather x2 -> x0, blocking collectives: 14.7 us -> none  [the longest x1 12.1 us: local(): everyone = lax.all_gather(slot_anchor, 'seq', axis=2, tiled=True)[0]]
    gather x2 -> x0, local copies, waits for them, and re-layouts: 12.6 us -> none  [fetch_windows(): picked = jnp.take(sources, flat_index.reshape(-1), axis=1)]
    and x8 -> x0, other arithmetic: 8.45 us -> none  [the longest x1 1.4 us: fetch_windows(): usable = in_shard[:, None, :, :] & frame_ok[:, :, None, None]]
    pallas_call x0 -> x3, Pallas kernels: none -> 8.37 us  [the longest x1 4.78 us: local(): pl.pallas_call(functools.partial(decode, n), out_shape=jax.ShapeDtypeStru...]
    ppermute x1 -> x9, starting transfers between devices: 5.78 us -> 13.8 us  [the longest x4 8.16 us: spread(): return lax.ppermute(x, ('seq', 'chan'), pairs)]
    all_to_all x1 -> x0, waiting for transfers between devices: 5.25 us -> none  [fetch_windows(): lax.all_to_all(picked, 'seq', split_axis=1, concat_axis=1, tiled=True)]
    unnamed x19 -> x2, local copies, waits for them, and re-layouts: 4.11 us -> 0.01 us
    psum x1 -> x0, blocking collectives: 4.02 us -> none  [decode_tiles(): colors = lax.psum(partial_colors, 'chan')]
  transfers between devices with their start and end apart: 2 -> 9, of which waited for: 1 -> 3; matrix products, arithmetic and copies ran while one was open for 25% -> 0% of each run, Pallas kernels for 0% -> 14%
where the time goes in v2:
time: 25.5 us; the launch traced here: 25.4 us
  starting transfers between devices  13.8 us (54%)
  Pallas kernels  8.37 us (33%)
  waiting for transfers between devices  2.48 us (10%)
  between operations  0.71 us (3%)
    ppermute x4, starting transfers between devices, spread(): return lax.ppermute(x, ('seq', 'chan'), pairs)  8.16 us
    pallas_call x1, Pallas kernels, local(): pl.pallas_call(functools.partial(decode, n), out_shape=jax.ShapeDtypeStru...  4.78 us
    ppermute x1, starting transfers between devices, local(): lax.ppermute(current, 'tm', [(i, i + 1) for i in range(tm_size - 1)])  4.55 us
    pallas_call x1, Pallas kernels, local(): pl.pallas_call(stage, out_shape=[jax.ShapeDtypeStruct((C_LAT, padded), BF...  2.32 us
    ppermute x4, waiting for transfers between devices, spread(): return lax.ppermute(x, ('seq', 'chan'), pairs)  2.3 us
    pallas_call x1, Pallas kernels, local(): pl.pallas_call(functools.partial(cut_windows, n), out_shape=[message] * (...  1.27 us
    ppermute x4, starting transfers between devices, swapped(): return lax.ppermute(x, 'chan', [(0, 1), (1, 0)])  1.1 us
  transfers between devices with their start and end apart: 9, of which 3 were waited for; matrix products, arithmetic and copies ran while one was open for 0% of the time, Pallas kernels for 14%

profile of v2, /device:TPU:0, one launch (start us, length us, event | category | flops | bytes accessed | tf_op | source)
XLA Modules:
  0.0 25.4 jit_solution(16305481592444900203)
XLA Ops:
  0.0 0.0 copy-start
  0.0 0.5 %collective-permute-start.8 = (bf16[3,3,3,512,128]{4,3,2,1,0:T(8,128)(2,1)}, bf16[3,3,3,512,128]{4,3,2,1,0:T(8,128)(2,1)S(1)}, u32[]{:S(2)}, u32[]{:S(2)}) collective-permute-start(bf16[3,3,3,512,128]{4,3,2,1,0:T(8,128)(2,1)} %refs_4_.1), channel_id=1, source_target_pairs={{0,1},{1,0},{2,3},{3,2},{4,5},{5,4},{6,7},{7,6},{8,9},{9,8},{10,11... | collective-permute-start | bytes 10616840 | tf_op jit(solution)/shard_map/ppermute | solution.py:195
  0.5 4.5 %collective-permute-start.2 = (bf16[16,7200]{1,0:T(8,128)(2,1)}, bf16[16,7200]{1,0:T(8,128)(2,1)S(1)}, u32[]{:S(2)}, u32[]{:S(2)}) collective-permute-start(bf16[16,7200]{1,0:T(8,128)(2,1)} %bitcast.5), channel_id=1, source_target_pairs={{0,2},{1,3},{4,6},{5,7},{8,10},{9,11},{12,14},{13,15},{16,18},{17,... | collective-permute-start | bytes 691208 | tf_op jit(solution)/shard_map/ppermute | solution.py:216
  5.0 0.1 collective-permute-start.6
  5.2 2.6 %collective-permute-start = (s32[3,1,4]{2,1,0:T(1,128)}, s32[3,1,4]{2,1,0:T(1,128)S(1)}, u32[]{:S(2)}, u32[]{:S(2)}) collective-permute-start(s32[3,1,4]{2,1,0:T(1,128)} %bitcast.11), channel_id=1, source_target_pairs={{0,8},{1,9},{4,12},{5,13},{8,0},{9,1},{12,4},{13,5},{2,10},{3,11},... | collective-permute-start | bytes 152 | tf_op jit(solution)/shard_map/ppermute | solution.py:204
  7.7 1.3 %collective-permute-start.1 = (s32[3,1,4]{2,1,0:T(1,128)}, s32[3,1,4]{2,1,0:T(1,128)S(1)}, u32[]{:S(2)}, u32[]{:S(2)}) collective-permute-start(s32[3,1,4]{2,1,0:T(1,128)} %bitcast.12), channel_id=1, source_target_pairs={{0,12},{1,5},{4,0},{5,9},{8,4},{9,13},{12,8},{13,1},{2,14},{3,7},{... | collective-permute-start | bytes 152 | tf_op jit(solution)/shard_map/ppermute | solution.py:204
  9.1 0.8 %collective-permute-done.ready.refs_2_ = s32[3,1,4]{2,1,0:T(1,128)S(1)} collective-permute-done((s32[3,1,4]{2,1,0:T(1,128)}, s32[3,1,4]{2,1,0:T(1,128)S(1)}, u32[]{:S(2)}, u32[]{:S(2)}) %collective-permute-start) | collective-permute-done | bytes 80 | tf_op jit(solution)/shard_map/ppermute | solution.py:204
  9.8 2.3 %stage.1 = (bf16[16,7424]{1,0:T(8,128)(2,1)S(1)}, s32[3,1,4]{2,1,0:T(1,128)S(1)}, bf16[432,256]{1,0:T(8,128)(2,1)S(1)}, bf16[12,128]{1,0:T(8,128)(2,1)S(1)}, bf16[3,3,3,512,128]{4,3,2,1,0:T(8,128)(2,1)S(1)}) custom-call(s32[3,1,4]{2,1,0:T(1,128)S(1)} %collective-permute-done.ready.refs_2_, bf16[16,7200]{1,0:T(8,128)(2,1)} %bitcast.6, s32[3,1,4]{2,1,0:T(1,128)} %bitcast.13, ...), custom_call_target="tpu_custom_call" | custom-call | flops 1 | bytes 1 | tf_op jit(solution)/shard_map/stage/pallas_call | solution.py:220
  12.2 0.0 collective-permute-done.1.refs_1_
  12.2 0.0 collective-permute-done.2.refs_4_
  12.2 1.3 %cut_windows.1 = (bf16[2,4,16,128]{3,2,1,0:T(8,128)(2,1)S(1)}, bf16[2,4,16,128]{3,2,1,0:T(8,128)(2,1)S(1)}, bf16[2,4,16,128]{3,2,1,0:T(8,128)(2,1)S(1)}) custom-call(s32[3,1,4]{2,1,0:T(1,128)S(1)} %get-tuple-element.13.refs_0_, s32[3,1,4]{2,1,0:T(1,128)S(1)} %collective-permute-done.1.refs_1_, s32[3,1,4]{2,1,0:T(1,128)S(1)} %collective-permute-done.ready.refs_2_, ...), custom_call_target="tpu_custom_call" | custom-call | tf_op jit(solution)/shard_map/cut_windows/pallas_call | solution.py:231
  13.5 1.6 %collective-permute-start.3 = (bf16[2,4,16,128]{3,2,1,0:T(8,128)(2,1)S(1)}, bf16[2,4,16,128]{3,2,1,0:T(8,128)(2,1)S(1)}, u32[]{:S(2)}, u32[]{:S(2)}) collective-permute-start(bf16[2,4,16,128]{3,2,1,0:T(8,128)(2,1)S(1)} %get-tuple-element.16), channel_id=1, source_target_pairs={{0,4},{1,13},{4,8},{5,1},{8,12},{9,5},{12,0},{13,9},{2,6},{3,15},{... | collective-permute-start | bytes 98312 | tf_op jit(solution)/shard_map/ppermute | solution.py:204
  15.1 2.6 %collective-permute-start.5 = (bf16[2,4,16,128]{3,2,1,0:T(8,128)(2,1)S(1)}, bf16[2,4,16,128]{3,2,1,0:T(8,128)(2,1)S(1)}, u32[]{:S(2)}, u32[]{:S(2)}) collective-permute-start(bf16[2,4,16,128]{3,2,1,0:T(8,128)(2,1)S(1)} %get-tuple-element.17), channel_id=1, source_target_pairs={{0,8},{1,9},{4,12},{5,13},{8,0},{9,1},{12,4},{13,5},{2,10},{3,11},... | collective-permute-start | bytes 98312 | tf_op jit(solution)/shard_map/ppermute | solution.py:204
  17.7 1.5 %collective-permute-done.3.refs_3_ = bf16[2,4,16,128]{3,2,1,0:T(8,128)(2,1)S(1)} collective-permute-done((bf16[2,4,16,128]{3,2,1,0:T(8,128)(2,1)S(1)}, bf16[2,4,16,128]{3,2,1,0:T(8,128)(2,1)S(1)}, u32[]{:S(2)}, u32[]{:S(2)}) %collective-permute-start.3) | collective-permute-done | bytes 32800 | tf_op jit(solution)/shard_map/ppermute | solution.py:204
  19.2 0.0 collective-permute-start.4
  19.2 0.0 copy-done
  19.2 0.5 %collective-permute-start.7 = (bf16[12,128]{1,0:T(8,128)(2,1)S(1)}, bf16[12,128]{1,0:T(8,128)(2,1)S(1)}, u32[]{:S(2)}, u32[]{:S(2)}) collective-permute-start(bf16[12,128]{1,0:T(8,128)(2,1)S(1)} %bitcast.10), channel_id=1, source_target_pairs={{0,1},{1,0},{2,3},{3,2},{4,5},{5,4},{6,7},{7,6},{8,9},{9,8},{10,11... | collective-permute-start | bytes 9224 | tf_op jit(solution)/shard_map/ppermute | solution.py:195
  20.4 0.2 collective-permute-done.7.refs_9_
  20.6 0.0 collective-permute-done.6.refs_7_
  20.6 0.0 collective-permute-done.5.refs_5_
  20.6 0.0 collective-permute-done.4.refs_4_
  20.6 0.0 collective-permute-done.8.refs_11_
  20.6 4.8 %decode.1 = bf16[1,3,1,4,128]{4,3,2,1,0:T(4,128)(2,1)} custom-call(s32[3,1,4]{2,1,0:T(1,128)S(1)} %get-tuple-element.13.refs_0_, s32[1,1]{1,0:T(1,128)S(6)} %copy.7.refs_1_, bf16[2,4,16,128]{3,2,1,0:T(8,128)(2,1)S(1)} %get-tuple-element.15.refs_2_, bf16[2,4,16,128]{3,2,1,0:T(8,128)(2,1)S(1)} %collective-permute-done.3.refs_3_, ...), custom_call_target="tpu_custom_call" | custom-call | tf_op jit(solution)/shard_map/decode/pallas_call | solution.py:245
Async XLA Ops:
  0.0 19.2 %copy-start = (bf16[128,12]{0,1:T(8,128)(2,1)S(1)}, bf16[128,12]{0,1:T(8,128)(2,1)}, u32[]{:S(2)}) copy-start(bf16[128,12]{0,1:T(8,128)(2,1)} %param.9) | copy-start | bytes 9220
  0.0 20.6 %collective-permute-start.8 = (bf16[3,3,3,512,128]{4,3,2,1,0:T(8,128)(2,1)}, bf16[3,3,3,512,128]{4,3,2,1,0:T(8,128)(2,1)S(1)}, u32[]{:S(2)}, u32[]{:S(2)}) collective-permute-start(bf16[3,3,3,512,128]{4,3,2,1,0:T(8,128)(2,1)} %refs_4_.1), channel_id=1, source_target_pairs={{0,1},{1,0},{2,3},{3,2},{4,5},{5,4},{6,7},{7,6},{8,9},{9,8},{10,11... | collective-permute-start | bytes 10616840 | tf_op jit(solution)/shard_map/ppermute | solution.py:195
  0.5 11.7 %collective-permute-start.2 = (bf16[16,7200]{1,0:T(8,128)(2,1)}, bf16[16,7200]{1,0:T(8,128)(2,1)S(1)}, u32[]{:S(2)}, u32[]{:S(2)}) collective-permute-start(bf16[16,7200]{1,0:T(8,128)(2,1)} %bitcast.5), channel_id=1, source_target_pairs={{0,2},{1,3},{4,6},{5,7},{8,10},{9,11},{12,14},{13,15},{16,18},{17,... | collective-permute-start | bytes 691208 | tf_op jit(solution)/shard_map/ppermute | solution.py:216
  5.0 15.6 %collective-permute-start.6 = (bf16[432,256]{1,0:T(8,128)(2,1)}, bf16[432,256]{1,0:T(8,128)(2,1)S(1)}, u32[]{:S(2)}, u32[]{:S(2)}) collective-permute-start(bf16[432,256]{1,0:T(8,128)(2,1)} %bitcast.7), channel_id=1, source_target_pairs={{0,1},{1,0},{2,3},{3,2},{4,5},{5,4},{6,7},{7,6},{8,9},{9,8},{10,11... | collective-permute-start | bytes 663560 | tf_op jit(solution)/shard_map/ppermute | solution.py:195
  5.2 4.7 %collective-permute-start = (s32[3,1,4]{2,1,0:T(1,128)}, s32[3,1,4]{2,1,0:T(1,128)S(1)}, u32[]{:S(2)}, u32[]{:S(2)}) collective-permute-start(s32[3,1,4]{2,1,0:T(1,128)} %bitcast.11), channel_id=1, source_target_pairs={{0,8},{1,9},{4,12},{5,13},{8,0},{9,1},{12,4},{13,5},{2,10},{3,11},... | collective-permute-start | bytes 152 | tf_op jit(solution)/shard_map/ppermute | solution.py:204
  7.7 4.4 %collective-permute-start.1 = (s32[3,1,4]{2,1,0:T(1,128)}, s32[3,1,4]{2,1,0:T(1,128)S(1)}, u32[]{:S(2)}, u32[]{:S(2)}) collective-permute-start(s32[3,1,4]{2,1,0:T(1,128)} %bitcast.12), channel_id=1, source_target_pairs={{0,12},{1,5},{4,0},{5,9},{8,4},{9,13},{12,8},{13,1},{2,14},{3,7},{... | collective-permute-start | bytes 152 | tf_op jit(solution)/shard_map/ppermute | solution.py:204
  13.5 5.8 %collective-permute-start.3 = (bf16[2,4,16,128]{3,2,1,0:T(8,128)(2,1)S(1)}, bf16[2,4,16,128]{3,2,1,0:T(8,128)(2,1)S(1)}, u32[]{:S(2)}, u32[]{:S(2)}) collective-permute-start(bf16[2,4,16,128]{3,2,1,0:T(8,128)(2,1)S(1)} %get-tuple-element.16), channel_id=1, source_target_pairs={{0,4},{1,13},{4,8},{5,1},{8,12},{9,5},{12,0},{13,9},{2,6},{3,15},{... | collective-permute-start | bytes 98312 | tf_op jit(solution)/shard_map/ppermute | solution.py:204
  15.1 5.5 %collective-permute-start.5 = (bf16[2,4,16,128]{3,2,1,0:T(8,128)(2,1)S(1)}, bf16[2,4,16,128]{3,2,1,0:T(8,128)(2,1)S(1)}, u32[]{:S(2)}, u32[]{:S(2)}) collective-permute-start(bf16[2,4,16,128]{3,2,1,0:T(8,128)(2,1)S(1)} %get-tuple-element.17), channel_id=1, source_target_pairs={{0,8},{1,9},{4,12},{5,13},{8,0},{9,1},{12,4},{13,5},{2,10},{3,11},... | collective-permute-start | bytes 98312 | tf_op jit(solution)/shard_map/ppermute | solution.py:204
  19.2 1.3 %collective-permute-start.4 = (bf16[2,4,16,128]{3,2,1,0:T(8,128)(2,1)S(1)}, bf16[2,4,16,128]{3,2,1,0:T(8,128)(2,1)S(1)}, u32[]{:S(2)}, u32[]{:S(2)}) collective-permute-start(bf16[2,4,16,128]{3,2,1,0:T(8,128)(2,1)S(1)} %collective-permute-done.3.refs_3_), channel_id=1, source_target_pairs={{0,1},{1,0},{2,3},{3,2},{4,5},{5,4},{6,7},{7,6},{8,9},{9,8},{10,11... | collective-permute-start | bytes 98312 | tf_op jit(solution)/shard_map/ppermute | solution.py:195
  19.2 1.3 %collective-permute-start.7 = (bf16[12,128]{1,0:T(8,128)(2,1)S(1)}, bf16[12,128]{1,0:T(8,128)(2,1)S(1)}, u32[]{:S(2)}, u32[]{:S(2)}) collective-permute-start(bf16[12,128]{1,0:T(8,128)(2,1)S(1)} %bitcast.10), channel_id=1, source_target_pairs={{0,1},{1,0},{2,3},{3,2},{4,5},{5,4},{6,7},{7,6},{8,9},{9,8},{10,11... | collective-permute-start | bytes 9224 | tf_op jit(solution)/shard_map/ppermute | solution.py:195

commit v3 on v2

v3 whole, which is shorter than its diff:
```python
import functools

import jax
import jax.numpy as jnp
from jax import lax
from jax.experimental import pallas as pl
from jax.experimental.pallas import tpu as pltpu
from jax.sharding import PartitionSpec as P

H_LAT = 45
W_LAT = 160
C_LAT = 16
C_MID = 512
FG = 4
TH = 2
TW = 16
MAXT = 4
ROWS = TH + 4
COLS = TW + 4
LANES = 128
TAPS = 3
WIDE = 24
ROOM = 2 * MAXT
BF16 = jnp.bfloat16
F32 = jnp.float32
VMEM = pl.BlockSpec(memory_space=pltpu.VMEM)
SMEM = pl.BlockSpec(memory_space=pltpu.SMEM)
HBM = pl.BlockSpec(memory_space=pltpu.HBM)
ANY = pl.BlockSpec(memory_space=pl.ANY)


def lane_ids(rows):
    return lax.broadcasted_iota(jnp.int32, (rows, LANES), 1)


def silu(v):
    return v * (0.5 * jnp.tanh(0.5 * v) + 0.5)


def fetched(sources, targets, sems):
    copies = [pltpu.make_async_copy(*pair, sems.at[i]) for i, pair in enumerate(zip(sources, targets))]
    for copy in copies:
        copy.start()
    return copies


def stage(ready, *refs):
    del ready
    (count, *sources), (cur_out, meta, *outs, cur, anchor, sems) = refs[:6], refs[6:]
    copies = []
    for i, pair in enumerate(zip(sources, (cur, anchor, *outs))):
        copies.append(pltpu.make_async_copy(*pair, sems.at[i]))
        copies[i].start()
    copies[0].wait()
    cur_out[:, : cur.shape[1]] = cur[...]
    copies[1].wait()
    meta[:TAPS] = anchor[...]
    meta[TAPS] = jnp.full(meta.shape[1:], count[0, 0], jnp.int32)
    for copy in copies[2:]:
        copy.wait()


def cut_windows(n, *refs):
    count = n // 2 + 1
    anchors, (cur, prev_ref, pix), outs, prev = refs[:count], refs[count : count + 3], refs[count + 3 : -1], refs[-1]
    shard = prev_ref.shape[1]
    per_frame = n // FG
    part_start = lax.rem(lax.axis_index("seq"), per_frame) * shard
    last_base = (shard - 1) // LANES * LANES
    lane = lane_ids(C_LAT)
    prev[:, :shard] = prev_ref[...]
    for k in range(count):
        anchor = anchors[k][...]
        for i in range(MAXT):
            row0 = anchor[1, 0, i] - 2
            col0 = anchor[2, 0, i] - 2
            first = jnp.maximum(-col0, 0)
            end = jnp.minimum(W_LAT - col0, COLS)
            totals = [jnp.zeros((C_LAT, LANES), BF16)] * 2
            for rho in range(ROWS):
                start = (row0 + rho) * W_LAT + col0 - part_start
                base = jnp.clip(start & -LANES, 0, last_base)
                base = pl.multiple_of(base, LANES)
                off = start - base
                from_low = lane >= off
                least = COLS * rho + jnp.maximum(first, -start)
                past = COLS * rho + jnp.minimum(end, shard - start)
                keep = (lane >= least) & (lane < past)
                for half, source in enumerate((prev, cur)):
                    low = source[:, pl.ds(base, LANES)]
                    high = source[:, pl.ds(base + LANES, LANES)]
                    moved = pltpu.roll(jnp.where(from_low, low, high), (COLS * rho - off) & (LANES - 1), 1)
                    totals[half] = jnp.where(keep, moved, totals[half])
            for half in range(2):
                outs[k][half * MAXT + i] = totals[half]
    for out in outs[1:]:
        out[ROOM] = jnp.concatenate([pix[...], jnp.zeros((C_LAT - pix.shape[0], LANES), BF16)], axis=0)


def decode(n, *refs):
    anchor, parts = refs[0][...], refs[1 : n + 1]
    own_in, other_in, own_pix, own_up, other_up, out, held, *scratch = refs[n + 1 :]
    hiddens, lineds = scratch[:TAPS], scratch[TAPS:]
    per_frame = n // FG
    me = lax.axis_index("seq")
    core = lax.axis_index("chan")
    held[me] = parts[0][...]
    for k in range(1, n // 2):
        by = jnp.where(core == 0, k, n - k)
        held[lax.rem(me + n - by, n)] = parts[2 * k - 1][:ROOM]
        held[lax.rem(me + by, n)] = parts[2 * k][:ROOM]
    held[lax.rem(me + n // 2, n)] = parts[n - 1][:ROOM]
    lane = lane_ids(C_LAT)

    def frame(j):
        pieces = []
        for i in range(MAXT):
            at = jnp.clip(anchor[0, 0, i], 0, FG - 1) + j
            late, rank = at // FG, lax.rem(at, FG) * per_frame
            piece = held[rank, late * MAXT + i]
            for p in range(1, per_frame):
                piece += held[rank + p, late * MAXT + i]
            pieces.append(piece)
        result = []
        for rho in range(ROWS):
            total = None
            for i, piece in enumerate(pieces):
                by = (WIDE * i - COLS * rho) % LANES
                piece = pltpu.roll(piece, by, 1) if by else piece
                total = piece if i == 0 else jnp.where(lane >= WIDE * i, piece, total)
            result.append([total] + [pltpu.roll(total, LANES - c, 1) for c in range(1, TAPS)])
        return result

    def turned(pieces):
        zeros = [jnp.zeros((C_LAT, LANES), BF16)] * (LANES // C_LAT - len(pieces))
        return jnp.concatenate(pieces + zeros, axis=0).T[: MAXT * WIDE]

    taps = [(b, c) for b in range(TAPS) for c in range(TAPS)]
    spots = range(TH + 2)
    frames = [frame(j) for j in range(TAPS + 2)]
    cells = [
        jnp.concatenate([turned([frames[j][r + b][c] for b, c in taps[:-1]]) for r in spots], axis=0)
        for j in range(TAPS + 2)
    ]
    tail = jnp.concatenate([turned([frames[j][r + 2][2] for j in range(TAPS + 2)]) for r in spots], axis=0)
    x = lax.broadcasted_iota(jnp.int32, (WIDE, LANES), 0)
    quarter, half = C_MID // 4, C_MID // 2
    for t in range(TAPS):
        volume = jnp.concatenate([*cells[t : t + TAPS], tail], axis=1)
        hidden, lined = hiddens[t], lineds[t]
        for first, weights in enumerate((own_in, other_in)):
            per_tap = len(taps) * C_LAT
            kernel = [weights[a * per_tap : a * per_tap + LANES] for a in range(TAPS)]
            for j in range(LANES // C_LAT):
                a = j - t
                ends = weights[a * per_tap + LANES : (a + 1) * per_tap] if 0 <= a < TAPS else None
                kernel.append(jnp.zeros((C_LAT, half), BF16) if ends is None else ends)
            pre = jnp.dot(volume, jnp.concatenate(kernel, axis=0), preferred_element_type=F32)
            for r in spots:
                for i in range(MAXT):
                    row = anchor[1, 0, i] - 1 + r
                    col = anchor[2, 0, i] - 1 + x
                    width = jnp.where((row >= 0) & (row < H_LAT), W_LAT, 0)
                    at = (r * MAXT + i) * WIDE
                    value = silu(pre[at : at + WIDE])
                    for q in range(2):
                        hidden[r * MAXT + i, 2 * first + q] = jnp.where(
                            (col >= 0) & (col < width), value[:, q * quarter : (q + 1) * quarter], 0.0
                        )
        for c in range(TAPS):
            for ri in range((TH + 2) * MAXT):
                for q in range(4):
                    lined[c, ri * TW : (ri + 1) * TW, q * quarter : (q + 1) * quarter] = hidden[
                        ri, q, c : c + TW
                    ].astype(BF16)
    outs = own_up.shape[-1]
    span = MAXT * TW
    total = jnp.zeros((TH * span, 2 * outs), F32)
    for a in range(TAPS):
        for c in range(TAPS):
            for b in range(TAPS):
                rows = lineds[a][c, b * span : (b + TH) * span]
                for first in range(2):
                    here = pl.ds(pl.multiple_of((first ^ core) * half, half), half)
                    weights = jnp.concatenate([own_up[a, b, c, here], other_up[a, b, c, here]], axis=1)
                    total += jnp.dot(rows[:, first * half : (first + 1) * half], weights, preferred_element_type=F32)
    upper = silu(total).astype(BF16)
    row = lax.broadcasted_iota(jnp.int32, (32, 12), 0)
    col = lax.broadcasted_iota(jnp.int32, (32, 12), 1)
    pick = ((row % 8) * 4 + row // 8 == col) & (row % 8 < 3)
    pix = jnp.concatenate([own_pix[...], parts[2][ROOM, : own_pix.shape[0]]], axis=1)
    pix = jnp.dot(pick.astype(BF16), pix, preferred_element_type=F32).astype(BF16)
    colors = lax.dot_general(pix, upper, (((1,), (1,)), ((), ())), preferred_element_type=F32)
    colors = colors.astype(BF16).astype(F32)
    lane = lane_ids(8)
    p, q = (lane // 32) % 2, lane % 2
    for i in range(MAXT):
        source = (lane // 64) * span + i * TW + (lane % 32) // 2
        pixel = jnp.zeros((8, LANES), F32)
        for pq in range(4):
            found = jnp.take_along_axis(colors[8 * pq : 8 * pq + 8], source, axis=1)
            pixel = jnp.where(2 * p + q == pq, found, pixel)
        pixel = jnp.where(i < anchor[TAPS, 0, 0], pixel, 0.0).astype(BF16)
        for e in range(3):
            out[0, e, 0, i : i + 1] = pixel[e : e + 1]


def in_hbm(x):
    return pltpu.with_memory_space_constraint(x, pltpu.HBM)


def swapped(x):
    return lax.ppermute(x, "chan", [(0, 1), (1, 0)])


def spread(x, by):
    size = lax.axis_size("seq")
    pairs = []
    for at in range(size):
        pairs.append((2 * at, 2 * ((at + by) % size)))
        pairs.append((2 * at + 1, 2 * ((at - by) % size) + 1))
    return lax.ppermute(x, ("seq", "chan"), pairs)


def local(latents, conv_in, conv_up, to_pixels, slot_anchor, slot_count):
    n = lax.axis_size("seq")
    current = latents[0]
    shard = current.shape[1]
    anchor = slot_anchor.transpose(1, 0, 2)
    in_flat = conv_in.reshape(-1, conv_in.shape[-1])
    pix = to_pixels.T
    anchors = [spread(anchor, -k) for k in range(1, n // 2 + 1)]
    tm_size = lax.axis_size("tm")
    previous = lax.ppermute(current, "tm", [(i, i + 1) for i in range(tm_size - 1)])
    other_in, other_up = swapped(in_flat), swapped(conv_up)
    padded = (shard - 1) // LANES * LANES + 2 * LANES
    own = (in_flat, pix, conv_up)
    cur_pad, meta, own_in, own_pix, own_up = pl.pallas_call(
        stage,
        out_shape=[
            jax.ShapeDtypeStruct((C_LAT, padded), BF16),
            jax.ShapeDtypeStruct((TAPS + 1, *anchor.shape[1:]), jnp.int32),
            *(jax.ShapeDtypeStruct(x.shape, BF16) for x in own),
        ],
        in_specs=[ANY, SMEM] + [HBM] * 5,
        out_specs=[VMEM] * 5,
        scratch_shapes=[
            pltpu.VMEM(current.shape, BF16),
            pltpu.VMEM(anchor.shape, jnp.int32),
            pltpu.SemaphoreType.DMA((5,)),
        ],
        compiler_params=pltpu.CompilerParams(vmem_limit_bytes=8 << 20),
        cost_estimate=pl.CostEstimate(flops=1, bytes_accessed=1, transcendentals=0),
        name="stage",
    )(anchors[-1], slot_count, *map(in_hbm, (current, anchor, *own)))
    message = jax.ShapeDtypeStruct((ROOM, C_LAT, LANES), BF16)
    extended = jax.ShapeDtypeStruct((ROOM + 1, C_LAT, LANES), BF16)
    cut = pl.pallas_call(
        functools.partial(cut_windows, n),
        out_shape=[message] + [extended] * (n // 2),
        in_specs=[VMEM] * (n // 2 + 4),
        out_specs=[VMEM] * (n // 2 + 1),
        scratch_shapes=[pltpu.VMEM((C_LAT, padded), BF16)],
        compiler_params=pltpu.CompilerParams(vmem_limit_bytes=4 << 20),
        name="cut_windows",
    )(meta, *anchors, cur_pad, previous, own_pix)
    parts = [cut[0]]
    for k in range(1, n // 2):
        arrived = spread(cut[k], k)
        parts += [arrived, swapped(arrived)]
    parts.append(spread(cut[n // 2], n // 2))
    pixels = pl.pallas_call(
        functools.partial(decode, n),
        out_shape=jax.ShapeDtypeStruct((1, 3, 1, MAXT, LANES), BF16),
        in_specs=[VMEM] * (n + 6),
        out_specs=VMEM,
        scratch_shapes=[
            pltpu.VMEM((n,) + message.shape, BF16),
        ]
        + [pltpu.VMEM(((TH + 2) * MAXT, 4, WIDE, C_MID // 4), F32)] * TAPS
        + [pltpu.VMEM((TAPS, (TH + 2) * MAXT * TW, C_MID), BF16)] * TAPS,
        compiler_params=pltpu.CompilerParams(vmem_limit_bytes=32 << 20),
        name="decode",
    )(meta, *parts, own_in, other_in, own_pix, own_up, other_up)
    return pixels.transpose(0, 3, 1, 2, 4)


def solution(mesh):
    placed = (
        P(("clip", "tm"), None, "seq"),
        P(None, None, None, None, "chan"),
        P(None, None, None, None, "chan"),
        P("chan", None),
        P(("clip", "tm"), None, "seq"),
        P(("clip", "tm"), "seq"),
    )
    return jax.shard_map(
        local,
        mesh=mesh,
        in_specs=placed,
        out_specs=P(("clip", "tm"), "seq", None, None, None),
        check_vma=False,
    )
```

time: 25.5 us -> 24 us (0.941)
  Pallas kernels: 8.37 us -> 6.96 us
  starting transfers between devices: 13.8 us -> 13.3 us
  waiting for transfers between devices: 2.48 us -> 2.91 us
    pallas_call x1, Pallas kernels: 4.78 us -> 3.89 us  [local(): pl.pallas_call(functools.partial(decode, n), out_shape=jax.ShapeDtypeStru...]
    pallas_call x1, Pallas kernels: 1.27 us -> 0.74 us  [local(): pl.pallas_call(functools.partial(cut_windows, n), out_shape=[message] + [...]
    ppermute x4, waiting for transfers between devices: 2.3 us -> 2.67 us  [spread(): return lax.ppermute(x, ('seq', 'chan'), pairs)]
    ppermute x4 -> x3, starting transfers between devices: 1.1 us -> 0.75 us  [swapped(): return lax.ppermute(x, 'chan', [(0, 1), (1, 0)])]
  transfers between devices with their start and end apart: 9 -> 8, of which waited for: 3 -> 4; matrix products, arithmetic and copies ran while one was open for 0% -> 0% of each run, Pallas kernels for 14% -> 13%
where the time goes in v3:
time: 24 us; the launch traced here: 23.9 us
  starting transfers between devices  13.3 us (55%)
  Pallas kernels  6.96 us (29%)
  waiting for transfers between devices  2.91 us (12%)
  between operations  0.7 us (3%)
    ppermute x4, starting transfers between devices, spread(): return lax.ppermute(x, ('seq', 'chan'), pairs)  8.16 us
    ppermute x1, starting transfers between devices, local(): lax.ppermute(current, 'tm', [(i, i + 1) for i in range(tm_size - 1)])  4.39 us
    pallas_call x1, Pallas kernels, local(): pl.pallas_call(functools.partial(decode, n), out_shape=jax.ShapeDtypeStru...  3.89 us
    ppermute x4, waiting for transfers between devices, spread(): return lax.ppermute(x, ('seq', 'chan'), pairs)  2.67 us
    pallas_call x1, Pallas kernels, local(): pl.pallas_call(stage, out_shape=[jax.ShapeDtypeStruct((C_LAT, padded), BF...  2.32 us
    ppermute x3, starting transfers between devices, swapped(): return lax.ppermute(x, 'chan', [(0, 1), (1, 0)])  0.75 us
    pallas_call x1, Pallas kernels, local(): pl.pallas_call(functools.partial(cut_windows, n), out_shape=[message] + [...  0.74 us
  transfers between devices with their start and end apart: 8, of which 4 were waited for; matrix products, arithmetic and copies ran while one was open for 0% of the time, Pallas kernels for 13%

profile of v3, /device:TPU:0, one launch (start us, length us, event | category | flops | bytes accessed | tf_op | source)
XLA Modules:
  0.0 23.9 jit_solution(3846358148695403513)
XLA Ops:
  0.0 0.5 %collective-permute-start.7 = (bf16[3,3,3,512,128]{4,3,2,1,0:T(8,128)(2,1)}, bf16[3,3,3,512,128]{4,3,2,1,0:T(8,128)(2,1)S(1)}, u32[]{:S(2)}, u32[]{:S(2)}) collective-permute-start(bf16[3,3,3,512,128]{4,3,2,1,0:T(8,128)(2,1)} %refs_5_.1), channel_id=1, source_target_pairs={{0,1},{1,0},{2,3},{3,2},{4,5},{5,4},{6,7},{7,6},{8,9},{9,8},{10,11... | collective-permute-start | bytes 10616840 | tf_op jit(solution)/shard_map/ppermute | solution.py:213
  0.5 4.4 %collective-permute-start.2 = (bf16[16,7200]{1,0:T(8,128)(2,1)}, bf16[16,7200]{1,0:T(8,128)(2,1)S(1)}, u32[]{:S(2)}, u32[]{:S(2)}) collective-permute-start(bf16[16,7200]{1,0:T(8,128)(2,1)} %bitcast.5), channel_id=1, source_target_pairs={{0,2},{1,3},{4,6},{5,7},{8,10},{9,11},{12,14},{13,15},{16,18},{17,... | collective-permute-start | bytes 691208 | tf_op jit(solution)/shard_map/ppermute | solution.py:234
  4.9 0.3 %collective-permute-start.6 = (bf16[432,256]{1,0:T(8,128)(2,1)}, bf16[432,256]{1,0:T(8,128)(2,1)S(1)}, u32[]{:S(2)}, u32[]{:S(2)}) collective-permute-start(bf16[432,256]{1,0:T(8,128)(2,1)} %bitcast.7), channel_id=1, source_target_pairs={{0,1},{1,0},{2,3},{3,2},{4,5},{5,4},{6,7},{7,6},{8,9},{9,8},{10,11... | collective-permute-start | bytes 663560 | tf_op jit(solution)/shard_map/ppermute | solution.py:213
  5.1 2.6 %collective-permute-start = (s32[3,1,4]{2,1,0:T(1,128)}, s32[3,1,4]{2,1,0:T(1,128)S(1)}, u32[]{:S(2)}, u32[]{:S(2)}) collective-permute-start(s32[3,1,4]{2,1,0:T(1,128)} %bitcast.10), channel_id=1, source_target_pairs={{0,8},{1,9},{4,12},{5,13},{8,0},{9,1},{12,4},{13,5},{2,10},{3,11},... | collective-permute-start | bytes 152 | tf_op jit(solution)/shard_map/ppermute | solution.py:222
  7.7 1.3 %collective-permute-start.1 = (s32[3,1,4]{2,1,0:T(1,128)}, s32[3,1,4]{2,1,0:T(1,128)S(1)}, u32[]{:S(2)}, u32[]{:S(2)}) collective-permute-start(s32[3,1,4]{2,1,0:T(1,128)} %bitcast.11), channel_id=1, source_target_pairs={{0,12},{1,5},{4,0},{5,9},{8,4},{9,13},{12,8},{13,1},{2,14},{3,7},{... | collective-permute-start | bytes 152 | tf_op jit(solution)/shard_map/ppermute | solution.py:222
  9.7 0.1 collective-permute-done.ready.refs_2_
  9.8 2.3 %stage.1 = (bf16[16,7424]{1,0:T(8,128)(2,1)S(1)}, s32[4,1,4]{2,1,0:T(1,128)S(1)}, bf16[432,256]{1,0:T(8,128)(2,1)S(1)}, bf16[12,128]{1,0:T(8,128)(2,1)S(1)}, bf16[3,3,3,512,128]{4,3,2,1,0:T(8,128)(2,1)S(1)}) custom-call(s32[3,1,4]{2,1,0:T(1,128)S(1)} %collective-permute-done.ready.refs_2_, s32[1,1]{1,0:T(1,128)S(6)} %copy.7.refs_0_, ...), custom_call_target="tpu_custom_call" | custom-call | flops 1 | bytes 1 | tf_op jit(solution)/shard_map/stage/pallas_call | solution.py:238
  12.2 0.0 collective-permute-done.1.refs_1_
  12.2 0.0 collective-permute-done.2.refs_4_
  12.2 0.7 %cut_windows.1 = (bf16[8,16,128]{2,1,0:T(8,128)(2,1)S(1)}, bf16[9,16,128]{2,1,0:T(8,128)(2,1)S(1)}, bf16[9,16,128]{2,1,0:T(8,128)(2,1)S(1)}) custom-call(s32[4,1,4]{2,1,0:T(1,128)S(1)} %get-tuple-element.13.refs_0_, s32[3,1,4]{2,1,0:T(1,128)S(1)} %collective-permute-done.1.refs_1_, s32[3,1,4]{2,1,0:T(1,128)S(1)} %collective-permute-done.ready.refs_2_, ...), custom_call_target="tpu_custom_call" | custom-call | tf_op jit(solution)/shard_map/cut_windows/pallas_call | solution.py:258
  12.9 1.6 %collective-permute-start.3 = (bf16[9,16,128]{2,1,0:T(8,128)(2,1)S(1)}, bf16[9,16,128]{2,1,0:T(8,128)(2,1)S(1)}, u32[]{:S(2)}, u32[]{:S(2)}) collective-permute-start(bf16[9,16,128]{2,1,0:T(8,128)(2,1)S(1)} %get-tuple-element.17), channel_id=1, source_target_pairs={{0,4},{1,13},{4,8},{5,1},{8,12},{9,5},{12,0},{13,9},{2,6},{3,15},{... | collective-permute-start | bytes 110600 | tf_op jit(solution)/shard_map/ppermute | solution.py:222
  14.6 2.6 %collective-permute-start.5 = (bf16[9,16,128]{2,1,0:T(8,128)(2,1)S(1)}, bf16[9,16,128]{2,1,0:T(8,128)(2,1)S(1)}, u32[]{:S(2)}, u32[]{:S(2)}) collective-permute-start(bf16[9,16,128]{2,1,0:T(8,128)(2,1)S(1)} %get-tuple-element.18), channel_id=1, source_target_pairs={{0,8},{1,9},{4,12},{5,13},{8,0},{9,1},{12,4},{13,5},{2,10},{3,11},... | collective-permute-start | bytes 110600 | tf_op jit(solution)/shard_map/ppermute | solution.py:222
  17.2 1.6 %collective-permute-done.3.refs_2_ = bf16[9,16,128]{2,1,0:T(8,128)(2,1)S(1)} collective-permute-done((bf16[9,16,128]{2,1,0:T(8,128)(2,1)S(1)}, bf16[9,16,128]{2,1,0:T(8,128)(2,1)S(1)}, u32[]{:S(2)}, u32[]{:S(2)}) %collective-permute-start.3) | collective-permute-done | bytes 36896 | tf_op jit(solution)/shard_map/ppermute | solution.py:222
  18.7 0.0 collective-permute-start.4
  18.8 0.0 collective-permute-done.6.refs_6_
  18.8 1.0 %collective-permute-done.5.refs_4_ = bf16[9,16,128]{2,1,0:T(8,128)(2,1)S(1)} collective-permute-done((bf16[9,16,128]{2,1,0:T(8,128)(2,1)S(1)}, bf16[9,16,128]{2,1,0:T(8,128)(2,1)S(1)}, u32[]{:S(2)}, u32[]{:S(2)}) %collective-permute-start.5) | collective-permute-done | bytes 36896 | tf_op jit(solution)/shard_map/ppermute | solution.py:222
  19.7 0.2 collective-permute-done.4.refs_3_
  20.0 0.0 collective-permute-done.7.refs_9_
  20.0 3.9 %decode.1 = bf16[1,3,1,4,128]{4,3,2,1,0:T(4,128)(2,1)} custom-call(s32[4,1,4]{2,1,0:T(1,128)S(1)} %get-tuple-element.13.refs_0_, bf16[8,16,128]{2,1,0:T(8,128)(2,1)S(1)} %get-tuple-element.16.refs_1_, bf16[9,16,128]{2,1,0:T(8,128)(2,1)S(1)} %collective-permute-done.3.refs_2_, bf16[9,16,128]{2,1,0:T(8,128)(2,1)S(1)} %collective-permute-done.4.refs_3_, ...), custom_call_target="tpu_custom_call" | custom-call | tf_op jit(solution)/shard_map/decode/pallas_call | solution.py:272
Async XLA Ops:
  0.0 20.0 %collective-permute-start.7 = (bf16[3,3,3,512,128]{4,3,2,1,0:T(8,128)(2,1)}, bf16[3,3,3,512,128]{4,3,2,1,0:T(8,128)(2,1)S(1)}, u32[]{:S(2)}, u32[]{:S(2)}) collective-permute-start(bf16[3,3,3,512,128]{4,3,2,1,0:T(8,128)(2,1)} %refs_5_.1), channel_id=1, source_target_pairs={{0,1},{1,0},{2,3},{3,2},{4,5},{5,4},{6,7},{7,6},{8,9},{9,8},{10,11... | collective-permute-start | bytes 10616840 | tf_op jit(solution)/shard_map/ppermute | solution.py:213
  0.5 11.7 %collective-permute-start.2 = (bf16[16,7200]{1,0:T(8,128)(2,1)}, bf16[16,7200]{1,0:T(8,128)(2,1)S(1)}, u32[]{:S(2)}, u32[]{:S(2)}) collective-permute-start(bf16[16,7200]{1,0:T(8,128)(2,1)} %bitcast.5), channel_id=1, source_target_pairs={{0,2},{1,3},{4,6},{5,7},{8,10},{9,11},{12,14},{13,15},{16,18},{17,... | collective-permute-start | bytes 691208 | tf_op jit(solution)/shard_map/ppermute | solution.py:234
  4.9 13.9 %collective-permute-start.6 = (bf16[432,256]{1,0:T(8,128)(2,1)}, bf16[432,256]{1,0:T(8,128)(2,1)S(1)}, u32[]{:S(2)}, u32[]{:S(2)}) collective-permute-start(bf16[432,256]{1,0:T(8,128)(2,1)} %bitcast.7), channel_id=1, source_target_pairs={{0,1},{1,0},{2,3},{3,2},{4,5},{5,4},{6,7},{7,6},{8,9},{9,8},{10,11... | collective-permute-start | bytes 663560 | tf_op jit(solution)/shard_map/ppermute | solution.py:213
  5.1 4.7 %collective-permute-start = (s32[3,1,4]{2,1,0:T(1,128)}, s32[3,1,4]{2,1,0:T(1,128)S(1)}, u32[]{:S(2)}, u32[]{:S(2)}) collective-permute-start(s32[3,1,4]{2,1,0:T(1,128)} %bitcast.10), channel_id=1, source_target_pairs={{0,8},{1,9},{4,12},{5,13},{8,0},{9,1},{12,4},{13,5},{2,10},{3,11},... | collective-permute-start | bytes 152 | tf_op jit(solution)/shard_map/ppermute | solution.py:222
  7.7 4.4 %collective-permute-start.1 = (s32[3,1,4]{2,1,0:T(1,128)}, s32[3,1,4]{2,1,0:T(1,128)S(1)}, u32[]{:S(2)}, u32[]{:S(2)}) collective-permute-start(s32[3,1,4]{2,1,0:T(1,128)} %bitcast.11), channel_id=1, source_target_pairs={{0,12},{1,5},{4,0},{5,9},{8,4},{9,13},{12,8},{13,1},{2,14},{3,7},{... | collective-permute-start | bytes 152 | tf_op jit(solution)/shard_map/ppermute | solution.py:222
  12.9 5.8 %collective-permute-start.3 = (bf16[9,16,128]{2,1,0:T(8,128)(2,1)S(1)}, bf16[9,16,128]{2,1,0:T(8,128)(2,1)S(1)}, u32[]{:S(2)}, u32[]{:S(2)}) collective-permute-start(bf16[9,16,128]{2,1,0:T(8,128)(2,1)S(1)} %get-tuple-element.17), channel_id=1, source_target_pairs={{0,4},{1,13},{4,8},{5,1},{8,12},{9,5},{12,0},{13,9},{2,6},{3,15},{... | collective-permute-start | bytes 110600 | tf_op jit(solution)/shard_map/ppermute | solution.py:222
  14.6 5.2 %collective-permute-start.5 = (bf16[9,16,128]{2,1,0:T(8,128)(2,1)S(1)}, bf16[9,16,128]{2,1,0:T(8,128)(2,1)S(1)}, u32[]{:S(2)}, u32[]{:S(2)}) collective-permute-start(bf16[9,16,128]{2,1,0:T(8,128)(2,1)S(1)} %get-tuple-element.18), channel_id=1, source_target_pairs={{0,8},{1,9},{4,12},{5,13},{8,0},{9,1},{12,4},{13,5},{2,10},{3,11},... | collective-permute-start | bytes 110600 | tf_op jit(solution)/shard_map/ppermute | solution.py:222
  18.7 1.2 %collective-permute-start.4 = (bf16[9,16,128]{2,1,0:T(8,128)(2,1)S(1)}, bf16[9,16,128]{2,1,0:T(8,128)(2,1)S(1)}, u32[]{:S(2)}, u32[]{:S(2)}) collective-permute-start(bf16[9,16,128]{2,1,0:T(8,128)(2,1)S(1)} %collective-permute-done.3.refs_2_), channel_id=1, source_target_pairs={{0,1},{1,0},{2,3},{3,2},{4,5},{5,4},{6,7},{7,6},{8,9},{9,8},{10,11... | collective-permute-start | bytes 110600 | tf_op jit(solution)/shard_map/ppermute | solution.py:213

commit v4 on v3

--- a/solution.py
+++ b/solution.py
@@ -44,24 +44,20 @@
     return copies
 
 
-def stage(ready, *refs):
-    del ready
-    (count, *sources), (cur_out, meta, *outs, cur, anchor, sems) = refs[:6], refs[6:]
+def stage(*refs):
+    sources, (cur_out, *outs, cur, sems) = refs[:5], refs[5:]
     copies = []
-    for i, pair in enumerate(zip(sources, (cur, anchor, *outs))):
+    for i, pair in enumerate(zip(sources, (cur, *outs))):
         copies.append(pltpu.make_async_copy(*pair, sems.at[i]))
         copies[i].start()
     copies[0].wait()
     cur_out[:, : cur.shape[1]] = cur[...]
-    copies[1].wait()
-    meta[:TAPS] = anchor[...]
-    meta[TAPS] = jnp.full(meta.shape[1:], count[0, 0], jnp.int32)
-    for copy in copies[2:]:
+    for copy in copies[1:]:
         copy.wait()
 
 
 def cut_windows(n, *refs):
-    count = n // 2 + 1
+    count = (len(refs) - 4) // 2
     anchors, (cur, prev_ref, pix), outs, prev = refs[:count], refs[count : count + 3], refs[count + 3 : -1], refs[-1]
     shard = prev_ref.shape[1]
     per_frame = n // FG
@@ -93,23 +89,22 @@
                     totals[half] = jnp.where(keep, moved, totals[half])
             for half in range(2):
                 outs[k][half * MAXT + i] = totals[half]
-    for out in outs[1:]:
+    for out in outs if outs[0].shape[0] > ROOM else ():
         out[ROOM] = jnp.concatenate([pix[...], jnp.zeros((C_LAT - pix.shape[0], LANES), BF16)], axis=0)
 
 
 def decode(n, *refs):
-    anchor, parts = refs[0][...], refs[1 : n + 1]
-    own_in, other_in, own_pix, own_up, other_up, out, held, *scratch = refs[n + 1 :]
+    count, anchor, parts = refs[0], refs[1][...], refs[2 : n + 2]
+    own_in, other_in, own_pix, own_up, other_up, out, held, *scratch = refs[n + 2 :]
     hiddens, lineds = scratch[:TAPS], scratch[TAPS:]
     per_frame = n // FG
     me = lax.axis_index("seq")
     core = lax.axis_index("chan")
     held[me] = parts[0][...]
     for k in range(1, n // 2):
-        by = jnp.where(core == 0, k, n - k)
-        held[lax.rem(me + n - by, n)] = parts[2 * k - 1][:ROOM]
-        held[lax.rem(me + by, n)] = parts[2 * k][:ROOM]
-    held[lax.rem(me + n // 2, n)] = parts[n - 1][:ROOM]
+        held[me ^ (2 * k - 1 + core)] = parts[2 * k - 1][:ROOM]
+        held[me ^ (2 * k - core)] = parts[2 * k][:ROOM]
+    held[me ^ (n - 1)] = parts[n - 1][:ROOM]
     lane = lane_ids(C_LAT)
 
     def frame(j):
@@ -200,7 +195,7 @@
         for pq in range(4):
             found = jnp.take_along_axis(colors[8 * pq : 8 * pq + 8], source, axis=1)
             pixel = jnp.where(2 * p + q == pq, found, pixel)
-        pixel = jnp.where(i < anchor[TAPS, 0, 0], pixel, 0.0).astype(BF16)
+        pixel = jnp.where(i < count[0, 0], pixel, 0.0).astype(BF16)
         for e in range(3):
             out[0, e, 0, i : i + 1] = pixel[e : e + 1]
 
@@ -213,12 +208,11 @@
     return lax.ppermute(x, "chan", [(0, 1), (1, 0)])
 
 
-def spread(x, by):
-    size = lax.axis_size("seq")
+def spread(x, first, second):
     pairs = []
-    for at in range(size):
-        pairs.append((2 * at, 2 * ((at + by) % size)))
-        pairs.append((2 * at + 1, 2 * ((at - by) % size) + 1))
+    for at in range(lax.axis_size("seq")):
+        pairs.append((2 * at, 2 * (at ^ first)))
+        pairs.append((2 * at + 1, 2 * (at ^ second) + 1))
     return lax.ppermute(x, ("seq", "chan"), pairs)
 
 
@@ -229,59 +223,61 @@
     anchor = slot_anchor.transpose(1, 0, 2)
     in_flat = conv_in.reshape(-1, conv_in.shape[-1])
     pix = to_pixels.T
-    anchors = [spread(anchor, -k) for k in range(1, n // 2 + 1)]
+    routes = [(2 * k - 1, 2 * k) for k in range(1, n // 2)] + [(n - 1, n - 1)]
+    anchors = [spread(anchor, *route) for route in routes]
     tm_size = lax.axis_size("tm")
     previous = lax.ppermute(current, "tm", [(i, i + 1) for i in range(tm_size - 1)])
     other_in, other_up = swapped(in_flat), swapped(conv_up)
     padded = (shard - 1) // LANES * LANES + 2 * LANES
-    own = (in_flat, pix, conv_up)
-    cur_pad, meta, own_in, own_pix, own_up = pl.pallas_call(
+    own = (current, anchor, in_flat, pix, conv_up)
+    cur_pad, anchor, own_in, own_pix, own_up = pl.pallas_call(
         stage,
         out_shape=[
             jax.ShapeDtypeStruct((C_LAT, padded), BF16),
-            jax.ShapeDtypeStruct((TAPS + 1, *anchor.shape[1:]), jnp.int32),
-            *(jax.ShapeDtypeStruct(x.shape, BF16) for x in own),
+            *(jax.ShapeDtypeStruct(x.shape, x.dtype) for x in own[1:]),
         ],
-        in_specs=[ANY, SMEM] + [HBM] * 5,
+        in_specs=[HBM] * 5,
         out_specs=[VMEM] * 5,
         scratch_shapes=[
             pltpu.VMEM(current.shape, BF16),
-            pltpu.VMEM(anchor.shape, jnp.int32),
             pltpu.SemaphoreType.DMA((5,)),
         ],
         compiler_params=pltpu.CompilerParams(vmem_limit_bytes=8 << 20),
         cost_estimate=pl.CostEstimate(flops=1, bytes_accessed=1, transcendentals=0),
         name="stage",
-    )(anchors[-1], slot_count, *map(in_hbm, (current, anchor, *own)))
-    message = jax.ShapeDtypeStruct((ROOM, C_LAT, LANES), BF16)
+    )(*map(in_hbm, own))
+    plain = jax.ShapeDtypeStruct((ROOM, C_LAT, LANES), BF16)
     extended = jax.ShapeDtypeStruct((ROOM + 1, C_LAT, LANES), BF16)
-    cut = pl.pallas_call(
-        functools.partial(cut_windows, n),
-        out_shape=[message] + [extended] * (n // 2),
-        in_specs=[VMEM] * (n // 2 + 4),
-        out_specs=[VMEM] * (n // 2 + 1),
-        scratch_shapes=[pltpu.VMEM((C_LAT, padded), BF16)],
-        compiler_params=pltpu.CompilerParams(vmem_limit_bytes=4 << 20),
-        name="cut_windows",
-    )(meta, *anchors, cur_pad, previous, own_pix)
+    cut = []
+    for targets, shape, name in (([anchor], plain, "cut_own"), (anchors, extended, "cut_windows")):
+        cut += pl.pallas_call(
+            functools.partial(cut_windows, n),
+            out_shape=[shape] * len(targets),
+            in_specs=[VMEM] * (len(targets) + 3),
+            out_specs=[VMEM] * len(targets),
+            scratch_shapes=[pltpu.VMEM((C_LAT, padded), BF16)],
+            compiler_params=pltpu.CompilerParams(vmem_limit_bytes=4 << 20),
+            cost_estimate=pl.CostEstimate(flops=1, bytes_accessed=1, transcendentals=0),
+            name=name,
+        )(*targets, cur_pad, previous, own_pix)
     parts = [cut[0]]
-    for k in range(1, n // 2):
-        arrived = spread(cut[k], k)
+    for message, route in zip(cut[1:], routes[:-1]):
+        arrived = spread(message, *route)
         parts += [arrived, swapped(arrived)]
-    parts.append(spread(cut[n // 2], n // 2))
+    parts.append(spread(cut[-1], *routes[-1]))
     pixels = pl.pallas_call(
         functools.partial(decode, n),
         out_shape=jax.ShapeDtypeStruct((1, 3, 1, MAXT, LANES), BF16),
-        in_specs=[VMEM] * (n + 6),
+        in_specs=[SMEM] + [VMEM] * (n + 6),
         out_specs=VMEM,
         scratch_shapes=[
-            pltpu.VMEM((n,) + message.shape, BF16),
+            pltpu.VMEM((n,) + plain.shape, BF16),
         ]
         + [pltpu.VMEM(((TH + 2) * MAXT, 4, WIDE, C_MID // 4), F32)] * TAPS
         + [pltpu.VMEM((TAPS, (TH + 2) * MAXT * TW, C_MID), BF16)] * TAPS,
         compiler_params=pltpu.CompilerParams(vmem_limit_bytes=32 << 20),
         name="decode",
-    )(meta, *parts, own_in, other_in, own_pix, own_up, other_up)
+    )(slot_count, anchor, *parts, own_in, other_in, own_pix, own_up, other_up)
     return pixels.transpose(0, 3, 1, 2, 4)
 
 

time: 24 us -> 22.8 us (0.950)
  starting transfers between devices: 13.3 us -> 11.8 us
    ppermute x4, starting transfers between devices: 8.16 us -> 6.67 us  [spread(): return lax.ppermute(x, ('seq', 'chan'), pairs)]
    ppermute x4, waiting for transfers between devices: 2.67 us -> 3.13 us  [spread(): return lax.ppermute(x, ('seq', 'chan'), pairs)]
    pallas_call x1 -> x2, Pallas kernels: 0.74 us -> 0.82 us  [local(): pl.pallas_call(functools.partial(cut_windows, n), out_shape=[shape] * len...]
  transfers between devices with their start and end apart: 8 -> 8, of which waited for: 4 -> 3; matrix products, arithmetic and copies ran while one was open for 0% -> 0% of each run, Pallas kernels for 13% -> 14%
where the time goes in v4:
time: 22.8 us; the launch traced here: 22.7 us
  starting transfers between devices  11.8 us (52%)
  Pallas kernels  7.03 us (31%)
  waiting for transfers between devices  3.14 us (14%)
  between operations  0.69 us (3%)
    ppermute x4, starting transfers between devices, spread(): return lax.ppermute(x, ('seq', 'chan'), pairs)  6.67 us
    ppermute x1, starting transfers between devices, local(): lax.ppermute(current, 'tm', [(i, i + 1) for i in range(tm_size - 1)])  4.39 us
    pallas_call x1, Pallas kernels, local(): pl.pallas_call(functools.partial(decode, n), out_shape=jax.ShapeDtypeStru...  3.89 us
    ppermute x4, waiting for transfers between devices, spread(): return lax.ppermute(x, ('seq', 'chan'), pairs)  3.13 us
    pallas_call x1, Pallas kernels, local(): pl.pallas_call(stage, out_shape=[jax.ShapeDtypeStruct((C_LAT, padded), BF...  2.32 us
    pallas_call x2, Pallas kernels, local(): pl.pallas_call(functools.partial(cut_windows, n), out_shape=[shape] * len...  0.82 us
    ppermute x3, starting transfers between devices, swapped(): return lax.ppermute(x, 'chan', [(0, 1), (1, 0)])  0.75 us
  transfers between devices with their start and end apart: 8, of which 3 were waited for; matrix products, arithmetic and copies ran while one was open for 0% of the time, Pallas kernels for 14%

profile of v4, /device:TPU:0, one launch (start us, length us, event | category | flops | bytes accessed | tf_op | source)
XLA Modules:
  0.0 22.7 jit_solution(3673565398608822493)
XLA Ops:
  0.0 0.5 %collective-permute-start.7 = (bf16[3,3,3,512,128]{4,3,2,1,0:T(8,128)(2,1)}, bf16[3,3,3,512,128]{4,3,2,1,0:T(8,128)(2,1)S(1)}, u32[]{:S(2)}, u32[]{:S(2)}) collective-permute-start(bf16[3,3,3,512,128]{4,3,2,1,0:T(8,128)(2,1)} %refs_4_.1), channel_id=1, source_target_pairs={{0,1},{1,0},{2,3},{3,2},{4,5},{5,4},{6,7},{7,6},{8,9},{9,8},{10,11... | collective-permute-start | bytes 10616840 | tf_op jit(solution)/shard_map/ppermute | solution.py:208
  0.5 4.4 %collective-permute-start = (bf16[16,7200]{1,0:T(8,128)(2,1)}, bf16[16,7200]{1,0:T(8,128)(2,1)S(1)}, u32[]{:S(2)}, u32[]{:S(2)}) collective-permute-start(bf16[16,7200]{1,0:T(8,128)(2,1)} %bitcast.5), channel_id=1, source_target_pairs={{0,2},{1,3},{4,6},{5,7},{8,10},{9,11},{12,14},{13,15},{16,18},{17,... | collective-permute-start | bytes 691208 | tf_op jit(solution)/shard_map/ppermute | solution.py:229
  4.9 0.3 %collective-permute-start.6 = (bf16[432,256]{1,0:T(8,128)(2,1)}, bf16[432,256]{1,0:T(8,128)(2,1)S(1)}, u32[]{:S(2)}, u32[]{:S(2)}) collective-permute-start(bf16[432,256]{1,0:T(8,128)(2,1)} %bitcast.7), channel_id=1, source_target_pairs={{0,1},{1,0},{2,3},{3,2},{4,5},{5,4},{6,7},{7,6},{8,9},{9,8},{10,11... | collective-permute-start | bytes 663560 | tf_op jit(solution)/shard_map/ppermute | solution.py:208
  5.1 1.6 %collective-permute-start.1 = (s32[3,1,4]{2,1,0:T(1,128)}, s32[3,1,4]{2,1,0:T(1,128)S(1)}, u32[]{:S(2)}, u32[]{:S(2)}) collective-permute-start(s32[3,1,4]{2,1,0:T(1,128)} %bitcast.10), channel_id=1, source_target_pairs={{0,4},{1,9},{4,0},{5,13},{8,12},{9,1},{12,8},{13,5},{2,6},{3,11},{... | collective-permute-start | bytes 152 | tf_op jit(solution)/shard_map/ppermute | solution.py:216
  6.7 2.5 %collective-permute-start.2 = (s32[3,1,4]{2,1,0:T(1,128)}, s32[3,1,4]{2,1,0:T(1,128)S(1)}, u32[]{:S(2)}, u32[]{:S(2)}) collective-permute-start(s32[3,1,4]{2,1,0:T(1,128)} %bitcast.11), channel_id=1, source_target_pairs={{0,12},{1,13},{4,8},{5,9},{8,4},{9,5},{12,0},{13,1},{2,14},{3,15},... | collective-permute-start | bytes 152 | tf_op jit(solution)/shard_map/ppermute | solution.py:216
  9.2 2.3 %stage.1 = (bf16[16,7424]{1,0:T(8,128)(2,1)S(1)}, s32[3,1,4]{2,1,0:T(1,128)S(1)}, bf16[432,256]{1,0:T(8,128)(2,1)S(1)}, bf16[12,128]{1,0:T(8,128)(2,1)S(1)}, bf16[3,3,3,512,128]{4,3,2,1,0:T(8,128)(2,1)S(1)}) custom-call(bf16[16,7200]{1,0:T(8,128)(2,1)} %bitcast.6, s32[3,1,4]{2,1,0:T(1,128)} %bitcast.12, bf16[432,256]{1,0:T(8,128)(2,1)} %bitcast.8, ...), custom_call_target="tpu_custom_call" | custom-call | flops 1 | bytes 1 | tf_op jit(solution)/shard_map/stage/pallas_call | solution.py:233
  11.5 0.0 collective-permute-done.1.refs_0_
  11.5 0.8 %collective-permute-done.2.refs_1_ = s32[3,1,4]{2,1,0:T(1,128)S(1)} collective-permute-done((s32[3,1,4]{2,1,0:T(1,128)}, s32[3,1,4]{2,1,0:T(1,128)S(1)}, u32[]{:S(2)}, u32[]{:S(2)}) %collective-permute-start.2) | collective-permute-done | bytes 80 | tf_op jit(solution)/shard_map/ppermute | solution.py:216
  12.3 0.0 collective-permute-done.refs_2_.refs_3_
  12.3 0.5 %cut_windows.1 = (bf16[9,16,128]{2,1,0:T(8,128)(2,1)S(1)}, bf16[9,16,128]{2,1,0:T(8,128)(2,1)S(1)}) custom-call(s32[3,1,4]{2,1,0:T(1,128)S(1)} %collective-permute-done.1.refs_0_, s32[3,1,4]{2,1,0:T(1,128)S(1)} %collective-permute-done.2.refs_1_, bf16[16,7424]{1,0:T(8,128)(2,1)S(1)} %get-tuple-element.13.refs_1_.refs_2_, ...), custom_call_target="tpu_custom_call" | custom-call | flops 1 | bytes 1 | tf_op jit(solution)/shard_map/cut_windows/pallas_call | solution.py:253
  12.8 0.1 collective-permute-start.3
  12.9 2.5 %collective-permute-start.5 = (bf16[9,16,128]{2,1,0:T(8,128)(2,1)S(1)}, bf16[9,16,128]{2,1,0:T(8,128)(2,1)S(1)}, u32[]{:S(2)}, u32[]{:S(2)}) collective-permute-start(bf16[9,16,128]{2,1,0:T(8,128)(2,1)S(1)} %get-tuple-element.16), channel_id=1, source_target_pairs={{0,12},{1,13},{4,8},{5,9},{8,4},{9,5},{12,0},{13,1},{2,14},{3,15},... | collective-permute-start | bytes 110600 | tf_op jit(solution)/shard_map/ppermute | solution.py:216
  15.5 1.8 %collective-permute-done.3.refs_3_ = bf16[9,16,128]{2,1,0:T(8,128)(2,1)S(1)} collective-permute-done((bf16[9,16,128]{2,1,0:T(8,128)(2,1)S(1)}, bf16[9,16,128]{2,1,0:T(8,128)(2,1)S(1)}, u32[]{:S(2)}, u32[]{:S(2)}) %collective-permute-start.3) | collective-permute-done | bytes 36896 | tf_op jit(solution)/shard_map/ppermute | solution.py:216
  17.3 0.0 collective-permute-start.4
  17.9 0.3 %cut_own.1.refs_2_ = bf16[8,16,128]{2,1,0:T(8,128)(2,1)S(1)} custom-call(s32[3,1,4]{2,1,0:T(1,128)S(1)} %get-tuple-element.12.refs_0_.refs_1_, bf16[16,7424]{1,0:T(8,128)(2,1)S(1)} %get-tuple-element.13.refs_1_.refs_2_, bf16[16,7200]{1,0:T(8,128)(2,1)S(1)} %collective-permute-done.refs_2_.refs_3_, bf16[12,128]{1,0:T(8,128)(2,1)S(1)} %get-tuple-element.14.refs_3_.refs_4_.refs_8_), custom_call_target="tpu_custom_call" | custom-call | flops 1 | bytes 1 | tf_op jit(solution)/shard_map/cut_own/pallas_call | solution.py:253
  18.2 0.0 collective-permute-done.6.refs_7_
  18.2 0.6 %collective-permute-done.5.refs_5_ = bf16[9,16,128]{2,1,0:T(8,128)(2,1)S(1)} collective-permute-done((bf16[9,16,128]{2,1,0:T(8,128)(2,1)S(1)}, bf16[9,16,128]{2,1,0:T(8,128)(2,1)S(1)}, u32[]{:S(2)}, u32[]{:S(2)}) %collective-permute-start.5) | collective-permute-done | bytes 36896 | tf_op jit(solution)/shard_map/ppermute | solution.py:216
  18.8 0.0 collective-permute-done.4.refs_4_
  18.8 0.0 collective-permute-done.7.refs_10_
  18.8 3.9 %decode.1 = bf16[1,3,1,4,128]{4,3,2,1,0:T(4,128)(2,1)} custom-call(s32[1,1]{1,0:T(1,128)S(6)} %copy.7.refs_0_, s32[3,1,4]{2,1,0:T(1,128)S(1)} %get-tuple-element.12.refs_0_.refs_1_, bf16[8,16,128]{2,1,0:T(8,128)(2,1)S(1)} %cut_own.1.refs_2_, bf16[9,16,128]{2,1,0:T(8,128)(2,1)S(1)} %collective-permute-done.3.refs_3_, ...), custom_call_target="tpu_custom_call" | custom-call | tf_op jit(solution)/shard_map/decode/pallas_call | solution.py:268
Async XLA Ops:
  0.0 18.8 %collective-permute-start.7 = (bf16[3,3,3,512,128]{4,3,2,1,0:T(8,128)(2,1)}, bf16[3,3,3,512,128]{4,3,2,1,0:T(8,128)(2,1)S(1)}, u32[]{:S(2)}, u32[]{:S(2)}) collective-permute-start(bf16[3,3,3,512,128]{4,3,2,1,0:T(8,128)(2,1)} %refs_4_.1), channel_id=1, source_target_pairs={{0,1},{1,0},{2,3},{3,2},{4,5},{5,4},{6,7},{7,6},{8,9},{9,8},{10,11... | collective-permute-start | bytes 10616840 | tf_op jit(solution)/shard_map/ppermute | solution.py:208
  0.5 11.9 %collective-permute-start = (bf16[16,7200]{1,0:T(8,128)(2,1)}, bf16[16,7200]{1,0:T(8,128)(2,1)S(1)}, u32[]{:S(2)}, u32[]{:S(2)}) collective-permute-start(bf16[16,7200]{1,0:T(8,128)(2,1)} %bitcast.5), channel_id=1, source_target_pairs={{0,2},{1,3},{4,6},{5,7},{8,10},{9,11},{12,14},{13,15},{16,18},{17,... | collective-permute-start | bytes 691208 | tf_op jit(solution)/shard_map/ppermute | solution.py:229
  4.9 13.4 %collective-permute-start.6 = (bf16[432,256]{1,0:T(8,128)(2,1)}, bf16[432,256]{1,0:T(8,128)(2,1)S(1)}, u32[]{:S(2)}, u32[]{:S(2)}) collective-permute-start(bf16[432,256]{1,0:T(8,128)(2,1)} %bitcast.7), channel_id=1, source_target_pairs={{0,1},{1,0},{2,3},{3,2},{4,5},{5,4},{6,7},{7,6},{8,9},{9,8},{10,11... | collective-permute-start | bytes 663560 | tf_op jit(solution)/shard_map/ppermute | solution.py:208
  5.1 6.4 %collective-permute-start.1 = (s32[3,1,4]{2,1,0:T(1,128)}, s32[3,1,4]{2,1,0:T(1,128)S(1)}, u32[]{:S(2)}, u32[]{:S(2)}) collective-permute-start(s32[3,1,4]{2,1,0:T(1,128)} %bitcast.10), channel_id=1, source_target_pairs={{0,4},{1,9},{4,0},{5,13},{8,12},{9,1},{12,8},{13,5},{2,6},{3,11},{... | collective-permute-start | bytes 152 | tf_op jit(solution)/shard_map/ppermute | solution.py:216
  6.7 5.6 %collective-permute-start.2 = (s32[3,1,4]{2,1,0:T(1,128)}, s32[3,1,4]{2,1,0:T(1,128)S(1)}, u32[]{:S(2)}, u32[]{:S(2)}) collective-permute-start(s32[3,1,4]{2,1,0:T(1,128)} %bitcast.11), channel_id=1, source_target_pairs={{0,12},{1,13},{4,8},{5,9},{8,4},{9,5},{12,0},{13,1},{2,14},{3,15},... | collective-permute-start | bytes 152 | tf_op jit(solution)/shard_map/ppermute | solution.py:216
  12.8 4.4 %collective-permute-start.3 = (bf16[9,16,128]{2,1,0:T(8,128)(2,1)S(1)}, bf16[9,16,128]{2,1,0:T(8,128)(2,1)S(1)}, u32[]{:S(2)}, u32[]{:S(2)}) collective-permute-start(bf16[9,16,128]{2,1,0:T(8,128)(2,1)S(1)} %get-tuple-element.15), channel_id=1, source_target_pairs={{0,4},{1,9},{4,0},{5,13},{8,12},{9,1},{12,8},{13,5},{2,6},{3,11},{... | collective-permute-start | bytes 110600 | tf_op jit(solution)/shard_map/ppermute | solution.py:216
  12.9 5.9 %collective-permute-start.5 = (bf16[9,16,128]{2,1,0:T(8,128)(2,1)S(1)}, bf16[9,16,128]{2,1,0:T(8,128)(2,1)S(1)}, u32[]{:S(2)}, u32[]{:S(2)}) collective-permute-start(bf16[9,16,128]{2,1,0:T(8,128)(2,1)S(1)} %get-tuple-element.16), channel_id=1, source_target_pairs={{0,12},{1,13},{4,8},{5,9},{8,4},{9,5},{12,0},{13,1},{2,14},{3,15},... | collective-permute-start | bytes 110600 | tf_op jit(solution)/shard_map/ppermute | solution.py:216
  17.3 1.5 %collective-permute-start.4 = (bf16[9,16,128]{2,1,0:T(8,128)(2,1)S(1)}, bf16[9,16,128]{2,1,0:T(8,128)(2,1)S(1)}, u32[]{:S(2)}, u32[]{:S(2)}) collective-permute-start(bf16[9,16,128]{2,1,0:T(8,128)(2,1)S(1)} %collective-permute-done.3.refs_3_), channel_id=1, source_target_pairs={{0,1},{1,0},{2,3},{3,2},{4,5},{5,4},{6,7},{7,6},{8,9},{9,8},{10,11... | collective-permute-start | bytes 110600 | tf_op jit(solution)/shard_map/ppermute | solution.py:208

commit v5 on v4

--- a/solution.py
+++ b/solution.py
@@ -64,7 +64,8 @@
     part_start = lax.rem(lax.axis_index("seq"), per_frame) * shard
     last_base = (shard - 1) // LANES * LANES
     lane = lane_ids(C_LAT)
-    prev[:, :shard] = prev_ref[...]
+    real = lax.axis_index("tm") > 0
+    prev[:, :shard] = jnp.where(real, prev_ref[...], jnp.zeros((), BF16))
     for k in range(count):
         anchor = anchors[k][...]
         for i in range(MAXT):
@@ -226,7 +227,7 @@
     routes = [(2 * k - 1, 2 * k) for k in range(1, n // 2)] + [(n - 1, n - 1)]
     anchors = [spread(anchor, *route) for route in routes]
     tm_size = lax.axis_size("tm")
-    previous = lax.ppermute(current, "tm", [(i, i + 1) for i in range(tm_size - 1)])
+    previous = lax.ppermute(current, "tm", [(i, (i + 1) % tm_size) for i in range(tm_size)])
     other_in, other_up = swapped(in_flat), swapped(conv_up)
     padded = (shard - 1) // LANES * LANES + 2 * LANES
     own = (current, anchor, in_flat, pix, conv_up)

time: 22.8 us -> 21.7 us (0.952)
  starting transfers between devices: 11.8 us -> 10.9 us
    ppermute x1, starting transfers between devices: 4.39 us -> 2.49 us  [local(): lax.ppermute(current, 'tm', [(i, (i + 1) % tm_size) for i in range(tm_siz...]
    ppermute x4, starting transfers between devices: 6.67 us -> 7.59 us  [spread(): return lax.ppermute(x, ('seq', 'chan'), pairs)]
  transfers between devices with their start and end apart: 8 -> 8, of which waited for: 3 -> 3; matrix products, arithmetic and copies ran while one was open for 0% -> 0% of each run, Pallas kernels for 14% -> 15%
where the time goes in v5:
time: 21.7 us; the launch traced here: 21.6 us
  starting transfers between devices  10.9 us (50%)
  Pallas kernels  7.04 us (32%)
  waiting for transfers between devices  2.99 us (14%)
  between operations  0.69 us (3%)
    ppermute x4, starting transfers between devices, spread(): return lax.ppermute(x, ('seq', 'chan'), pairs)  7.59 us
    pallas_call x1, Pallas kernels, local(): pl.pallas_call(functools.partial(decode, n), out_shape=jax.ShapeDtypeStru...  3.89 us
    ppermute x4, waiting for transfers between devices, spread(): return lax.ppermute(x, ('seq', 'chan'), pairs)  2.98 us
    ppermute x1, starting transfers between devices, local(): lax.ppermute(current, 'tm', [(i, (i + 1) % tm_size) for i in range(tm_siz...  2.49 us
    pallas_call x1, Pallas kernels, local(): pl.pallas_call(stage, out_shape=[jax.ShapeDtypeStruct((C_LAT, padded), BF...  2.32 us
    pallas_call x2, Pallas kernels, local(): pl.pallas_call(functools.partial(cut_windows, n), out_shape=[shape] * len...  0.83 us
    ppermute x3, starting transfers between devices, swapped(): return lax.ppermute(x, 'chan', [(0, 1), (1, 0)])  0.79 us
  transfers between devices with their start and end apart: 8, of which 3 were waited for; matrix products, arithmetic and copies ran while one was open for 0% of the time, Pallas kernels for 15%

profile of v5, /device:TPU:0, one launch (start us, length us, event | category | flops | bytes accessed | tf_op | source)
XLA Modules:
  0.0 21.6 jit_solution(1883159917521990653)
XLA Ops:
  0.0 0.5 %collective-permute-start.7 = (bf16[3,3,3,512,128]{4,3,2,1,0:T(8,128)(2,1)}, bf16[3,3,3,512,128]{4,3,2,1,0:T(8,128)(2,1)S(1)}, u32[]{:S(2)}, u32[]{:S(2)}) collective-permute-start(bf16[3,3,3,512,128]{4,3,2,1,0:T(8,128)(2,1)} %refs_4_.1), channel_id=1, source_target_pairs={{0,1},{1,0},{2,3},{3,2},{4,5},{5,4},{6,7},{7,6},{8,9},{9,8},{10,11... | collective-permute-start | bytes 10616840 | tf_op jit(solution)/shard_map/ppermute | solution.py:209
  0.5 2.5 %collective-permute-start = (bf16[16,7200]{1,0:T(8,128)(2,1)}, bf16[16,7200]{1,0:T(8,128)(2,1)S(1)}, u32[]{:S(2)}, u32[]{:S(2)}) collective-permute-start(bf16[16,7200]{1,0:T(8,128)(2,1)} %bitcast.5), channel_id=1, source_target_pairs={{0,2},{2,0},{1,3},{3,1},{4,6},{6,4},{5,7},{7,5},{8,10},{10,8},{9,1... | collective-permute-start | bytes 691208 | tf_op jit(solution)/shard_map/ppermute | solution.py:230
  2.9 0.2 %collective-permute-start.6 = (bf16[432,256]{1,0:T(8,128)(2,1)}, bf16[432,256]{1,0:T(8,128)(2,1)S(1)}, u32[]{:S(2)}, u32[]{:S(2)}) collective-permute-start(bf16[432,256]{1,0:T(8,128)(2,1)} %bitcast.7), channel_id=1, source_target_pairs={{0,1},{1,0},{2,3},{3,2},{4,5},{5,4},{6,7},{7,6},{8,9},{9,8},{10,11... | collective-permute-start | bytes 663560 | tf_op jit(solution)/shard_map/ppermute | solution.py:209
  3.2 1.6 %collective-permute-start.1 = (s32[3,1,4]{2,1,0:T(1,128)}, s32[3,1,4]{2,1,0:T(1,128)S(1)}, u32[]{:S(2)}, u32[]{:S(2)}) collective-permute-start(s32[3,1,4]{2,1,0:T(1,128)} %bitcast.10), channel_id=1, source_target_pairs={{0,4},{1,9},{4,0},{5,13},{8,12},{9,1},{12,8},{13,5},{2,6},{3,11},{... | collective-permute-start | bytes 152 | tf_op jit(solution)/shard_map/ppermute | solution.py:217
  4.7 2.5 %collective-permute-start.2 = (s32[3,1,4]{2,1,0:T(1,128)}, s32[3,1,4]{2,1,0:T(1,128)S(1)}, u32[]{:S(2)}, u32[]{:S(2)}) collective-permute-start(s32[3,1,4]{2,1,0:T(1,128)} %bitcast.11), channel_id=1, source_target_pairs={{0,12},{1,13},{4,8},{5,9},{8,4},{9,5},{12,0},{13,1},{2,14},{3,15},... | collective-permute-start | bytes 152 | tf_op jit(solution)/shard_map/ppermute | solution.py:217
  7.2 2.3 %stage.1 = (bf16[16,7424]{1,0:T(8,128)(2,1)S(1)}, s32[3,1,4]{2,1,0:T(1,128)S(1)}, bf16[432,256]{1,0:T(8,128)(2,1)S(1)}, bf16[12,128]{1,0:T(8,128)(2,1)S(1)}, bf16[3,3,3,512,128]{4,3,2,1,0:T(8,128)(2,1)S(1)}) custom-call(bf16[16,7200]{1,0:T(8,128)(2,1)} %bitcast.6, s32[3,1,4]{2,1,0:T(1,128)} %bitcast.12, bf16[432,256]{1,0:T(8,128)(2,1)} %bitcast.8, ...), custom_call_target="tpu_custom_call" | custom-call | flops 1 | bytes 1 | tf_op jit(solution)/shard_map/stage/pallas_call | solution.py:234
  9.6 0.0 collective-permute-done.1.refs_0_
  9.6 0.8 %collective-permute-done.2.refs_1_ = s32[3,1,4]{2,1,0:T(1,128)S(1)} collective-permute-done((s32[3,1,4]{2,1,0:T(1,128)}, s32[3,1,4]{2,1,0:T(1,128)S(1)}, u32[]{:S(2)}, u32[]{:S(2)}) %collective-permute-start.2) | collective-permute-done | bytes 80 | tf_op jit(solution)/shard_map/ppermute | solution.py:217
  10.3 0.0 collective-permute-done.refs_2_.refs_3_
  10.3 0.5 %cut_windows.1 = (bf16[9,16,128]{2,1,0:T(8,128)(2,1)S(1)}, bf16[9,16,128]{2,1,0:T(8,128)(2,1)S(1)}) custom-call(s32[3,1,4]{2,1,0:T(1,128)S(1)} %collective-permute-done.1.refs_0_, s32[3,1,4]{2,1,0:T(1,128)S(1)} %collective-permute-done.2.refs_1_, bf16[16,7424]{1,0:T(8,128)(2,1)S(1)} %get-tuple-element.13.refs_1_.refs_2_, ...), custom_call_target="tpu_custom_call" | custom-call | flops 1 | bytes 1 | tf_op jit(solution)/shard_map/cut_windows/pallas_call | solution.py:254
  10.9 1.1 %collective-permute-start.3 = (bf16[9,16,128]{2,1,0:T(8,128)(2,1)S(1)}, bf16[9,16,128]{2,1,0:T(8,128)(2,1)S(1)}, u32[]{:S(2)}, u32[]{:S(2)}) collective-permute-start(bf16[9,16,128]{2,1,0:T(8,128)(2,1)S(1)} %get-tuple-element.15), channel_id=1, source_target_pairs={{0,4},{1,9},{4,0},{5,13},{8,12},{9,1},{12,8},{13,5},{2,6},{3,11},{... | collective-permute-start | bytes 110600 | tf_op jit(solution)/shard_map/ppermute | solution.py:217
  11.9 2.5 %collective-permute-start.5 = (bf16[9,16,128]{2,1,0:T(8,128)(2,1)S(1)}, bf16[9,16,128]{2,1,0:T(8,128)(2,1)S(1)}, u32[]{:S(2)}, u32[]{:S(2)}) collective-permute-start(bf16[9,16,128]{2,1,0:T(8,128)(2,1)S(1)} %get-tuple-element.16), channel_id=1, source_target_pairs={{0,12},{1,13},{4,8},{5,9},{8,4},{9,5},{12,0},{13,1},{2,14},{3,15},... | collective-permute-start | bytes 110600 | tf_op jit(solution)/shard_map/ppermute | solution.py:217
  14.4 0.6 %collective-permute-done.3.refs_3_ = bf16[9,16,128]{2,1,0:T(8,128)(2,1)S(1)} collective-permute-done((bf16[9,16,128]{2,1,0:T(8,128)(2,1)S(1)}, bf16[9,16,128]{2,1,0:T(8,128)(2,1)S(1)}, u32[]{:S(2)}, u32[]{:S(2)}) %collective-permute-start.3) | collective-permute-done | bytes 36896 | tf_op jit(solution)/shard_map/ppermute | solution.py:217
  15.0 0.1 collective-permute-start.4
  15.8 0.3 %cut_own.1.refs_2_ = bf16[8,16,128]{2,1,0:T(8,128)(2,1)S(1)} custom-call(s32[3,1,4]{2,1,0:T(1,128)S(1)} %get-tuple-element.12.refs_0_.refs_1_, bf16[16,7424]{1,0:T(8,128)(2,1)S(1)} %get-tuple-element.13.refs_1_.refs_2_, bf16[16,7200]{1,0:T(8,128)(2,1)S(1)} %collective-permute-done.refs_2_.refs_3_, bf16[12,128]{1,0:T(8,128)(2,1)S(1)} %get-tuple-element.14.refs_3_.refs_4_.refs_8_), custom_call_target="tpu_custom_call" | custom-call | flops 1 | bytes 1 | tf_op jit(solution)/shard_map/cut_own/pallas_call | solution.py:254
  16.1 0.0 collective-permute-done.6.refs_7_
  16.1 1.6 %collective-permute-done.5.refs_5_ = bf16[9,16,128]{2,1,0:T(8,128)(2,1)S(1)} collective-permute-done((bf16[9,16,128]{2,1,0:T(8,128)(2,1)S(1)}, bf16[9,16,128]{2,1,0:T(8,128)(2,1)S(1)}, u32[]{:S(2)}, u32[]{:S(2)}) %collective-permute-start.5) | collective-permute-done | bytes 36896 | tf_op jit(solution)/shard_map/ppermute | solution.py:217
  17.7 0.0 collective-permute-done.4.refs_4_
  17.7 0.0 collective-permute-done.7.refs_10_
  17.7 3.9 %decode.1 = bf16[1,3,1,4,128]{4,3,2,1,0:T(4,128)(2,1)} custom-call(s32[1,1]{1,0:T(1,128)S(6)} %copy.7.refs_0_, s32[3,1,4]{2,1,0:T(1,128)S(1)} %get-tuple-element.12.refs_0_.refs_1_, bf16[8,16,128]{2,1,0:T(8,128)(2,1)S(1)} %cut_own.1.refs_2_, bf16[9,16,128]{2,1,0:T(8,128)(2,1)S(1)} %collective-permute-done.3.refs_3_, ...), custom_call_target="tpu_custom_call" | custom-call | tf_op jit(solution)/shard_map/decode/pallas_call | solution.py:269
Async XLA Ops:
  0.0 17.7 %collective-permute-start.7 = (bf16[3,3,3,512,128]{4,3,2,1,0:T(8,128)(2,1)}, bf16[3,3,3,512,128]{4,3,2,1,0:T(8,128)(2,1)S(1)}, u32[]{:S(2)}, u32[]{:S(2)}) collective-permute-start(bf16[3,3,3,512,128]{4,3,2,1,0:T(8,128)(2,1)} %refs_4_.1), channel_id=1, source_target_pairs={{0,1},{1,0},{2,3},{3,2},{4,5},{5,4},{6,7},{7,6},{8,9},{9,8},{10,11... | collective-permute-start | bytes 10616840 | tf_op jit(solution)/shard_map/ppermute | solution.py:209
  0.5 9.9 %collective-permute-start = (bf16[16,7200]{1,0:T(8,128)(2,1)}, bf16[16,7200]{1,0:T(8,128)(2,1)S(1)}, u32[]{:S(2)}, u32[]{:S(2)}) collective-permute-start(bf16[16,7200]{1,0:T(8,128)(2,1)} %bitcast.5), channel_id=1, source_target_pairs={{0,2},{2,0},{1,3},{3,1},{4,6},{6,4},{5,7},{7,5},{8,10},{10,8},{9,1... | collective-permute-start | bytes 691208 | tf_op jit(solution)/shard_map/ppermute | solution.py:230
  2.9 13.2 %collective-permute-start.6 = (bf16[432,256]{1,0:T(8,128)(2,1)}, bf16[432,256]{1,0:T(8,128)(2,1)S(1)}, u32[]{:S(2)}, u32[]{:S(2)}) collective-permute-start(bf16[432,256]{1,0:T(8,128)(2,1)} %bitcast.7), channel_id=1, source_target_pairs={{0,1},{1,0},{2,3},{3,2},{4,5},{5,4},{6,7},{7,6},{8,9},{9,8},{10,11... | collective-permute-start | bytes 663560 | tf_op jit(solution)/shard_map/ppermute | solution.py:209
  3.2 6.4 %collective-permute-start.1 = (s32[3,1,4]{2,1,0:T(1,128)}, s32[3,1,4]{2,1,0:T(1,128)S(1)}, u32[]{:S(2)}, u32[]{:S(2)}) collective-permute-start(s32[3,1,4]{2,1,0:T(1,128)} %bitcast.10), channel_id=1, source_target_pairs={{0,4},{1,9},{4,0},{5,13},{8,12},{9,1},{12,8},{13,5},{2,6},{3,11},{... | collective-permute-start | bytes 152 | tf_op jit(solution)/shard_map/ppermute | solution.py:217
  4.7 5.6 %collective-permute-start.2 = (s32[3,1,4]{2,1,0:T(1,128)}, s32[3,1,4]{2,1,0:T(1,128)S(1)}, u32[]{:S(2)}, u32[]{:S(2)}) collective-permute-start(s32[3,1,4]{2,1,0:T(1,128)} %bitcast.11), channel_id=1, source_target_pairs={{0,12},{1,13},{4,8},{5,9},{8,4},{9,5},{12,0},{13,1},{2,14},{3,15},... | collective-permute-start | bytes 152 | tf_op jit(solution)/shard_map/ppermute | solution.py:217
  10.9 4.2 %collective-permute-start.3 = (bf16[9,16,128]{2,1,0:T(8,128)(2,1)S(1)}, bf16[9,16,128]{2,1,0:T(8,128)(2,1)S(1)}, u32[]{:S(2)}, u32[]{:S(2)}) collective-permute-start(bf16[9,16,128]{2,1,0:T(8,128)(2,1)S(1)} %get-tuple-element.15), channel_id=1, source_target_pairs={{0,4},{1,9},{4,0},{5,13},{8,12},{9,1},{12,8},{13,5},{2,6},{3,11},{... | collective-permute-start | bytes 110600 | tf_op jit(solution)/shard_map/ppermute | solution.py:217
  11.9 5.8 %collective-permute-start.5 = (bf16[9,16,128]{2,1,0:T(8,128)(2,1)S(1)}, bf16[9,16,128]{2,1,0:T(8,128)(2,1)S(1)}, u32[]{:S(2)}, u32[]{:S(2)}) collective-permute-start(bf16[9,16,128]{2,1,0:T(8,128)(2,1)S(1)} %get-tuple-element.16), channel_id=1, source_target_pairs={{0,12},{1,13},{4,8},{5,9},{8,4},{9,5},{12,0},{13,1},{2,14},{3,15},... | collective-permute-start | bytes 110600 | tf_op jit(solution)/shard_map/ppermute | solution.py:217
  15.0 2.6 %collective-permute-start.4 = (bf16[9,16,128]{2,1,0:T(8,128)(2,1)S(1)}, bf16[9,16,128]{2,1,0:T(8,128)(2,1)S(1)}, u32[]{:S(2)}, u32[]{:S(2)}) collective-permute-start(bf16[9,16,128]{2,1,0:T(8,128)(2,1)S(1)} %collective-permute-done.3.refs_3_), channel_id=1, source_target_pairs={{0,1},{1,0},{2,3},{3,2},{4,5},{5,4},{6,7},{7,6},{8,9},{9,8},{10,11... | collective-permute-start | bytes 110600 | tf_op jit(solution)/shard_map/ppermute | solution.py:209

commit v6 on v5

--- a/solution.py
+++ b/solution.py
@@ -96,8 +96,7 @@
 
 def decode(n, *refs):
     count, anchor, parts = refs[0], refs[1][...], refs[2 : n + 2]
-    own_in, other_in, own_pix, own_up, other_up, out, held, *scratch = refs[n + 2 :]
-    hiddens, lineds = scratch[:TAPS], scratch[TAPS:]
+    own_in, other_in, own_pix, own_up, other_up, out, held, *lineds = refs[n + 2 :]
     per_frame = n // FG
     me = lax.axis_index("seq")
     core = lax.axis_index("chan")
@@ -108,11 +107,13 @@
     held[me ^ (n - 1)] = parts[n - 1][:ROOM]
     lane = lane_ids(C_LAT)
 
+    firsts = [anchor[0, 0, i] & (FG - 1) for i in range(MAXT)]
+
     def frame(j):
         pieces = []
         for i in range(MAXT):
-            at = jnp.clip(anchor[0, 0, i], 0, FG - 1) + j
-            late, rank = at // FG, lax.rem(at, FG) * per_frame
+            at = firsts[i] + j
+            late, rank = at >> 2, (at & (FG - 1)) * per_frame
             piece = held[rank, late * MAXT + i]
             for p in range(1, per_frame):
                 piece += held[rank + p, late * MAXT + i]
@@ -143,7 +144,7 @@
     quarter, half = C_MID // 4, C_MID // 2
     for t in range(TAPS):
         volume = jnp.concatenate([*cells[t : t + TAPS], tail], axis=1)
-        hidden, lined = hiddens[t], lineds[t]
+        lined = lineds[t]
         for first, weights in enumerate((own_in, other_in)):
             per_tap = len(taps) * C_LAT
             kernel = [weights[a * per_tap : a * per_tap + LANES] for a in range(TAPS)]
@@ -160,15 +161,11 @@
                     at = (r * MAXT + i) * WIDE
                     value = silu(pre[at : at + WIDE])
                     for q in range(2):
-                        hidden[r * MAXT + i, 2 * first + q] = jnp.where(
-                            (col >= 0) & (col < width), value[:, q * quarter : (q + 1) * quarter], 0.0
-                        )
-        for c in range(TAPS):
-            for ri in range((TH + 2) * MAXT):
-                for q in range(4):
-                    lined[c, ri * TW : (ri + 1) * TW, q * quarter : (q + 1) * quarter] = hidden[
-                        ri, q, c : c + TW
-                    ].astype(BF16)
+                        part = slice((2 * first + q) * quarter, (2 * first + q + 1) * quarter)
+                        kept = jnp.where((col >= 0) & (col < width), value[:, q * quarter : (q + 1) * quarter], 0.0)
+                        for c in range(TAPS):
+                            moved = pltpu.roll(kept, WIDE - c, 0) if c else kept
+                            lined[c, (r * MAXT + i) * TW : (r * MAXT + i + 1) * TW, part] = moved[:TW].astype(BF16)
     outs = own_up.shape[-1]
     span = MAXT * TW
     total = jnp.zeros((TH * span, 2 * outs), F32)
@@ -274,7 +271,6 @@
         scratch_shapes=[
             pltpu.VMEM((n,) + plain.shape, BF16),
         ]
-        + [pltpu.VMEM(((TH + 2) * MAXT, 4, WIDE, C_MID // 4), F32)] * TAPS
         + [pltpu.VMEM((TAPS, (TH + 2) * MAXT * TW, C_MID), BF16)] * TAPS,
         compiler_params=pltpu.CompilerParams(vmem_limit_bytes=32 << 20),
         name="decode",

time: 21.7 us -> 21.5 us (level)
  no operation moved by 1% of the time
where the time goes in v6:
time: 21.5 us; the launch traced here: 21.4 us
  starting transfers between devices  10.9 us (51%)
  Pallas kernels  6.84 us (32%)
  waiting for transfers between devices  2.99 us (14%)
  between operations  0.69 us (3%)
    ppermute x4, starting transfers between devices, spread(): return lax.ppermute(x, ('seq', 'chan'), pairs)  7.59 us
    pallas_call x1, Pallas kernels, local(): pl.pallas_call(functools.partial(decode, n), out_shape=jax.ShapeDtypeStru...  3.68 us
    ppermute x4, waiting for transfers between devices, spread(): return lax.ppermute(x, ('seq', 'chan'), pairs)  2.98 us
    ppermute x1, starting transfers between devices, local(): lax.ppermute(current, 'tm', [(i, (i + 1) % tm_size) for i in range(tm_siz...  2.49 us
    pallas_call x1, Pallas kernels, local(): pl.pallas_call(stage, out_shape=[jax.ShapeDtypeStruct((C_LAT, padded), BF...  2.32 us
    pallas_call x2, Pallas kernels, local(): pl.pallas_call(functools.partial(cut_windows, n), out_shape=[shape] * len...  0.83 us
    ppermute x3, starting transfers between devices, swapped(): return lax.ppermute(x, 'chan', [(0, 1), (1, 0)])  0.79 us
  transfers between devices with their start and end apart: 8, of which 3 were waited for; matrix products, arithmetic and copies ran while one was open for 0% of the time, Pallas kernels for 15%

profile of v6, /device:TPU:0, one launch (start us, length us, event | category | flops | bytes accessed | tf_op | source)
XLA Modules:
  0.0 21.4 jit_solution(15485671107287429948)
XLA Ops:
  0.0 0.5 %collective-permute-start.7 = (bf16[3,3,3,512,128]{4,3,2,1,0:T(8,128)(2,1)}, bf16[3,3,3,512,128]{4,3,2,1,0:T(8,128)(2,1)S(1)}, u32[]{:S(2)}, u32[]{:S(2)}) collective-permute-start(bf16[3,3,3,512,128]{4,3,2,1,0:T(8,128)(2,1)} %refs_4_.1), channel_id=1, source_target_pairs={{0,1},{1,0},{2,3},{3,2},{4,5},{5,4},{6,7},{7,6},{8,9},{9,8},{10,11... | collective-permute-start | bytes 10616840 | tf_op jit(solution)/shard_map/ppermute | solution.py:206
  0.5 2.5 %collective-permute-start = (bf16[16,7200]{1,0:T(8,128)(2,1)}, bf16[16,7200]{1,0:T(8,128)(2,1)S(1)}, u32[]{:S(2)}, u32[]{:S(2)}) collective-permute-start(bf16[16,7200]{1,0:T(8,128)(2,1)} %bitcast.5), channel_id=1, source_target_pairs={{0,2},{2,0},{1,3},{3,1},{4,6},{6,4},{5,7},{7,5},{8,10},{10,8},{9,1... | collective-permute-start | bytes 691208 | tf_op jit(solution)/shard_map/ppermute | solution.py:227
  2.9 0.2 %collective-permute-start.6 = (bf16[432,256]{1,0:T(8,128)(2,1)}, bf16[432,256]{1,0:T(8,128)(2,1)S(1)}, u32[]{:S(2)}, u32[]{:S(2)}) collective-permute-start(bf16[432,256]{1,0:T(8,128)(2,1)} %bitcast.7), channel_id=1, source_target_pairs={{0,1},{1,0},{2,3},{3,2},{4,5},{5,4},{6,7},{7,6},{8,9},{9,8},{10,11... | collective-permute-start | bytes 663560 | tf_op jit(solution)/shard_map/ppermute | solution.py:206
  3.2 1.6 %collective-permute-start.1 = (s32[3,1,4]{2,1,0:T(1,128)}, s32[3,1,4]{2,1,0:T(1,128)S(1)}, u32[]{:S(2)}, u32[]{:S(2)}) collective-permute-start(s32[3,1,4]{2,1,0:T(1,128)} %bitcast.10), channel_id=1, source_target_pairs={{0,4},{1,9},{4,0},{5,13},{8,12},{9,1},{12,8},{13,5},{2,6},{3,11},{... | collective-permute-start | bytes 152 | tf_op jit(solution)/shard_map/ppermute | solution.py:214
  4.7 2.5 %collective-permute-start.2 = (s32[3,1,4]{2,1,0:T(1,128)}, s32[3,1,4]{2,1,0:T(1,128)S(1)}, u32[]{:S(2)}, u32[]{:S(2)}) collective-permute-start(s32[3,1,4]{2,1,0:T(1,128)} %bitcast.11), channel_id=1, source_target_pairs={{0,12},{1,13},{4,8},{5,9},{8,4},{9,5},{12,0},{13,1},{2,14},{3,15},... | collective-permute-start | bytes 152 | tf_op jit(solution)/shard_map/ppermute | solution.py:214
  7.2 2.3 %stage.1 = (bf16[16,7424]{1,0:T(8,128)(2,1)S(1)}, s32[3,1,4]{2,1,0:T(1,128)S(1)}, bf16[432,256]{1,0:T(8,128)(2,1)S(1)}, bf16[12,128]{1,0:T(8,128)(2,1)S(1)}, bf16[3,3,3,512,128]{4,3,2,1,0:T(8,128)(2,1)S(1)}) custom-call(bf16[16,7200]{1,0:T(8,128)(2,1)} %bitcast.6, s32[3,1,4]{2,1,0:T(1,128)} %bitcast.12, bf16[432,256]{1,0:T(8,128)(2,1)} %bitcast.8, ...), custom_call_target="tpu_custom_call" | custom-call | flops 1 | bytes 1 | tf_op jit(solution)/shard_map/stage/pallas_call | solution.py:231
  9.6 0.0 collective-permute-done.1.refs_0_
  9.6 0.8 %collective-permute-done.2.refs_1_ = s32[3,1,4]{2,1,0:T(1,128)S(1)} collective-permute-done((s32[3,1,4]{2,1,0:T(1,128)}, s32[3,1,4]{2,1,0:T(1,128)S(1)}, u32[]{:S(2)}, u32[]{:S(2)}) %collective-permute-start.2) | collective-permute-done | bytes 80 | tf_op jit(solution)/shard_map/ppermute | solution.py:214
  10.3 0.0 collective-permute-done.refs_2_.refs_3_
  10.3 0.5 %cut_windows.1 = (bf16[9,16,128]{2,1,0:T(8,128)(2,1)S(1)}, bf16[9,16,128]{2,1,0:T(8,128)(2,1)S(1)}) custom-call(s32[3,1,4]{2,1,0:T(1,128)S(1)} %collective-permute-done.1.refs_0_, s32[3,1,4]{2,1,0:T(1,128)S(1)} %collective-permute-done.2.refs_1_, bf16[16,7424]{1,0:T(8,128)(2,1)S(1)} %get-tuple-element.13.refs_1_.refs_2_, ...), custom_call_target="tpu_custom_call" | custom-call | flops 1 | bytes 1 | tf_op jit(solution)/shard_map/cut_windows/pallas_call | solution.py:251
  10.9 1.1 %collective-permute-start.3 = (bf16[9,16,128]{2,1,0:T(8,128)(2,1)S(1)}, bf16[9,16,128]{2,1,0:T(8,128)(2,1)S(1)}, u32[]{:S(2)}, u32[]{:S(2)}) collective-permute-start(bf16[9,16,128]{2,1,0:T(8,128)(2,1)S(1)} %get-tuple-element.15), channel_id=1, source_target_pairs={{0,4},{1,9},{4,0},{5,13},{8,12},{9,1},{12,8},{13,5},{2,6},{3,11},{... | collective-permute-start | bytes 110600 | tf_op jit(solution)/shard_map/ppermute | solution.py:214
  11.9 2.5 %collective-permute-start.5 = (bf16[9,16,128]{2,1,0:T(8,128)(2,1)S(1)}, bf16[9,16,128]{2,1,0:T(8,128)(2,1)S(1)}, u32[]{:S(2)}, u32[]{:S(2)}) collective-permute-start(bf16[9,16,128]{2,1,0:T(8,128)(2,1)S(1)} %get-tuple-element.16), channel_id=1, source_target_pairs={{0,12},{1,13},{4,8},{5,9},{8,4},{9,5},{12,0},{13,1},{2,14},{3,15},... | collective-permute-start | bytes 110600 | tf_op jit(solution)/shard_map/ppermute | solution.py:214
  14.4 0.6 %collective-permute-done.3.refs_3_ = bf16[9,16,128]{2,1,0:T(8,128)(2,1)S(1)} collective-permute-done((bf16[9,16,128]{2,1,0:T(8,128)(2,1)S(1)}, bf16[9,16,128]{2,1,0:T(8,128)(2,1)S(1)}, u32[]{:S(2)}, u32[]{:S(2)}) %collective-permute-start.3) | collective-permute-done | bytes 36896 | tf_op jit(solution)/shard_map/ppermute | solution.py:214
  15.0 0.1 collective-permute-start.4
  15.8 0.3 %cut_own.1.refs_2_ = bf16[8,16,128]{2,1,0:T(8,128)(2,1)S(1)} custom-call(s32[3,1,4]{2,1,0:T(1,128)S(1)} %get-tuple-element.12.refs_0_.refs_1_, bf16[16,7424]{1,0:T(8,128)(2,1)S(1)} %get-tuple-element.13.refs_1_.refs_2_, bf16[16,7200]{1,0:T(8,128)(2,1)S(1)} %collective-permute-done.refs_2_.refs_3_, bf16[12,128]{1,0:T(8,128)(2,1)S(1)} %get-tuple-element.14.refs_3_.refs_4_.refs_8_), custom_call_target="tpu_custom_call" | custom-call | flops 1 | bytes 1 | tf_op jit(solution)/shard_map/cut_own/pallas_call | solution.py:251
  16.1 0.0 collective-permute-done.6.refs_7_
  16.1 1.6 %collective-permute-done.5.refs_5_ = bf16[9,16,128]{2,1,0:T(8,128)(2,1)S(1)} collective-permute-done((bf16[9,16,128]{2,1,0:T(8,128)(2,1)S(1)}, bf16[9,16,128]{2,1,0:T(8,128)(2,1)S(1)}, u32[]{:S(2)}, u32[]{:S(2)}) %collective-permute-start.5) | collective-permute-done | bytes 36896 | tf_op jit(solution)/shard_map/ppermute | solution.py:214
  17.7 0.0 collective-permute-done.4.refs_4_
  17.7 0.0 collective-permute-done.7.refs_10_
  17.7 3.7 %decode.1 = bf16[1,3,1,4,128]{4,3,2,1,0:T(4,128)(2,1)} custom-call(s32[1,1]{1,0:T(1,128)S(6)} %copy.7.refs_0_, s32[3,1,4]{2,1,0:T(1,128)S(1)} %get-tuple-element.12.refs_0_.refs_1_, bf16[8,16,128]{2,1,0:T(8,128)(2,1)S(1)} %cut_own.1.refs_2_, bf16[9,16,128]{2,1,0:T(8,128)(2,1)S(1)} %collective-permute-done.3.refs_3_, ...), custom_call_target="tpu_custom_call" | custom-call | tf_op jit(solution)/shard_map/decode/pallas_call | solution.py:266
Async XLA Ops:
  0.0 17.7 %collective-permute-start.7 = (bf16[3,3,3,512,128]{4,3,2,1,0:T(8,128)(2,1)}, bf16[3,3,3,512,128]{4,3,2,1,0:T(8,128)(2,1)S(1)}, u32[]{:S(2)}, u32[]{:S(2)}) collective-permute-start(bf16[3,3,3,512,128]{4,3,2,1,0:T(8,128)(2,1)} %refs_4_.1), channel_id=1, source_target_pairs={{0,1},{1,0},{2,3},{3,2},{4,5},{5,4},{6,7},{7,6},{8,9},{9,8},{10,11... | collective-permute-start | bytes 10616840 | tf_op jit(solution)/shard_map/ppermute | solution.py:206
  0.5 9.9 %collective-permute-start = (bf16[16,7200]{1,0:T(8,128)(2,1)}, bf16[16,7200]{1,0:T(8,128)(2,1)S(1)}, u32[]{:S(2)}, u32[]{:S(2)}) collective-permute-start(bf16[16,7200]{1,0:T(8,128)(2,1)} %bitcast.5), channel_id=1, source_target_pairs={{0,2},{2,0},{1,3},{3,1},{4,6},{6,4},{5,7},{7,5},{8,10},{10,8},{9,1... | collective-permute-start | bytes 691208 | tf_op jit(solution)/shard_map/ppermute | solution.py:227
  2.9 13.2 %collective-permute-start.6 = (bf16[432,256]{1,0:T(8,128)(2,1)}, bf16[432,256]{1,0:T(8,128)(2,1)S(1)}, u32[]{:S(2)}, u32[]{:S(2)}) collective-permute-start(bf16[432,256]{1,0:T(8,128)(2,1)} %bitcast.7), channel_id=1, source_target_pairs={{0,1},{1,0},{2,3},{3,2},{4,5},{5,4},{6,7},{7,6},{8,9},{9,8},{10,11... | collective-permute-start | bytes 663560 | tf_op jit(solution)/shard_map/ppermute | solution.py:206
  3.2 6.4 %collective-permute-start.1 = (s32[3,1,4]{2,1,0:T(1,128)}, s32[3,1,4]{2,1,0:T(1,128)S(1)}, u32[]{:S(2)}, u32[]{:S(2)}) collective-permute-start(s32[3,1,4]{2,1,0:T(1,128)} %bitcast.10), channel_id=1, source_target_pairs={{0,4},{1,9},{4,0},{5,13},{8,12},{9,1},{12,8},{13,5},{2,6},{3,11},{... | collective-permute-start | bytes 152 | tf_op jit(solution)/shard_map/ppermute | solution.py:214
  4.7 5.6 %collective-permute-start.2 = (s32[3,1,4]{2,1,0:T(1,128)}, s32[3,1,4]{2,1,0:T(1,128)S(1)}, u32[]{:S(2)}, u32[]{:S(2)}) collective-permute-start(s32[3,1,4]{2,1,0:T(1,128)} %bitcast.11), channel_id=1, source_target_pairs={{0,12},{1,13},{4,8},{5,9},{8,4},{9,5},{12,0},{13,1},{2,14},{3,15},... | collective-permute-start | bytes 152 | tf_op jit(solution)/shard_map/ppermute | solution.py:214
  10.9 4.2 %collective-permute-start.3 = (bf16[9,16,128]{2,1,0:T(8,128)(2,1)S(1)}, bf16[9,16,128]{2,1,0:T(8,128)(2,1)S(1)}, u32[]{:S(2)}, u32[]{:S(2)}) collective-permute-start(bf16[9,16,128]{2,1,0:T(8,128)(2,1)S(1)} %get-tuple-element.15), channel_id=1, source_target_pairs={{0,4},{1,9},{4,0},{5,13},{8,12},{9,1},{12,8},{13,5},{2,6},{3,11},{... | collective-permute-start | bytes 110600 | tf_op jit(solution)/shard_map/ppermute | solution.py:214
  11.9 5.8 %collective-permute-start.5 = (bf16[9,16,128]{2,1,0:T(8,128)(2,1)S(1)}, bf16[9,16,128]{2,1,0:T(8,128)(2,1)S(1)}, u32[]{:S(2)}, u32[]{:S(2)}) collective-permute-start(bf16[9,16,128]{2,1,0:T(8,128)(2,1)S(1)} %get-tuple-element.16), channel_id=1, source_target_pairs={{0,12},{1,13},{4,8},{5,9},{8,4},{9,5},{12,0},{13,1},{2,14},{3,15},... | collective-permute-start | bytes 110600 | tf_op jit(solution)/shard_map/ppermute | solution.py:214
  15.0 2.6 %collective-permute-start.4 = (bf16[9,16,128]{2,1,0:T(8,128)(2,1)S(1)}, bf16[9,16,128]{2,1,0:T(8,128)(2,1)S(1)}, u32[]{:S(2)}, u32[]{:S(2)}) collective-permute-start(bf16[9,16,128]{2,1,0:T(8,128)(2,1)S(1)} %collective-permute-done.3.refs_3_), channel_id=1, source_target_pairs={{0,1},{1,0},{2,3},{3,2},{4,5},{5,4},{6,7},{7,6},{8,9},{9,8},{10,11... | collective-permute-start | bytes 110600 | tf_op jit(solution)/shard_map/ppermute | solution.py:206

commit v7 on v6

--- a/solution.py
+++ b/solution.py
@@ -63,33 +63,34 @@
     per_frame = n // FG
     part_start = lax.rem(lax.axis_index("seq"), per_frame) * shard
     last_base = (shard - 1) // LANES * LANES
+    last_base = (shard - 1) // LANES * LANES
     lane = lane_ids(C_LAT)
+    spot_row, spot_col = lane // COLS, lane % COLS
+    spot = jnp.where(spot_row < ROWS, spot_row * W_LAT + spot_col, -H_LAT * W_LAT)
+    of_row = [spot_row == rho for rho in range(ROWS)]
     real = lax.axis_index("tm") > 0
     prev[:, :shard] = jnp.where(real, prev_ref[...], jnp.zeros((), BF16))
     for k in range(count):
         anchor = anchors[k][...]
         for i in range(MAXT):
-            row0 = anchor[1, 0, i] - 2
             col0 = anchor[2, 0, i] - 2
-            first = jnp.maximum(-col0, 0)
-            end = jnp.minimum(W_LAT - col0, COLS)
-            totals = [jnp.zeros((C_LAT, LANES), BF16)] * 2
+            origin = (anchor[1, 0, i] - 2) * W_LAT + col0 - part_start
+            token, col = spot + origin, spot_col + col0
+            keep = (token >= 0) & (token < shard) & (col >= 0) & (col < W_LAT)
+            totals = [None, None]
             for rho in range(ROWS):
-                start = (row0 + rho) * W_LAT + col0 - part_start
-                base = jnp.clip(start & -LANES, 0, last_base)
+                start = origin + rho * W_LAT
+                base = jnp.minimum(jnp.maximum(start & -LANES, 0), last_base)
                 base = pl.multiple_of(base, LANES)
                 off = start - base
                 from_low = lane >= off
-                least = COLS * rho + jnp.maximum(first, -start)
-                past = COLS * rho + jnp.minimum(end, shard - start)
-                keep = (lane >= least) & (lane < past)
                 for half, source in enumerate((prev, cur)):
                     low = source[:, pl.ds(base, LANES)]
                     high = source[:, pl.ds(base + LANES, LANES)]
                     moved = pltpu.roll(jnp.where(from_low, low, high), (COLS * rho - off) & (LANES - 1), 1)
-                    totals[half] = jnp.where(keep, moved, totals[half])
+                    totals[half] = moved if rho == 0 else jnp.where(of_row[rho], moved, totals[half])
             for half in range(2):
-                outs[k][half * MAXT + i] = totals[half]
+                outs[k][half * MAXT + i] = jnp.where(keep, totals[half], jnp.zeros((), BF16))
     for out in outs if outs[0].shape[0] > ROOM else ():
         out[ROOM] = jnp.concatenate([pix[...], jnp.zeros((C_LAT - pix.shape[0], LANES), BF16)], axis=0)
 
@@ -101,10 +102,11 @@
     me = lax.axis_index("seq")
     core = lax.axis_index("chan")
     held[me] = parts[0][...]
-    for k in range(1, n // 2):
-        held[me ^ (2 * k - 1 + core)] = parts[2 * k - 1][:ROOM]
-        held[me ^ (2 * k - core)] = parts[2 * k][:ROOM]
-    held[me ^ (n - 1)] = parts[n - 1][:ROOM]
+    routes = seq_routes(n)
+    for k, (first, second) in enumerate(routes[:-1]):
+        held[me ^ (first + core * (second - first))] = parts[2 * k + 1][:ROOM]
+        held[me ^ (second + core * (first - second))] = parts[2 * k + 2][:ROOM]
+    held[me ^ routes[-1][0]] = parts[n - 1][:ROOM]
     lane = lane_ids(C_LAT)
 
     firsts = [anchor[0, 0, i] & (FG - 1) for i in range(MAXT)]
@@ -202,6 +204,11 @@
     return pltpu.with_memory_space_constraint(x, pltpu.HBM)
 
 
+def seq_routes(n):
+    codes = [1, *range(3, n), 2]
+    return list(zip(codes[:-1:2], codes[1:-1:2])) + [(codes[-1], codes[-1])]
+
+
 def swapped(x):
     return lax.ppermute(x, "chan", [(0, 1), (1, 0)])
 
@@ -221,7 +228,7 @@
     anchor = slot_anchor.transpose(1, 0, 2)
     in_flat = conv_in.reshape(-1, conv_in.shape[-1])
     pix = to_pixels.T
-    routes = [(2 * k - 1, 2 * k) for k in range(1, n // 2)] + [(n - 1, n - 1)]
+    routes = seq_routes(n)
     anchors = [spread(anchor, *route) for route in routes]
     tm_size = lax.axis_size("tm")
     previous = lax.ppermute(current, "tm", [(i, (i + 1) % tm_size) for i in range(tm_size)])

time: 21.5 us -> 21.1 us (0.981)
  waiting for transfers between devices: 2.99 us -> 0.99 us
  starting transfers between devices: 10.9 us -> 12.6 us
    ppermute x4, waiting for transfers between devices: 2.98 us -> 0.98 us  [spread(): return lax.ppermute(x, ('seq', 'chan'), pairs)]
    ppermute x3, starting transfers between devices: 0.79 us -> 1.67 us  [swapped(): return lax.ppermute(x, 'chan', [(0, 1), (1, 0)])]
    ppermute x4, starting transfers between devices: 7.59 us -> 8.46 us  [spread(): return lax.ppermute(x, ('seq', 'chan'), pairs)]
  transfers between devices with their start and end apart: 8 -> 8, of which waited for: 3 -> 1; matrix products, arithmetic and copies ran while one was open for 0% -> 0% of each run, Pallas kernels for 15% -> 14%
where the time goes in v7:
time: 21.1 us; the launch traced here: 21 us
  starting transfers between devices  12.6 us (60%)
  Pallas kernels  6.66 us (32%)
  waiting for transfers between devices  0.99 us (5%)
  between operations  0.71 us (3%)
    ppermute x4, starting transfers between devices, spread(): return lax.ppermute(x, ('seq', 'chan'), pairs)  8.46 us
    pallas_call x1, Pallas kernels, local(): pl.pallas_call(functools.partial(decode, n), out_shape=jax.ShapeDtypeStru...  3.68 us
    ppermute x1, starting transfers between devices, local(): lax.ppermute(current, 'tm', [(i, (i + 1) % tm_size) for i in range(tm_siz...  2.49 us
    pallas_call x1, Pallas kernels, local(): pl.pallas_call(stage, out_shape=[jax.ShapeDtypeStruct((C_LAT, padded), BF...  2.32 us
    ppermute x3, starting transfers between devices, swapped(): return lax.ppermute(x, 'chan', [(0, 1), (1, 0)])  1.67 us
    ppermute x4, waiting for transfers between devices, spread(): return lax.ppermute(x, ('seq', 'chan'), pairs)  0.98 us
    pallas_call x2, Pallas kernels, local(): pl.pallas_call(functools.partial(cut_windows, n), out_shape=[shape] * len...  0.66 us
  transfers between devices with their start and end apart: 8, of which 1 were waited for; matrix products, arithmetic and copies ran while one was open for 0% of the time, Pallas kernels for 14%

profile of v7, /device:TPU:0, one launch (start us, length us, event | category | flops | bytes accessed | tf_op | source)
XLA Modules:
  0.0 21.0 jit_solution(1244411535050343533)
XLA Ops:
  0.0 0.5 %collective-permute-start.7 = (bf16[3,3,3,512,128]{4,3,2,1,0:T(8,128)(2,1)}, bf16[3,3,3,512,128]{4,3,2,1,0:T(8,128)(2,1)S(1)}, u32[]{:S(2)}, u32[]{:S(2)}) collective-permute-start(bf16[3,3,3,512,128]{4,3,2,1,0:T(8,128)(2,1)} %refs_4_.1), channel_id=1, source_target_pairs={{0,1},{1,0},{2,3},{3,2},{4,5},{5,4},{6,7},{7,6},{8,9},{9,8},{10,11... | collective-permute-start | bytes 10616840 | tf_op jit(solution)/shard_map/ppermute | solution.py:213
  0.5 2.5 %collective-permute-start = (bf16[16,7200]{1,0:T(8,128)(2,1)}, bf16[16,7200]{1,0:T(8,128)(2,1)S(1)}, u32[]{:S(2)}, u32[]{:S(2)}) collective-permute-start(bf16[16,7200]{1,0:T(8,128)(2,1)} %bitcast.5), channel_id=1, source_target_pairs={{0,2},{2,0},{1,3},{3,1},{4,6},{6,4},{5,7},{7,5},{8,10},{10,8},{9,1... | collective-permute-start | bytes 691208 | tf_op jit(solution)/shard_map/ppermute | solution.py:234
  2.9 0.2 %collective-permute-start.6 = (bf16[432,256]{1,0:T(8,128)(2,1)}, bf16[432,256]{1,0:T(8,128)(2,1)S(1)}, u32[]{:S(2)}, u32[]{:S(2)}) collective-permute-start(bf16[432,256]{1,0:T(8,128)(2,1)} %bitcast.7), channel_id=1, source_target_pairs={{0,1},{1,0},{2,3},{3,2},{4,5},{5,4},{6,7},{7,6},{8,9},{9,8},{10,11... | collective-permute-start | bytes 663560 | tf_op jit(solution)/shard_map/ppermute | solution.py:213
  3.2 1.6 %collective-permute-start.1 = (s32[3,1,4]{2,1,0:T(1,128)}, s32[3,1,4]{2,1,0:T(1,128)S(1)}, u32[]{:S(2)}, u32[]{:S(2)}) collective-permute-start(s32[3,1,4]{2,1,0:T(1,128)} %bitcast.10), channel_id=1, source_target_pairs={{0,4},{1,13},{4,0},{5,9},{8,12},{9,5},{12,8},{13,1},{2,6},{3,15},{... | collective-permute-start | bytes 152 | tf_op jit(solution)/shard_map/ppermute | solution.py:221
  4.7 2.6 %collective-permute-start.2 = (s32[3,1,4]{2,1,0:T(1,128)}, s32[3,1,4]{2,1,0:T(1,128)S(1)}, u32[]{:S(2)}, u32[]{:S(2)}) collective-permute-start(s32[3,1,4]{2,1,0:T(1,128)} %bitcast.11), channel_id=1, source_target_pairs={{0,8},{1,9},{4,12},{5,13},{8,0},{9,1},{12,4},{13,5},{2,10},{3,11},... | collective-permute-start | bytes 152 | tf_op jit(solution)/shard_map/ppermute | solution.py:221
  7.3 2.3 %stage.1 = (bf16[16,7424]{1,0:T(8,128)(2,1)S(1)}, s32[3,1,4]{2,1,0:T(1,128)S(1)}, bf16[432,256]{1,0:T(8,128)(2,1)S(1)}, bf16[12,128]{1,0:T(8,128)(2,1)S(1)}, bf16[3,3,3,512,128]{4,3,2,1,0:T(8,128)(2,1)S(1)}) custom-call(bf16[16,7200]{1,0:T(8,128)(2,1)} %bitcast.6, s32[3,1,4]{2,1,0:T(1,128)} %bitcast.12, bf16[432,256]{1,0:T(8,128)(2,1)} %bitcast.8, ...), custom_call_target="tpu_custom_call" | custom-call | flops 1 | bytes 1 | tf_op jit(solution)/shard_map/stage/pallas_call | solution.py:238
  9.7 0.0 collective-permute-done.1.refs_0_
  9.7 0.0 collective-permute-done.2.refs_1_
  9.7 0.0 collective-permute-done.refs_2_.refs_3_
  9.7 0.4 %cut_windows.1 = (bf16[9,16,128]{2,1,0:T(8,128)(2,1)S(1)}, bf16[9,16,128]{2,1,0:T(8,128)(2,1)S(1)}) custom-call(s32[3,1,4]{2,1,0:T(1,128)S(1)} %collective-permute-done.1.refs_0_, s32[3,1,4]{2,1,0:T(1,128)S(1)} %collective-permute-done.2.refs_1_, bf16[16,7424]{1,0:T(8,128)(2,1)S(1)} %get-tuple-element.13.refs_1_.refs_2_, ...), custom_call_target="tpu_custom_call" | custom-call | flops 1 | bytes 1 | tf_op jit(solution)/shard_map/cut_windows/pallas_call | solution.py:258
  10.1 1.7 %collective-permute-start.3 = (bf16[9,16,128]{2,1,0:T(8,128)(2,1)S(1)}, bf16[9,16,128]{2,1,0:T(8,128)(2,1)S(1)}, u32[]{:S(2)}, u32[]{:S(2)}) collective-permute-start(bf16[9,16,128]{2,1,0:T(8,128)(2,1)S(1)} %get-tuple-element.15), channel_id=1, source_target_pairs={{0,4},{1,13},{4,0},{5,9},{8,12},{9,5},{12,8},{13,1},{2,6},{3,15},{... | collective-permute-start | bytes 110600 | tf_op jit(solution)/shard_map/ppermute | solution.py:221
  11.8 2.6 %collective-permute-start.5 = (bf16[9,16,128]{2,1,0:T(8,128)(2,1)S(1)}, bf16[9,16,128]{2,1,0:T(8,128)(2,1)S(1)}, u32[]{:S(2)}, u32[]{:S(2)}) collective-permute-start(bf16[9,16,128]{2,1,0:T(8,128)(2,1)S(1)} %get-tuple-element.16), channel_id=1, source_target_pairs={{0,8},{1,9},{4,12},{5,13},{8,0},{9,1},{12,4},{13,5},{2,10},{3,11},... | collective-permute-start | bytes 110600 | tf_op jit(solution)/shard_map/ppermute | solution.py:221
  14.4 0.0 collective-permute-done.3.refs_3_
  14.4 1.0 %collective-permute-start.4 = (bf16[9,16,128]{2,1,0:T(8,128)(2,1)S(1)}, bf16[9,16,128]{2,1,0:T(8,128)(2,1)S(1)}, u32[]{:S(2)}, u32[]{:S(2)}) collective-permute-start(bf16[9,16,128]{2,1,0:T(8,128)(2,1)S(1)} %collective-permute-done.3.refs_3_), channel_id=1, source_target_pairs={{0,1},{1,0},{2,3},{3,2},{4,5},{5,4},{6,7},{7,6},{8,9},{9,8},{10,11... | collective-permute-start | bytes 110600 | tf_op jit(solution)/shard_map/ppermute | solution.py:213
  16.0 0.3 %cut_own.1.refs_2_ = bf16[8,16,128]{2,1,0:T(8,128)(2,1)S(1)} custom-call(s32[3,1,4]{2,1,0:T(1,128)S(1)} %get-tuple-element.12.refs_0_.refs_1_, bf16[16,7424]{1,0:T(8,128)(2,1)S(1)} %get-tuple-element.13.refs_1_.refs_2_, bf16[16,7200]{1,0:T(8,128)(2,1)S(1)} %collective-permute-done.refs_2_.refs_3_, bf16[12,128]{1,0:T(8,128)(2,1)S(1)} %get-tuple-element.14.refs_3_.refs_4_.refs_8_), custom_call_target="tpu_custom_call" | custom-call | flops 1 | bytes 1 | tf_op jit(solution)/shard_map/cut_own/pallas_call | solution.py:258
  16.3 0.0 collective-permute-done.6.refs_7_
  16.3 1.0 %collective-permute-done.5.refs_5_ = bf16[9,16,128]{2,1,0:T(8,128)(2,1)S(1)} collective-permute-done((bf16[9,16,128]{2,1,0:T(8,128)(2,1)S(1)}, bf16[9,16,128]{2,1,0:T(8,128)(2,1)S(1)}, u32[]{:S(2)}, u32[]{:S(2)}) %collective-permute-start.5) | collective-permute-done | bytes 36896 | tf_op jit(solution)/shard_map/ppermute | solution.py:221
  17.3 0.0 collective-permute-done.4.refs_4_
  17.3 0.0 collective-permute-done.7.refs_10_
  17.3 3.7 %decode.1 = bf16[1,3,1,4,128]{4,3,2,1,0:T(4,128)(2,1)} custom-call(s32[1,1]{1,0:T(1,128)S(6)} %copy.7.refs_0_, s32[3,1,4]{2,1,0:T(1,128)S(1)} %get-tuple-element.12.refs_0_.refs_1_, bf16[8,16,128]{2,1,0:T(8,128)(2,1)S(1)} %cut_own.1.refs_2_, bf16[9,16,128]{2,1,0:T(8,128)(2,1)S(1)} %collective-permute-done.3.refs_3_, ...), custom_call_target="tpu_custom_call" | custom-call | tf_op jit(solution)/shard_map/decode/pallas_call | solution.py:273
Async XLA Ops:
  0.0 17.3 %collective-permute-start.7 = (bf16[3,3,3,512,128]{4,3,2,1,0:T(8,128)(2,1)}, bf16[3,3,3,512,128]{4,3,2,1,0:T(8,128)(2,1)S(1)}, u32[]{:S(2)}, u32[]{:S(2)}) collective-permute-start(bf16[3,3,3,512,128]{4,3,2,1,0:T(8,128)(2,1)} %refs_4_.1), channel_id=1, source_target_pairs={{0,1},{1,0},{2,3},{3,2},{4,5},{5,4},{6,7},{7,6},{8,9},{9,8},{10,11... | collective-permute-start | bytes 10616840 | tf_op jit(solution)/shard_map/ppermute | solution.py:213
  0.5 9.2 %collective-permute-start = (bf16[16,7200]{1,0:T(8,128)(2,1)}, bf16[16,7200]{1,0:T(8,128)(2,1)S(1)}, u32[]{:S(2)}, u32[]{:S(2)}) collective-permute-start(bf16[16,7200]{1,0:T(8,128)(2,1)} %bitcast.5), channel_id=1, source_target_pairs={{0,2},{2,0},{1,3},{3,1},{4,6},{6,4},{5,7},{7,5},{8,10},{10,8},{9,1... | collective-permute-start | bytes 691208 | tf_op jit(solution)/shard_map/ppermute | solution.py:234
  2.9 13.4 %collective-permute-start.6 = (bf16[432,256]{1,0:T(8,128)(2,1)}, bf16[432,256]{1,0:T(8,128)(2,1)S(1)}, u32[]{:S(2)}, u32[]{:S(2)}) collective-permute-start(bf16[432,256]{1,0:T(8,128)(2,1)} %bitcast.7), channel_id=1, source_target_pairs={{0,1},{1,0},{2,3},{3,2},{4,5},{5,4},{6,7},{7,6},{8,9},{9,8},{10,11... | collective-permute-start | bytes 663560 | tf_op jit(solution)/shard_map/ppermute | solution.py:213
  3.2 6.5 %collective-permute-start.1 = (s32[3,1,4]{2,1,0:T(1,128)}, s32[3,1,4]{2,1,0:T(1,128)S(1)}, u32[]{:S(2)}, u32[]{:S(2)}) collective-permute-start(s32[3,1,4]{2,1,0:T(1,128)} %bitcast.10), channel_id=1, source_target_pairs={{0,4},{1,13},{4,0},{5,9},{8,12},{9,5},{12,8},{13,1},{2,6},{3,15},{... | collective-permute-start | bytes 152 | tf_op jit(solution)/shard_map/ppermute | solution.py:221
  4.7 4.9 %collective-permute-start.2 = (s32[3,1,4]{2,1,0:T(1,128)}, s32[3,1,4]{2,1,0:T(1,128)S(1)}, u32[]{:S(2)}, u32[]{:S(2)}) collective-permute-start(s32[3,1,4]{2,1,0:T(1,128)} %bitcast.11), channel_id=1, source_target_pairs={{0,8},{1,9},{4,12},{5,13},{8,0},{9,1},{12,4},{13,5},{2,10},{3,11},... | collective-permute-start | bytes 152 | tf_op jit(solution)/shard_map/ppermute | solution.py:221
  10.1 4.3 %collective-permute-start.3 = (bf16[9,16,128]{2,1,0:T(8,128)(2,1)S(1)}, bf16[9,16,128]{2,1,0:T(8,128)(2,1)S(1)}, u32[]{:S(2)}, u32[]{:S(2)}) collective-permute-start(bf16[9,16,128]{2,1,0:T(8,128)(2,1)S(1)} %get-tuple-element.15), channel_id=1, source_target_pairs={{0,4},{1,13},{4,0},{5,9},{8,12},{9,5},{12,8},{13,1},{2,6},{3,15},{... | collective-permute-start | bytes 110600 | tf_op jit(solution)/shard_map/ppermute | solution.py:221
  11.8 5.5 %collective-permute-start.5 = (bf16[9,16,128]{2,1,0:T(8,128)(2,1)S(1)}, bf16[9,16,128]{2,1,0:T(8,128)(2,1)S(1)}, u32[]{:S(2)}, u32[]{:S(2)}) collective-permute-start(bf16[9,16,128]{2,1,0:T(8,128)(2,1)S(1)} %get-tuple-element.16), channel_id=1, source_target_pairs={{0,8},{1,9},{4,12},{5,13},{8,0},{9,1},{12,4},{13,5},{2,10},{3,11},... | collective-permute-start | bytes 110600 | tf_op jit(solution)/shard_map/ppermute | solution.py:221
  14.4 2.9 %collective-permute-start.4 = (bf16[9,16,128]{2,1,0:T(8,128)(2,1)S(1)}, bf16[9,16,128]{2,1,0:T(8,128)(2,1)S(1)}, u32[]{:S(2)}, u32[]{:S(2)}) collective-permute-start(bf16[9,16,128]{2,1,0:T(8,128)(2,1)S(1)} %collective-permute-done.3.refs_3_), channel_id=1, source_target_pairs={{0,1},{1,0},{2,3},{3,2},{4,5},{5,4},{6,7},{7,6},{8,9},{9,8},{10,11... | collective-permute-start | bytes 110600 | tf_op jit(solution)/shard_map/ppermute | solution.py:213

commit v8 on v7

--- a/solution.py
+++ b/solution.py
@@ -57,8 +57,8 @@
 
 
 def cut_windows(n, *refs):
-    count = (len(refs) - 4) // 2
-    anchors, (cur, prev_ref, pix), outs, prev = refs[:count], refs[count : count + 3], refs[count + 3 : -1], refs[-1]
+    count = (len(refs) - 3) // 2
+    anchors, (cur, prev_ref), outs, prev = refs[:count], refs[count : count + 2], refs[count + 2 : -1], refs[-1]
     shard = prev_ref.shape[1]
     per_frame = n // FG
     part_start = lax.rem(lax.axis_index("seq"), per_frame) * shard
@@ -91,22 +91,20 @@
                     totals[half] = moved if rho == 0 else jnp.where(of_row[rho], moved, totals[half])
             for half in range(2):
                 outs[k][half * MAXT + i] = jnp.where(keep, totals[half], jnp.zeros((), BF16))
-    for out in outs if outs[0].shape[0] > ROOM else ():
-        out[ROOM] = jnp.concatenate([pix[...], jnp.zeros((C_LAT - pix.shape[0], LANES), BF16)], axis=0)
 
 
 def decode(n, *refs):
     count, anchor, parts = refs[0], refs[1][...], refs[2 : n + 2]
-    own_in, other_in, own_pix, own_up, other_up, out, held, *lineds = refs[n + 2 :]
+    own_in, other_in, own_pix, other_pix, own_up, other_up, out, held, *lineds = refs[n + 2 :]
     per_frame = n // FG
     me = lax.axis_index("seq")
     core = lax.axis_index("chan")
     held[me] = parts[0][...]
     routes = seq_routes(n)
     for k, (first, second) in enumerate(routes[:-1]):
-        held[me ^ (first + core * (second - first))] = parts[2 * k + 1][:ROOM]
-        held[me ^ (second + core * (first - second))] = parts[2 * k + 2][:ROOM]
-    held[me ^ routes[-1][0]] = parts[n - 1][:ROOM]
+        held[me ^ (first + core * (second - first))] = parts[2 * k + 1][...]
+        held[me ^ (second + core * (first - second))] = parts[2 * k + 2][...]
+    held[me ^ routes[-1][0]] = parts[n - 1][...]
     lane = lane_ids(C_LAT)
 
     firsts = [anchor[0, 0, i] & (FG - 1) for i in range(MAXT)]
@@ -183,7 +181,7 @@
     row = lax.broadcasted_iota(jnp.int32, (32, 12), 0)
     col = lax.broadcasted_iota(jnp.int32, (32, 12), 1)
     pick = ((row % 8) * 4 + row // 8 == col) & (row % 8 < 3)
-    pix = jnp.concatenate([own_pix[...], parts[2][ROOM, : own_pix.shape[0]]], axis=1)
+    pix = jnp.concatenate([own_pix[...], other_pix[...]], axis=1)
     pix = jnp.dot(pick.astype(BF16), pix, preferred_element_type=F32).astype(BF16)
     colors = lax.dot_general(pix, upper, (((1,), (1,)), ((), ())), preferred_element_type=F32)
     colors = colors.astype(BF16).astype(F32)
@@ -252,19 +250,18 @@
         name="stage",
     )(*map(in_hbm, own))
     plain = jax.ShapeDtypeStruct((ROOM, C_LAT, LANES), BF16)
-    extended = jax.ShapeDtypeStruct((ROOM + 1, C_LAT, LANES), BF16)
     cut = []
-    for targets, shape, name in (([anchor], plain, "cut_own"), (anchors, extended, "cut_windows")):
+    for targets, shape, name in (([anchor], plain, "cut_own"), (anchors, plain, "cut_windows")):
         cut += pl.pallas_call(
             functools.partial(cut_windows, n),
             out_shape=[shape] * len(targets),
-            in_specs=[VMEM] * (len(targets) + 3),
+            in_specs=[VMEM] * (len(targets) + 2),
             out_specs=[VMEM] * len(targets),
             scratch_shapes=[pltpu.VMEM((C_LAT, padded), BF16)],
             compiler_params=pltpu.CompilerParams(vmem_limit_bytes=4 << 20),
             cost_estimate=pl.CostEstimate(flops=1, bytes_accessed=1, transcendentals=0),
             name=name,
-        )(*targets, cur_pad, previous, own_pix)
+        )(*targets, cur_pad, previous)
     parts = [cut[0]]
     for message, route in zip(cut[1:], routes[:-1]):
         arrived = spread(message, *route)
@@ -273,7 +270,7 @@
     pixels = pl.pallas_call(
         functools.partial(decode, n),
         out_shape=jax.ShapeDtypeStruct((1, 3, 1, MAXT, LANES), BF16),
-        in_specs=[SMEM] + [VMEM] * (n + 6),
+        in_specs=[SMEM] + [VMEM] * (n + 7),
         out_specs=VMEM,
         scratch_shapes=[
             pltpu.VMEM((n,) + plain.shape, BF16),
@@ -281,7 +278,7 @@
         + [pltpu.VMEM((TAPS, (TH + 2) * MAXT * TW, C_MID), BF16)] * TAPS,
         compiler_params=pltpu.CompilerParams(vmem_limit_bytes=32 << 20),
         name="decode",
-    )(slot_count, anchor, *parts, own_in, other_in, own_pix, own_up, other_up)
+    )(slot_count, anchor, *parts, own_in, other_in, own_pix, swapped(pix), own_up, other_up)
     return pixels.transpose(0, 3, 1, 2, 4)
 
 

time: 21.1 us -> 21 us (level)
    ppermute x4, waiting for transfers between devices: 0.98 us -> 0.52 us  [spread(): return lax.ppermute(x, ('seq', 'chan'), pairs)]
    ppermute x3 -> x4, waiting for transfers between devices: 0.01 us -> 0.25 us  [swapped(): return lax.ppermute(x, 'chan', [(0, 1), (1, 0)])]
    ppermute x3 -> x4, starting transfers between devices: 1.67 us -> 1.63 us  [swapped(): return lax.ppermute(x, 'chan', [(0, 1), (1, 0)])]
  transfers between devices with their start and end apart: 8 -> 9, of which waited for: 1 -> 2; matrix products, arithmetic and copies ran while one was open for 0% -> 0% of each run, Pallas kernels for 14% -> 14%
where the time goes in v8:
time: 21 us; the launch traced here: 20.8 us
  starting transfers between devices  12.6 us (60%)
  Pallas kernels  6.7 us (32%)
  waiting for transfers between devices  0.78 us (4%)
  between operations  0.71 us (3%)
    ppermute x4, starting transfers between devices, spread(): return lax.ppermute(x, ('seq', 'chan'), pairs)  8.46 us
    pallas_call x1, Pallas kernels, local(): pl.pallas_call(functools.partial(decode, n), out_shape=jax.ShapeDtypeStru...  3.73 us
    ppermute x1, starting transfers between devices, local(): lax.ppermute(current, 'tm', [(i, (i + 1) % tm_size) for i in range(tm_siz...  2.55 us
    pallas_call x1, Pallas kernels, local(): pl.pallas_call(stage, out_shape=[jax.ShapeDtypeStruct((C_LAT, padded), BF...  2.32 us
    ppermute x4, starting transfers between devices, swapped(): return lax.ppermute(x, 'chan', [(0, 1), (1, 0)])  1.63 us
    pallas_call x2, Pallas kernels, local(): pl.pallas_call(functools.partial(cut_windows, n), out_shape=[shape] * len...  0.65 us
    ppermute x4, waiting for transfers between devices, spread(): return lax.ppermute(x, ('seq', 'chan'), pairs)  0.52 us
  transfers between devices with their start and end apart: 9, of which 2 were waited for; matrix products, arithmetic and copies ran while one was open for 0% of the time, Pallas kernels for 14%

profile of v8, /device:TPU:0, one launch (start us, length us, event | category | flops | bytes accessed | tf_op | source)
XLA Modules:
  0.0 20.8 jit_solution(14341419352327705260)
XLA Ops:
  0.0 0.0 copy-start
  0.0 0.5 %collective-permute-start.8 = (bf16[3,3,3,512,128]{4,3,2,1,0:T(8,128)(2,1)}, bf16[3,3,3,512,128]{4,3,2,1,0:T(8,128)(2,1)S(1)}, u32[]{:S(2)}, u32[]{:S(2)}) collective-permute-start(bf16[3,3,3,512,128]{4,3,2,1,0:T(8,128)(2,1)} %refs_4_.1), channel_id=1, source_target_pairs={{0,1},{1,0},{2,3},{3,2},{4,5},{5,4},{6,7},{7,6},{8,9},{9,8},{10,11... | collective-permute-start | bytes 10616840 | tf_op jit(solution)/shard_map/ppermute | solution.py:211
  0.5 2.5 %collective-permute-start = (bf16[16,7200]{1,0:T(8,128)(2,1)}, bf16[16,7200]{1,0:T(8,128)(2,1)S(1)}, u32[]{:S(2)}, u32[]{:S(2)}) collective-permute-start(bf16[16,7200]{1,0:T(8,128)(2,1)} %bitcast.5), channel_id=1, source_target_pairs={{0,2},{2,0},{1,3},{3,1},{4,6},{6,4},{5,7},{7,5},{8,10},{10,8},{9,1... | collective-permute-start | bytes 691208 | tf_op jit(solution)/shard_map/ppermute | solution.py:232
  3.0 0.2 collective-permute-start.6
  3.2 1.6 %collective-permute-start.1 = (s32[3,1,4]{2,1,0:T(1,128)}, s32[3,1,4]{2,1,0:T(1,128)S(1)}, u32[]{:S(2)}, u32[]{:S(2)}) collective-permute-start(s32[3,1,4]{2,1,0:T(1,128)} %bitcast.11), channel_id=1, source_target_pairs={{0,4},{1,13},{4,0},{5,9},{8,12},{9,5},{12,8},{13,1},{2,6},{3,15},{... | collective-permute-start | bytes 152 | tf_op jit(solution)/shard_map/ppermute | solution.py:219
  4.7 2.6 %collective-permute-start.2 = (s32[3,1,4]{2,1,0:T(1,128)}, s32[3,1,4]{2,1,0:T(1,128)S(1)}, u32[]{:S(2)}, u32[]{:S(2)}) collective-permute-start(s32[3,1,4]{2,1,0:T(1,128)} %bitcast.12), channel_id=1, source_target_pairs={{0,8},{1,9},{4,12},{5,13},{8,0},{9,1},{12,4},{13,5},{2,10},{3,11},... | collective-permute-start | bytes 152 | tf_op jit(solution)/shard_map/ppermute | solution.py:219
  7.3 2.3 %stage.1 = (bf16[16,7424]{1,0:T(8,128)(2,1)S(1)}, s32[3,1,4]{2,1,0:T(1,128)S(1)}, bf16[432,256]{1,0:T(8,128)(2,1)S(1)}, bf16[12,128]{1,0:T(8,128)(2,1)S(1)}, bf16[3,3,3,512,128]{4,3,2,1,0:T(8,128)(2,1)S(1)}) custom-call(bf16[16,7200]{1,0:T(8,128)(2,1)} %bitcast.6, s32[3,1,4]{2,1,0:T(1,128)} %bitcast.13, bf16[432,256]{1,0:T(8,128)(2,1)} %bitcast.8, ...), custom_call_target="tpu_custom_call" | custom-call | flops 1 | bytes 1 | tf_op jit(solution)/shard_map/stage/pallas_call | solution.py:236
  9.7 0.0 collective-permute-done.1.refs_0_
  9.7 0.0 collective-permute-done.2.refs_1_
  9.7 0.0 collective-permute-done.refs_2_.refs_3_
  9.7 0.4 %cut_windows.1 = (bf16[8,16,128]{2,1,0:T(8,128)(2,1)S(1)}, bf16[8,16,128]{2,1,0:T(8,128)(2,1)S(1)}) custom-call(s32[3,1,4]{2,1,0:T(1,128)S(1)} %collective-permute-done.1.refs_0_, s32[3,1,4]{2,1,0:T(1,128)S(1)} %collective-permute-done.2.refs_1_, bf16[16,7424]{1,0:T(8,128)(2,1)S(1)} %get-tuple-element.13.refs_1_.refs_2_, ...), custom_call_target="tpu_custom_call" | custom-call | flops 1 | bytes 1 | tf_op jit(solution)/shard_map/cut_windows/pallas_call | solution.py:255
  10.1 1.7 %collective-permute-start.3 = (bf16[8,16,128]{2,1,0:T(8,128)(2,1)S(1)}, bf16[8,16,128]{2,1,0:T(8,128)(2,1)S(1)}, u32[]{:S(2)}, u32[]{:S(2)}) collective-permute-start(bf16[8,16,128]{2,1,0:T(8,128)(2,1)S(1)} %get-tuple-element.14), channel_id=1, source_target_pairs={{0,4},{1,13},{4,0},{5,9},{8,12},{9,5},{12,8},{13,1},{2,6},{3,15},{... | collective-permute-start | bytes 98312 | tf_op jit(solution)/shard_map/ppermute | solution.py:219
  11.8 2.6 %collective-permute-start.5 = (bf16[8,16,128]{2,1,0:T(8,128)(2,1)S(1)}, bf16[8,16,128]{2,1,0:T(8,128)(2,1)S(1)}, u32[]{:S(2)}, u32[]{:S(2)}) collective-permute-start(bf16[8,16,128]{2,1,0:T(8,128)(2,1)S(1)} %get-tuple-element.15), channel_id=1, source_target_pairs={{0,8},{1,9},{4,12},{5,13},{8,0},{9,1},{12,4},{13,5},{2,10},{3,11},... | collective-permute-start | bytes 98312 | tf_op jit(solution)/shard_map/ppermute | solution.py:219
  14.4 0.0 collective-permute-done.3.refs_3_
  14.4 1.0 %collective-permute-start.4 = (bf16[8,16,128]{2,1,0:T(8,128)(2,1)S(1)}, bf16[8,16,128]{2,1,0:T(8,128)(2,1)S(1)}, u32[]{:S(2)}, u32[]{:S(2)}) collective-permute-start(bf16[8,16,128]{2,1,0:T(8,128)(2,1)S(1)} %collective-permute-done.3.refs_3_), channel_id=1, source_target_pairs={{0,1},{1,0},{2,3},{3,2},{4,5},{5,4},{6,7},{7,6},{8,9},{9,8},{10,11... | collective-permute-start | bytes 98312 | tf_op jit(solution)/shard_map/ppermute | solution.py:211
  15.4 0.0 copy-done
  15.4 0.0 collective-permute-start.7
  16.1 0.3 %cut_own.1.refs_2_ = bf16[8,16,128]{2,1,0:T(8,128)(2,1)S(1)} custom-call(s32[3,1,4]{2,1,0:T(1,128)S(1)} %get-tuple-element.12.refs_0_.refs_1_, bf16[16,7424]{1,0:T(8,128)(2,1)S(1)} %get-tuple-element.13.refs_1_.refs_2_, bf16[16,7200]{1,0:T(8,128)(2,1)S(1)} %collective-permute-done.refs_2_.refs_3_), custom_call_target="tpu_custom_call" | custom-call | flops 1 | bytes 1 | tf_op jit(solution)/shard_map/cut_own/pallas_call | solution.py:255
  16.3 0.2 %collective-permute-done.7.refs_9_ = bf16[12,128]{1,0:T(8,128)(2,1)S(1)} collective-permute-done((bf16[12,128]{1,0:T(8,128)(2,1)S(1)}, bf16[12,128]{1,0:T(8,128)(2,1)S(1)}, u32[]{:S(2)}, u32[]{:S(2)}) %collective-permute-start.7) | collective-permute-done | bytes 3104 | tf_op jit(solution)/shard_map/ppermute | solution.py:211
  16.6 0.0 collective-permute-done.6.refs_7_
  16.6 0.5 %collective-permute-done.5.refs_5_ = bf16[8,16,128]{2,1,0:T(8,128)(2,1)S(1)} collective-permute-done((bf16[8,16,128]{2,1,0:T(8,128)(2,1)S(1)}, bf16[8,16,128]{2,1,0:T(8,128)(2,1)S(1)}, u32[]{:S(2)}, u32[]{:S(2)}) %collective-permute-start.5) | collective-permute-done | bytes 32800 | tf_op jit(solution)/shard_map/ppermute | solution.py:219
  17.1 0.0 collective-permute-done.4.refs_4_
  17.1 0.0 collective-permute-done.8.refs_11_
  17.1 3.7 %decode.1 = bf16[1,3,1,4,128]{4,3,2,1,0:T(4,128)(2,1)} custom-call(s32[1,1]{1,0:T(1,128)S(6)} %copy.7.refs_0_, s32[3,1,4]{2,1,0:T(1,128)S(1)} %get-tuple-element.12.refs_0_.refs_1_, bf16[8,16,128]{2,1,0:T(8,128)(2,1)S(1)} %cut_own.1.refs_2_, bf16[8,16,128]{2,1,0:T(8,128)(2,1)S(1)} %collective-permute-done.3.refs_3_, ...), custom_call_target="tpu_custom_call" | custom-call | tf_op jit(solution)/shard_map/decode/pallas_call | solution.py:270
Async XLA Ops:
  0.0 15.4 %copy-start = (bf16[128,12]{0,1:T(8,128)(2,1)S(1)}, bf16[128,12]{0,1:T(8,128)(2,1)}, u32[]{:S(2)}) copy-start(bf16[128,12]{0,1:T(8,128)(2,1)} %param.9) | copy-start | bytes 9220
  0.0 17.1 %collective-permute-start.8 = (bf16[3,3,3,512,128]{4,3,2,1,0:T(8,128)(2,1)}, bf16[3,3,3,512,128]{4,3,2,1,0:T(8,128)(2,1)S(1)}, u32[]{:S(2)}, u32[]{:S(2)}) collective-permute-start(bf16[3,3,3,512,128]{4,3,2,1,0:T(8,128)(2,1)} %refs_4_.1), channel_id=1, source_target_pairs={{0,1},{1,0},{2,3},{3,2},{4,5},{5,4},{6,7},{7,6},{8,9},{9,8},{10,11... | collective-permute-start | bytes 10616840 | tf_op jit(solution)/shard_map/ppermute | solution.py:211
  0.5 9.2 %collective-permute-start = (bf16[16,7200]{1,0:T(8,128)(2,1)}, bf16[16,7200]{1,0:T(8,128)(2,1)S(1)}, u32[]{:S(2)}, u32[]{:S(2)}) collective-permute-start(bf16[16,7200]{1,0:T(8,128)(2,1)} %bitcast.5), channel_id=1, source_target_pairs={{0,2},{2,0},{1,3},{3,1},{4,6},{6,4},{5,7},{7,5},{8,10},{10,8},{9,1... | collective-permute-start | bytes 691208 | tf_op jit(solution)/shard_map/ppermute | solution.py:232
  3.0 13.6 %collective-permute-start.6 = (bf16[432,256]{1,0:T(8,128)(2,1)}, bf16[432,256]{1,0:T(8,128)(2,1)S(1)}, u32[]{:S(2)}, u32[]{:S(2)}) collective-permute-start(bf16[432,256]{1,0:T(8,128)(2,1)} %bitcast.7), channel_id=1, source_target_pairs={{0,1},{1,0},{2,3},{3,2},{4,5},{5,4},{6,7},{7,6},{8,9},{9,8},{10,11... | collective-permute-start | bytes 663560 | tf_op jit(solution)/shard_map/ppermute | solution.py:211
  3.2 6.5 %collective-permute-start.1 = (s32[3,1,4]{2,1,0:T(1,128)}, s32[3,1,4]{2,1,0:T(1,128)S(1)}, u32[]{:S(2)}, u32[]{:S(2)}) collective-permute-start(s32[3,1,4]{2,1,0:T(1,128)} %bitcast.11), channel_id=1, source_target_pairs={{0,4},{1,13},{4,0},{5,9},{8,12},{9,5},{12,8},{13,1},{2,6},{3,15},{... | collective-permute-start | bytes 152 | tf_op jit(solution)/shard_map/ppermute | solution.py:219
  4.7 4.9 %collective-permute-start.2 = (s32[3,1,4]{2,1,0:T(1,128)}, s32[3,1,4]{2,1,0:T(1,128)S(1)}, u32[]{:S(2)}, u32[]{:S(2)}) collective-permute-start(s32[3,1,4]{2,1,0:T(1,128)} %bitcast.12), channel_id=1, source_target_pairs={{0,8},{1,9},{4,12},{5,13},{8,0},{9,1},{12,4},{13,5},{2,10},{3,11},... | collective-permute-start | bytes 152 | tf_op jit(solution)/shard_map/ppermute | solution.py:219
  10.1 4.3 %collective-permute-start.3 = (bf16[8,16,128]{2,1,0:T(8,128)(2,1)S(1)}, bf16[8,16,128]{2,1,0:T(8,128)(2,1)S(1)}, u32[]{:S(2)}, u32[]{:S(2)}) collective-permute-start(bf16[8,16,128]{2,1,0:T(8,128)(2,1)S(1)} %get-tuple-element.14), channel_id=1, source_target_pairs={{0,4},{1,13},{4,0},{5,9},{8,12},{9,5},{12,8},{13,1},{2,6},{3,15},{... | collective-permute-start | bytes 98312 | tf_op jit(solution)/shard_map/ppermute | solution.py:219
  11.8 5.3 %collective-permute-start.5 = (bf16[8,16,128]{2,1,0:T(8,128)(2,1)S(1)}, bf16[8,16,128]{2,1,0:T(8,128)(2,1)S(1)}, u32[]{:S(2)}, u32[]{:S(2)}) collective-permute-start(bf16[8,16,128]{2,1,0:T(8,128)(2,1)S(1)} %get-tuple-element.15), channel_id=1, source_target_pairs={{0,8},{1,9},{4,12},{5,13},{8,0},{9,1},{12,4},{13,5},{2,10},{3,11},... | collective-permute-start | bytes 98312 | tf_op jit(solution)/shard_map/ppermute | solution.py:219
  14.4 2.7 %collective-permute-start.4 = (bf16[8,16,128]{2,1,0:T(8,128)(2,1)S(1)}, bf16[8,16,128]{2,1,0:T(8,128)(2,1)S(1)}, u32[]{:S(2)}, u32[]{:S(2)}) collective-permute-start(bf16[8,16,128]{2,1,0:T(8,128)(2,1)S(1)} %collective-permute-done.3.refs_3_), channel_id=1, source_target_pairs={{0,1},{1,0},{2,3},{3,2},{4,5},{5,4},{6,7},{7,6},{8,9},{9,8},{10,11... | collective-permute-start | bytes 98312 | tf_op jit(solution)/shard_map/ppermute | solution.py:211
  15.4 1.2 %collective-permute-start.7 = (bf16[12,128]{1,0:T(8,128)(2,1)S(1)}, bf16[12,128]{1,0:T(8,128)(2,1)S(1)}, u32[]{:S(2)}, u32[]{:S(2)}) collective-permute-start(bf16[12,128]{1,0:T(8,128)(2,1)S(1)} %bitcast.10), channel_id=1, source_target_pairs={{0,1},{1,0},{2,3},{3,2},{4,5},{5,4},{6,7},{7,6},{8,9},{9,8},{10,11... | collective-permute-start | bytes 9224 | tf_op jit(solution)/shard_map/ppermute | solution.py:211

commit v9 on v8

--- a/solution.py
+++ b/solution.py
@@ -58,18 +58,19 @@
 
 def cut_windows(n, *refs):
     count = (len(refs) - 3) // 2
-    anchors, (cur, prev_ref), outs, prev = refs[:count], refs[count : count + 2], refs[count + 2 : -1], refs[-1]
+    anchors, (cur, prev_ref), outs, room = refs[:count], refs[count : count + 2], refs[count + 2 : -1], refs[-1]
     shard = prev_ref.shape[1]
     per_frame = n // FG
     part_start = lax.rem(lax.axis_index("seq"), per_frame) * shard
     last_base = (shard - 1) // LANES * LANES
     last_base = (shard - 1) // LANES * LANES
-    lane = lane_ids(C_LAT)
+    lane = lane_ids(2 * C_LAT)
     spot_row, spot_col = lane // COLS, lane % COLS
     spot = jnp.where(spot_row < ROWS, spot_row * W_LAT + spot_col, -H_LAT * W_LAT)
     of_row = [spot_row == rho for rho in range(ROWS)]
     real = lax.axis_index("tm") > 0
-    prev[:, :shard] = jnp.where(real, prev_ref[...], jnp.zeros((), BF16))
+    room[:C_LAT, :shard] = jnp.where(real, prev_ref[...], jnp.zeros((), BF16))
+    room[C_LAT:, :shard] = cur[:, :shard]
     for k in range(count):
         anchor = anchors[k][...]
         for i in range(MAXT):
@@ -77,20 +78,19 @@
             origin = (anchor[1, 0, i] - 2) * W_LAT + col0 - part_start
             token, col = spot + origin, spot_col + col0
             keep = (token >= 0) & (token < shard) & (col >= 0) & (col < W_LAT)
-            totals = [None, None]
+            total = None
             for rho in range(ROWS):
                 start = origin + rho * W_LAT
                 base = jnp.minimum(jnp.maximum(start & -LANES, 0), last_base)
                 base = pl.multiple_of(base, LANES)
                 off = start - base
-                from_low = lane >= off
-                for half, source in enumerate((prev, cur)):
-                    low = source[:, pl.ds(base, LANES)]
-                    high = source[:, pl.ds(base + LANES, LANES)]
-                    moved = pltpu.roll(jnp.where(from_low, low, high), (COLS * rho - off) & (LANES - 1), 1)
-                    totals[half] = moved if rho == 0 else jnp.where(of_row[rho], moved, totals[half])
+                both = room[:, pl.ds(base, 2 * LANES)]
+                both = jnp.where(lane >= off, both[:, :LANES], both[:, LANES:])
+                moved = pltpu.roll(both, (COLS * rho - off) & (LANES - 1), 1)
+                total = moved if rho == 0 else jnp.where(of_row[rho], moved, total)
+            total = jnp.where(keep, total, jnp.zeros((), BF16))
             for half in range(2):
-                outs[k][half * MAXT + i] = jnp.where(keep, totals[half], jnp.zeros((), BF16))
+                outs[k][half * MAXT + i] = total[half * C_LAT : (half + 1) * C_LAT]
 
 
 def decode(n, *refs):
@@ -257,7 +257,7 @@
             out_shape=[shape] * len(targets),
             in_specs=[VMEM] * (len(targets) + 2),
             out_specs=[VMEM] * len(targets),
-            scratch_shapes=[pltpu.VMEM((C_LAT, padded), BF16)],
+            scratch_shapes=[pltpu.VMEM((2 * C_LAT, padded), BF16)],
             compiler_params=pltpu.CompilerParams(vmem_limit_bytes=4 << 20),
             cost_estimate=pl.CostEstimate(flops=1, bytes_accessed=1, transcendentals=0),
             name=name,

time: 21 us -> 20.9 us (level)
  no operation moved by 1% of the time
where the time goes in v9:
time: 20.9 us; the launch traced here: 20.8 us
  starting transfers between devices  12.6 us (60%)
  Pallas kernels  6.61 us (32%)
  waiting for transfers between devices  0.8 us (4%)
  between operations  0.71 us (3%)
    ppermute x4, starting transfers between devices, spread(): return lax.ppermute(x, ('seq', 'chan'), pairs)  8.46 us
    pallas_call x1, Pallas kernels, local(): pl.pallas_call(functools.partial(decode, n), out_shape=jax.ShapeDtypeStru...  3.73 us
    ppermute x1, starting transfers between devices, local(): lax.ppermute(current, 'tm', [(i, (i + 1) % tm_size) for i in range(tm_siz...  2.55 us
    pallas_call x1, Pallas kernels, local(): pl.pallas_call(stage, out_shape=[jax.ShapeDtypeStruct((C_LAT, padded), BF...  2.32 us
    ppermute x4, starting transfers between devices, swapped(): return lax.ppermute(x, 'chan', [(0, 1), (1, 0)])  1.63 us
    pallas_call x2, Pallas kernels, local(): pl.pallas_call(functools.partial(cut_windows, n), out_shape=[shape] * len...  0.57 us
    ppermute x4, waiting for transfers between devices, spread(): return lax.ppermute(x, ('seq', 'chan'), pairs)  0.52 us
  transfers between devices with their start and end apart: 9, of which 2 were waited for; matrix products, arithmetic and copies ran while one was open for 0% of the time, Pallas kernels for 14%

profile of v9, /device:TPU:0, one launch (start us, length us, event | category | flops | bytes accessed | tf_op | source)
XLA Modules:
  0.0 20.8 jit_solution(16975122593021282784)
XLA Ops:
  0.0 0.0 copy-start
  0.0 0.5 %collective-permute-start.8 = (bf16[3,3,3,512,128]{4,3,2,1,0:T(8,128)(2,1)}, bf16[3,3,3,512,128]{4,3,2,1,0:T(8,128)(2,1)S(1)}, u32[]{:S(2)}, u32[]{:S(2)}) collective-permute-start(bf16[3,3,3,512,128]{4,3,2,1,0:T(8,128)(2,1)} %refs_4_.1), channel_id=1, source_target_pairs={{0,1},{1,0},{2,3},{3,2},{4,5},{5,4},{6,7},{7,6},{8,9},{9,8},{10,11... | collective-permute-start | bytes 10616840 | tf_op jit(solution)/shard_map/ppermute | solution.py:211
  0.5 2.5 %collective-permute-start = (bf16[16,7200]{1,0:T(8,128)(2,1)}, bf16[16,7200]{1,0:T(8,128)(2,1)S(1)}, u32[]{:S(2)}, u32[]{:S(2)}) collective-permute-start(bf16[16,7200]{1,0:T(8,128)(2,1)} %bitcast.5), channel_id=1, source_target_pairs={{0,2},{2,0},{1,3},{3,1},{4,6},{6,4},{5,7},{7,5},{8,10},{10,8},{9,1... | collective-permute-start | bytes 691208 | tf_op jit(solution)/shard_map/ppermute | solution.py:232
  3.0 0.2 collective-permute-start.6
  3.2 1.6 %collective-permute-start.1 = (s32[3,1,4]{2,1,0:T(1,128)}, s32[3,1,4]{2,1,0:T(1,128)S(1)}, u32[]{:S(2)}, u32[]{:S(2)}) collective-permute-start(s32[3,1,4]{2,1,0:T(1,128)} %bitcast.11), channel_id=1, source_target_pairs={{0,4},{1,13},{4,0},{5,9},{8,12},{9,5},{12,8},{13,1},{2,6},{3,15},{... | collective-permute-start | bytes 152 | tf_op jit(solution)/shard_map/ppermute | solution.py:219
  4.7 2.6 %collective-permute-start.2 = (s32[3,1,4]{2,1,0:T(1,128)}, s32[3,1,4]{2,1,0:T(1,128)S(1)}, u32[]{:S(2)}, u32[]{:S(2)}) collective-permute-start(s32[3,1,4]{2,1,0:T(1,128)} %bitcast.12), channel_id=1, source_target_pairs={{0,8},{1,9},{4,12},{5,13},{8,0},{9,1},{12,4},{13,5},{2,10},{3,11},... | collective-permute-start | bytes 152 | tf_op jit(solution)/shard_map/ppermute | solution.py:219
  7.3 2.3 %stage.1 = (bf16[16,7424]{1,0:T(8,128)(2,1)S(1)}, s32[3,1,4]{2,1,0:T(1,128)S(1)}, bf16[432,256]{1,0:T(8,128)(2,1)S(1)}, bf16[12,128]{1,0:T(8,128)(2,1)S(1)}, bf16[3,3,3,512,128]{4,3,2,1,0:T(8,128)(2,1)S(1)}) custom-call(bf16[16,7200]{1,0:T(8,128)(2,1)} %bitcast.6, s32[3,1,4]{2,1,0:T(1,128)} %bitcast.13, bf16[432,256]{1,0:T(8,128)(2,1)} %bitcast.8, ...), custom_call_target="tpu_custom_call" | custom-call | flops 1 | bytes 1 | tf_op jit(solution)/shard_map/stage/pallas_call | solution.py:236
  9.7 0.0 collective-permute-done.1.refs_0_
  9.7 0.0 collective-permute-done.2.refs_1_
  9.7 0.0 collective-permute-done.refs_2_.refs_3_
  9.7 0.3 %cut_windows.1 = (bf16[8,16,128]{2,1,0:T(8,128)(2,1)S(1)}, bf16[8,16,128]{2,1,0:T(8,128)(2,1)S(1)}) custom-call(s32[3,1,4]{2,1,0:T(1,128)S(1)} %collective-permute-done.1.refs_0_, s32[3,1,4]{2,1,0:T(1,128)S(1)} %collective-permute-done.2.refs_1_, bf16[16,7424]{1,0:T(8,128)(2,1)S(1)} %get-tuple-element.13.refs_1_.refs_2_, ...), custom_call_target="tpu_custom_call" | custom-call | flops 1 | bytes 1 | tf_op jit(solution)/shard_map/cut_windows/pallas_call | solution.py:255
  10.0 1.7 %collective-permute-start.3 = (bf16[8,16,128]{2,1,0:T(8,128)(2,1)S(1)}, bf16[8,16,128]{2,1,0:T(8,128)(2,1)S(1)}, u32[]{:S(2)}, u32[]{:S(2)}) collective-permute-start(bf16[8,16,128]{2,1,0:T(8,128)(2,1)S(1)} %get-tuple-element.14), channel_id=1, source_target_pairs={{0,4},{1,13},{4,0},{5,9},{8,12},{9,5},{12,8},{13,1},{2,6},{3,15},{... | collective-permute-start | bytes 98312 | tf_op jit(solution)/shard_map/ppermute | solution.py:219
  11.7 2.6 %collective-permute-start.5 = (bf16[8,16,128]{2,1,0:T(8,128)(2,1)S(1)}, bf16[8,16,128]{2,1,0:T(8,128)(2,1)S(1)}, u32[]{:S(2)}, u32[]{:S(2)}) collective-permute-start(bf16[8,16,128]{2,1,0:T(8,128)(2,1)S(1)} %get-tuple-element.15), channel_id=1, source_target_pairs={{0,8},{1,9},{4,12},{5,13},{8,0},{9,1},{12,4},{13,5},{2,10},{3,11},... | collective-permute-start | bytes 98312 | tf_op jit(solution)/shard_map/ppermute | solution.py:219
  14.3 0.0 collective-permute-done.3.refs_3_
  14.3 1.0 %collective-permute-start.4 = (bf16[8,16,128]{2,1,0:T(8,128)(2,1)S(1)}, bf16[8,16,128]{2,1,0:T(8,128)(2,1)S(1)}, u32[]{:S(2)}, u32[]{:S(2)}) collective-permute-start(bf16[8,16,128]{2,1,0:T(8,128)(2,1)S(1)} %collective-permute-done.3.refs_3_), channel_id=1, source_target_pairs={{0,1},{1,0},{2,3},{3,2},{4,5},{5,4},{6,7},{7,6},{8,9},{9,8},{10,11... | collective-permute-start | bytes 98312 | tf_op jit(solution)/shard_map/ppermute | solution.py:211
  15.3 0.0 copy-done
  15.3 0.0 collective-permute-start.7
  16.0 0.2 %cut_own.1.refs_2_ = bf16[8,16,128]{2,1,0:T(8,128)(2,1)S(1)} custom-call(s32[3,1,4]{2,1,0:T(1,128)S(1)} %get-tuple-element.12.refs_0_.refs_1_, bf16[16,7424]{1,0:T(8,128)(2,1)S(1)} %get-tuple-element.13.refs_1_.refs_2_, bf16[16,7200]{1,0:T(8,128)(2,1)S(1)} %collective-permute-done.refs_2_.refs_3_), custom_call_target="tpu_custom_call" | custom-call | flops 1 | bytes 1 | tf_op jit(solution)/shard_map/cut_own/pallas_call | solution.py:255
  16.2 0.3 %collective-permute-done.7.refs_9_ = bf16[12,128]{1,0:T(8,128)(2,1)S(1)} collective-permute-done((bf16[12,128]{1,0:T(8,128)(2,1)S(1)}, bf16[12,128]{1,0:T(8,128)(2,1)S(1)}, u32[]{:S(2)}, u32[]{:S(2)}) %collective-permute-start.7) | collective-permute-done | bytes 3104 | tf_op jit(solution)/shard_map/ppermute | solution.py:211
  16.5 0.0 collective-permute-done.6.refs_7_
  16.5 0.5 %collective-permute-done.5.refs_5_ = bf16[8,16,128]{2,1,0:T(8,128)(2,1)S(1)} collective-permute-done((bf16[8,16,128]{2,1,0:T(8,128)(2,1)S(1)}, bf16[8,16,128]{2,1,0:T(8,128)(2,1)S(1)}, u32[]{:S(2)}, u32[]{:S(2)}) %collective-permute-start.5) | collective-permute-done | bytes 32800 | tf_op jit(solution)/shard_map/ppermute | solution.py:219
  17.0 0.0 collective-permute-done.4.refs_4_
  17.0 0.0 collective-permute-done.8.refs_11_
  17.0 3.7 %decode.1 = bf16[1,3,1,4,128]{4,3,2,1,0:T(4,128)(2,1)} custom-call(s32[1,1]{1,0:T(1,128)S(6)} %copy.7.refs_0_, s32[3,1,4]{2,1,0:T(1,128)S(1)} %get-tuple-element.12.refs_0_.refs_1_, bf16[8,16,128]{2,1,0:T(8,128)(2,1)S(1)} %cut_own.1.refs_2_, bf16[8,16,128]{2,1,0:T(8,128)(2,1)S(1)} %collective-permute-done.3.refs_3_, ...), custom_call_target="tpu_custom_call" | custom-call | tf_op jit(solution)/shard_map/decode/pallas_call | solution.py:270
Async XLA Ops:
  0.0 15.3 %copy-start = (bf16[128,12]{0,1:T(8,128)(2,1)S(1)}, bf16[128,12]{0,1:T(8,128)(2,1)}, u32[]{:S(2)}) copy-start(bf16[128,12]{0,1:T(8,128)(2,1)} %param.9) | copy-start | bytes 9220
  0.0 17.0 %collective-permute-start.8 = (bf16[3,3,3,512,128]{4,3,2,1,0:T(8,128)(2,1)}, bf16[3,3,3,512,128]{4,3,2,1,0:T(8,128)(2,1)S(1)}, u32[]{:S(2)}, u32[]{:S(2)}) collective-permute-start(bf16[3,3,3,512,128]{4,3,2,1,0:T(8,128)(2,1)} %refs_4_.1), channel_id=1, source_target_pairs={{0,1},{1,0},{2,3},{3,2},{4,5},{5,4},{6,7},{7,6},{8,9},{9,8},{10,11... | collective-permute-start | bytes 10616840 | tf_op jit(solution)/shard_map/ppermute | solution.py:211
  0.5 9.2 %collective-permute-start = (bf16[16,7200]{1,0:T(8,128)(2,1)}, bf16[16,7200]{1,0:T(8,128)(2,1)S(1)}, u32[]{:S(2)}, u32[]{:S(2)}) collective-permute-start(bf16[16,7200]{1,0:T(8,128)(2,1)} %bitcast.5), channel_id=1, source_target_pairs={{0,2},{2,0},{1,3},{3,1},{4,6},{6,4},{5,7},{7,5},{8,10},{10,8},{9,1... | collective-permute-start | bytes 691208 | tf_op jit(solution)/shard_map/ppermute | solution.py:232
  3.0 13.5 %collective-permute-start.6 = (bf16[432,256]{1,0:T(8,128)(2,1)}, bf16[432,256]{1,0:T(8,128)(2,1)S(1)}, u32[]{:S(2)}, u32[]{:S(2)}) collective-permute-start(bf16[432,256]{1,0:T(8,128)(2,1)} %bitcast.7), channel_id=1, source_target_pairs={{0,1},{1,0},{2,3},{3,2},{4,5},{5,4},{6,7},{7,6},{8,9},{9,8},{10,11... | collective-permute-start | bytes 663560 | tf_op jit(solution)/shard_map/ppermute | solution.py:211
  3.2 6.5 %collective-permute-start.1 = (s32[3,1,4]{2,1,0:T(1,128)}, s32[3,1,4]{2,1,0:T(1,128)S(1)}, u32[]{:S(2)}, u32[]{:S(2)}) collective-permute-start(s32[3,1,4]{2,1,0:T(1,128)} %bitcast.11), channel_id=1, source_target_pairs={{0,4},{1,13},{4,0},{5,9},{8,12},{9,5},{12,8},{13,1},{2,6},{3,15},{... | collective-permute-start | bytes 152 | tf_op jit(solution)/shard_map/ppermute | solution.py:219
  4.7 4.9 %collective-permute-start.2 = (s32[3,1,4]{2,1,0:T(1,128)}, s32[3,1,4]{2,1,0:T(1,128)S(1)}, u32[]{:S(2)}, u32[]{:S(2)}) collective-permute-start(s32[3,1,4]{2,1,0:T(1,128)} %bitcast.12), channel_id=1, source_target_pairs={{0,8},{1,9},{4,12},{5,13},{8,0},{9,1},{12,4},{13,5},{2,10},{3,11},... | collective-permute-start | bytes 152 | tf_op jit(solution)/shard_map/ppermute | solution.py:219
  10.0 4.3 %collective-permute-start.3 = (bf16[8,16,128]{2,1,0:T(8,128)(2,1)S(1)}, bf16[8,16,128]{2,1,0:T(8,128)(2,1)S(1)}, u32[]{:S(2)}, u32[]{:S(2)}) collective-permute-start(bf16[8,16,128]{2,1,0:T(8,128)(2,1)S(1)} %get-tuple-element.14), channel_id=1, source_target_pairs={{0,4},{1,13},{4,0},{5,9},{8,12},{9,5},{12,8},{13,1},{2,6},{3,15},{... | collective-permute-start | bytes 98312 | tf_op jit(solution)/shard_map/ppermute | solution.py:219
  11.7 5.3 %collective-permute-start.5 = (bf16[8,16,128]{2,1,0:T(8,128)(2,1)S(1)}, bf16[8,16,128]{2,1,0:T(8,128)(2,1)S(1)}, u32[]{:S(2)}, u32[]{:S(2)}) collective-permute-start(bf16[8,16,128]{2,1,0:T(8,128)(2,1)S(1)} %get-tuple-element.15), channel_id=1, source_target_pairs={{0,8},{1,9},{4,12},{5,13},{8,0},{9,1},{12,4},{13,5},{2,10},{3,11},... | collective-permute-start | bytes 98312 | tf_op jit(solution)/shard_map/ppermute | solution.py:219
  14.3 2.7 %collective-permute-start.4 = (bf16[8,16,128]{2,1,0:T(8,128)(2,1)S(1)}, bf16[8,16,128]{2,1,0:T(8,128)(2,1)S(1)}, u32[]{:S(2)}, u32[]{:S(2)}) collective-permute-start(bf16[8,16,128]{2,1,0:T(8,128)(2,1)S(1)} %collective-permute-done.3.refs_3_), channel_id=1, source_target_pairs={{0,1},{1,0},{2,3},{3,2},{4,5},{5,4},{6,7},{7,6},{8,9},{9,8},{10,11... | collective-permute-start | bytes 98312 | tf_op jit(solution)/shard_map/ppermute | solution.py:211
  15.3 1.2 %collective-permute-start.7 = (bf16[12,128]{1,0:T(8,128)(2,1)S(1)}, bf16[12,128]{1,0:T(8,128)(2,1)S(1)}, u32[]{:S(2)}, u32[]{:S(2)}) collective-permute-start(bf16[12,128]{1,0:T(8,128)(2,1)S(1)} %bitcast.10), channel_id=1, source_target_pairs={{0,1},{1,0},{2,3},{3,2},{4,5},{5,4},{6,7},{7,6},{8,9},{9,8},{10,11... | collective-permute-start | bytes 9224 | tf_op jit(solution)/shard_map/ppermute | solution.py:211

commit v10 on v9

--- a/solution.py
+++ b/solution.py
@@ -143,12 +143,12 @@
     x = lax.broadcasted_iota(jnp.int32, (WIDE, LANES), 0)
     quarter, half = C_MID // 4, C_MID // 2
     for t in range(TAPS):
-        volume = jnp.concatenate([*cells[t : t + TAPS], tail], axis=1)
+        volume = jnp.concatenate([*cells[t : t + TAPS], tail[:, : (TAPS + 2) * C_LAT]], axis=1)
         lined = lineds[t]
         for first, weights in enumerate((own_in, other_in)):
             per_tap = len(taps) * C_LAT
             kernel = [weights[a * per_tap : a * per_tap + LANES] for a in range(TAPS)]
-            for j in range(LANES // C_LAT):
+            for j in range(TAPS + 2):
                 a = j - t
                 ends = weights[a * per_tap + LANES : (a + 1) * per_tap] if 0 <= a < TAPS else None
                 kernel.append(jnp.zeros((C_LAT, half), BF16) if ends is None else ends)

time: 20.9 us -> 20.9 us (level)
  no operation moved by 1% of the time
where the time goes in v10:
time: 20.9 us; the launch traced here: 20.8 us
  starting transfers between devices  12.6 us (60%)
  Pallas kernels  6.63 us (32%)
  waiting for transfers between devices  0.8 us (4%)
  between operations  0.71 us (3%)
    ppermute x4, starting transfers between devices, spread(): return lax.ppermute(x, ('seq', 'chan'), pairs)  8.46 us
    pallas_call x1, Pallas kernels, local(): pl.pallas_call(functools.partial(decode, n), out_shape=jax.ShapeDtypeStru...  3.75 us
    ppermute x1, starting transfers between devices, local(): lax.ppermute(current, 'tm', [(i, (i + 1) % tm_size) for i in range(tm_siz...  2.55 us
    pallas_call x1, Pallas kernels, local(): pl.pallas_call(stage, out_shape=[jax.ShapeDtypeStruct((C_LAT, padded), BF...  2.32 us
    ppermute x4, starting transfers between devices, swapped(): return lax.ppermute(x, 'chan', [(0, 1), (1, 0)])  1.63 us
    pallas_call x2, Pallas kernels, local(): pl.pallas_call(functools.partial(cut_windows, n), out_shape=[shape] * len...  0.57 us
    ppermute x4, waiting for transfers between devices, spread(): return lax.ppermute(x, ('seq', 'chan'), pairs)  0.52 us
  transfers between devices with their start and end apart: 9, of which 2 were waited for; matrix products, arithmetic and copies ran while one was open for 0% of the time, Pallas kernels for 14%

profile of v10, /device:TPU:0, one launch (start us, length us, event | category | flops | bytes accessed | tf_op | source)
XLA Modules:
  0.0 20.8 jit_solution(9617912567521148141)
XLA Ops:
  0.0 0.0 copy-start
  0.0 0.5 %collective-permute-start.8 = (bf16[3,3,3,512,128]{4,3,2,1,0:T(8,128)(2,1)}, bf16[3,3,3,512,128]{4,3,2,1,0:T(8,128)(2,1)S(1)}, u32[]{:S(2)}, u32[]{:S(2)}) collective-permute-start(bf16[3,3,3,512,128]{4,3,2,1,0:T(8,128)(2,1)} %refs_4_.1), channel_id=1, source_target_pairs={{0,1},{1,0},{2,3},{3,2},{4,5},{5,4},{6,7},{7,6},{8,9},{9,8},{10,11... | collective-permute-start | bytes 10616840 | tf_op jit(solution)/shard_map/ppermute | solution.py:211
  0.5 2.5 %collective-permute-start = (bf16[16,7200]{1,0:T(8,128)(2,1)}, bf16[16,7200]{1,0:T(8,128)(2,1)S(1)}, u32[]{:S(2)}, u32[]{:S(2)}) collective-permute-start(bf16[16,7200]{1,0:T(8,128)(2,1)} %bitcast.5), channel_id=1, source_target_pairs={{0,2},{2,0},{1,3},{3,1},{4,6},{6,4},{5,7},{7,5},{8,10},{10,8},{9,1... | collective-permute-start | bytes 691208 | tf_op jit(solution)/shard_map/ppermute | solution.py:232
  3.0 0.2 collective-permute-start.6
  3.2 1.6 %collective-permute-start.1 = (s32[3,1,4]{2,1,0:T(1,128)}, s32[3,1,4]{2,1,0:T(1,128)S(1)}, u32[]{:S(2)}, u32[]{:S(2)}) collective-permute-start(s32[3,1,4]{2,1,0:T(1,128)} %bitcast.11), channel_id=1, source_target_pairs={{0,4},{1,13},{4,0},{5,9},{8,12},{9,5},{12,8},{13,1},{2,6},{3,15},{... | collective-permute-start | bytes 152 | tf_op jit(solution)/shard_map/ppermute | solution.py:219
  4.7 2.6 %collective-permute-start.2 = (s32[3,1,4]{2,1,0:T(1,128)}, s32[3,1,4]{2,1,0:T(1,128)S(1)}, u32[]{:S(2)}, u32[]{:S(2)}) collective-permute-start(s32[3,1,4]{2,1,0:T(1,128)} %bitcast.12), channel_id=1, source_target_pairs={{0,8},{1,9},{4,12},{5,13},{8,0},{9,1},{12,4},{13,5},{2,10},{3,11},... | collective-permute-start | bytes 152 | tf_op jit(solution)/shard_map/ppermute | solution.py:219
  7.3 2.3 %stage.1 = (bf16[16,7424]{1,0:T(8,128)(2,1)S(1)}, s32[3,1,4]{2,1,0:T(1,128)S(1)}, bf16[432,256]{1,0:T(8,128)(2,1)S(1)}, bf16[12,128]{1,0:T(8,128)(2,1)S(1)}, bf16[3,3,3,512,128]{4,3,2,1,0:T(8,128)(2,1)S(1)}) custom-call(bf16[16,7200]{1,0:T(8,128)(2,1)} %bitcast.6, s32[3,1,4]{2,1,0:T(1,128)} %bitcast.13, bf16[432,256]{1,0:T(8,128)(2,1)} %bitcast.8, ...), custom_call_target="tpu_custom_call" | custom-call | flops 1 | bytes 1 | tf_op jit(solution)/shard_map/stage/pallas_call | solution.py:236
  9.7 0.0 collective-permute-done.1.refs_0_
  9.7 0.0 collective-permute-done.2.refs_1_
  9.7 0.0 collective-permute-done.refs_2_.refs_3_
  9.7 0.3 %cut_windows.1 = (bf16[8,16,128]{2,1,0:T(8,128)(2,1)S(1)}, bf16[8,16,128]{2,1,0:T(8,128)(2,1)S(1)}) custom-call(s32[3,1,4]{2,1,0:T(1,128)S(1)} %collective-permute-done.1.refs_0_, s32[3,1,4]{2,1,0:T(1,128)S(1)} %collective-permute-done.2.refs_1_, bf16[16,7424]{1,0:T(8,128)(2,1)S(1)} %get-tuple-element.13.refs_1_.refs_2_, ...), custom_call_target="tpu_custom_call" | custom-call | flops 1 | bytes 1 | tf_op jit(solution)/shard_map/cut_windows/pallas_call | solution.py:255
  10.0 1.7 %collective-permute-start.3 = (bf16[8,16,128]{2,1,0:T(8,128)(2,1)S(1)}, bf16[8,16,128]{2,1,0:T(8,128)(2,1)S(1)}, u32[]{:S(2)}, u32[]{:S(2)}) collective-permute-start(bf16[8,16,128]{2,1,0:T(8,128)(2,1)S(1)} %get-tuple-element.14), channel_id=1, source_target_pairs={{0,4},{1,13},{4,0},{5,9},{8,12},{9,5},{12,8},{13,1},{2,6},{3,15},{... | collective-permute-start | bytes 98312 | tf_op jit(solution)/shard_map/ppermute | solution.py:219
  11.7 2.6 %collective-permute-start.5 = (bf16[8,16,128]{2,1,0:T(8,128)(2,1)S(1)}, bf16[8,16,128]{2,1,0:T(8,128)(2,1)S(1)}, u32[]{:S(2)}, u32[]{:S(2)}) collective-permute-start(bf16[8,16,128]{2,1,0:T(8,128)(2,1)S(1)} %get-tuple-element.15), channel_id=1, source_target_pairs={{0,8},{1,9},{4,12},{5,13},{8,0},{9,1},{12,4},{13,5},{2,10},{3,11},... | collective-permute-start | bytes 98312 | tf_op jit(solution)/shard_map/ppermute | solution.py:219
  14.3 0.0 collective-permute-done.3.refs_3_
  14.3 1.0 %collective-permute-start.4 = (bf16[8,16,128]{2,1,0:T(8,128)(2,1)S(1)}, bf16[8,16,128]{2,1,0:T(8,128)(2,1)S(1)}, u32[]{:S(2)}, u32[]{:S(2)}) collective-permute-start(bf16[8,16,128]{2,1,0:T(8,128)(2,1)S(1)} %collective-permute-done.3.refs_3_), channel_id=1, source_target_pairs={{0,1},{1,0},{2,3},{3,2},{4,5},{5,4},{6,7},{7,6},{8,9},{9,8},{10,11... | collective-permute-start | bytes 98312 | tf_op jit(solution)/shard_map/ppermute | solution.py:211
  15.3 0.0 copy-done
  15.3 0.0 collective-permute-start.7
  16.0 0.2 %cut_own.1.refs_2_ = bf16[8,16,128]{2,1,0:T(8,128)(2,1)S(1)} custom-call(s32[3,1,4]{2,1,0:T(1,128)S(1)} %get-tuple-element.12.refs_0_.refs_1_, bf16[16,7424]{1,0:T(8,128)(2,1)S(1)} %get-tuple-element.13.refs_1_.refs_2_, bf16[16,7200]{1,0:T(8,128)(2,1)S(1)} %collective-permute-done.refs_2_.refs_3_), custom_call_target="tpu_custom_call" | custom-call | flops 1 | bytes 1 | tf_op jit(solution)/shard_map/cut_own/pallas_call | solution.py:255
  16.2 0.3 %collective-permute-done.7.refs_9_ = bf16[12,128]{1,0:T(8,128)(2,1)S(1)} collective-permute-done((bf16[12,128]{1,0:T(8,128)(2,1)S(1)}, bf16[12,128]{1,0:T(8,128)(2,1)S(1)}, u32[]{:S(2)}, u32[]{:S(2)}) %collective-permute-start.7) | collective-permute-done | bytes 3104 | tf_op jit(solution)/shard_map/ppermute | solution.py:211
  16.5 0.0 collective-permute-done.6.refs_7_
  16.5 0.5 %collective-permute-done.5.refs_5_ = bf16[8,16,128]{2,1,0:T(8,128)(2,1)S(1)} collective-permute-done((bf16[8,16,128]{2,1,0:T(8,128)(2,1)S(1)}, bf16[8,16,128]{2,1,0:T(8,128)(2,1)S(1)}, u32[]{:S(2)}, u32[]{:S(2)}) %collective-permute-start.5) | collective-permute-done | bytes 32800 | tf_op jit(solution)/shard_map/ppermute | solution.py:219
  17.0 0.0 collective-permute-done.4.refs_4_
  17.0 0.0 collective-permute-done.8.refs_11_
  17.0 3.7 %decode.1 = bf16[1,3,1,4,128]{4,3,2,1,0:T(4,128)(2,1)} custom-call(s32[1,1]{1,0:T(1,128)S(6)} %copy.7.refs_0_, s32[3,1,4]{2,1,0:T(1,128)S(1)} %get-tuple-element.12.refs_0_.refs_1_, bf16[8,16,128]{2,1,0:T(8,128)(2,1)S(1)} %cut_own.1.refs_2_, bf16[8,16,128]{2,1,0:T(8,128)(2,1)S(1)} %collective-permute-done.3.refs_3_, ...), custom_call_target="tpu_custom_call" | custom-call | tf_op jit(solution)/shard_map/decode/pallas_call | solution.py:270
Async XLA Ops:
  0.0 15.3 %copy-start = (bf16[128,12]{0,1:T(8,128)(2,1)S(1)}, bf16[128,12]{0,1:T(8,128)(2,1)}, u32[]{:S(2)}) copy-start(bf16[128,12]{0,1:T(8,128)(2,1)} %param.9) | copy-start | bytes 9220
  0.0 17.0 %collective-permute-start.8 = (bf16[3,3,3,512,128]{4,3,2,1,0:T(8,128)(2,1)}, bf16[3,3,3,512,128]{4,3,2,1,0:T(8,128)(2,1)S(1)}, u32[]{:S(2)}, u32[]{:S(2)}) collective-permute-start(bf16[3,3,3,512,128]{4,3,2,1,0:T(8,128)(2,1)} %refs_4_.1), channel_id=1, source_target_pairs={{0,1},{1,0},{2,3},{3,2},{4,5},{5,4},{6,7},{7,6},{8,9},{9,8},{10,11... | collective-permute-start | bytes 10616840 | tf_op jit(solution)/shard_map/ppermute | solution.py:211
  0.5 9.2 %collective-permute-start = (bf16[16,7200]{1,0:T(8,128)(2,1)}, bf16[16,7200]{1,0:T(8,128)(2,1)S(1)}, u32[]{:S(2)}, u32[]{:S(2)}) collective-permute-start(bf16[16,7200]{1,0:T(8,128)(2,1)} %bitcast.5), channel_id=1, source_target_pairs={{0,2},{2,0},{1,3},{3,1},{4,6},{6,4},{5,7},{7,5},{8,10},{10,8},{9,1... | collective-permute-start | bytes 691208 | tf_op jit(solution)/shard_map/ppermute | solution.py:232
  3.0 13.5 %collective-permute-start.6 = (bf16[432,256]{1,0:T(8,128)(2,1)}, bf16[432,256]{1,0:T(8,128)(2,1)S(1)}, u32[]{:S(2)}, u32[]{:S(2)}) collective-permute-start(bf16[432,256]{1,0:T(8,128)(2,1)} %bitcast.7), channel_id=1, source_target_pairs={{0,1},{1,0},{2,3},{3,2},{4,5},{5,4},{6,7},{7,6},{8,9},{9,8},{10,11... | collective-permute-start | bytes 663560 | tf_op jit(solution)/shard_map/ppermute | solution.py:211
  3.2 6.5 %collective-permute-start.1 = (s32[3,1,4]{2,1,0:T(1,128)}, s32[3,1,4]{2,1,0:T(1,128)S(1)}, u32[]{:S(2)}, u32[]{:S(2)}) collective-permute-start(s32[3,1,4]{2,1,0:T(1,128)} %bitcast.11), channel_id=1, source_target_pairs={{0,4},{1,13},{4,0},{5,9},{8,12},{9,5},{12,8},{13,1},{2,6},{3,15},{... | collective-permute-start | bytes 152 | tf_op jit(solution)/shard_map/ppermute | solution.py:219
  4.7 4.9 %collective-permute-start.2 = (s32[3,1,4]{2,1,0:T(1,128)}, s32[3,1,4]{2,1,0:T(1,128)S(1)}, u32[]{:S(2)}, u32[]{:S(2)}) collective-permute-start(s32[3,1,4]{2,1,0:T(1,128)} %bitcast.12), channel_id=1, source_target_pairs={{0,8},{1,9},{4,12},{5,13},{8,0},{9,1},{12,4},{13,5},{2,10},{3,11},... | collective-permute-start | bytes 152 | tf_op jit(solution)/shard_map/ppermute | solution.py:219
  10.0 4.3 %collective-permute-start.3 = (bf16[8,16,128]{2,1,0:T(8,128)(2,1)S(1)}, bf16[8,16,128]{2,1,0:T(8,128)(2,1)S(1)}, u32[]{:S(2)}, u32[]{:S(2)}) collective-permute-start(bf16[8,16,128]{2,1,0:T(8,128)(2,1)S(1)} %get-tuple-element.14), channel_id=1, source_target_pairs={{0,4},{1,13},{4,0},{5,9},{8,12},{9,5},{12,8},{13,1},{2,6},{3,15},{... | collective-permute-start | bytes 98312 | tf_op jit(solution)/shard_map/ppermute | solution.py:219
  11.7 5.3 %collective-permute-start.5 = (bf16[8,16,128]{2,1,0:T(8,128)(2,1)S(1)}, bf16[8,16,128]{2,1,0:T(8,128)(2,1)S(1)}, u32[]{:S(2)}, u32[]{:S(2)}) collective-permute-start(bf16[8,16,128]{2,1,0:T(8,128)(2,1)S(1)} %get-tuple-element.15), channel_id=1, source_target_pairs={{0,8},{1,9},{4,12},{5,13},{8,0},{9,1},{12,4},{13,5},{2,10},{3,11},... | collective-permute-start | bytes 98312 | tf_op jit(solution)/shard_map/ppermute | solution.py:219
  14.3 2.7 %collective-permute-start.4 = (bf16[8,16,128]{2,1,0:T(8,128)(2,1)S(1)}, bf16[8,16,128]{2,1,0:T(8,128)(2,1)S(1)}, u32[]{:S(2)}, u32[]{:S(2)}) collective-permute-start(bf16[8,16,128]{2,1,0:T(8,128)(2,1)S(1)} %collective-permute-done.3.refs_3_), channel_id=1, source_target_pairs={{0,1},{1,0},{2,3},{3,2},{4,5},{5,4},{6,7},{7,6},{8,9},{9,8},{10,11... | collective-permute-start | bytes 98312 | tf_op jit(solution)/shard_map/ppermute | solution.py:211
  15.3 1.2 %collective-permute-start.7 = (bf16[12,128]{1,0:T(8,128)(2,1)S(1)}, bf16[12,128]{1,0:T(8,128)(2,1)S(1)}, u32[]{:S(2)}, u32[]{:S(2)}) collective-permute-start(bf16[12,128]{1,0:T(8,128)(2,1)S(1)} %bitcast.10), channel_id=1, source_target_pairs={{0,1},{1,0},{2,3},{3,2},{4,5},{5,4},{6,7},{7,6},{8,9},{9,8},{10,11... | collective-permute-start | bytes 9224 | tf_op jit(solution)/shard_map/ppermute | solution.py:211
